TPU v7x, 32 devices: a whole 2x2x4 slice. The times are simulated.
32 devices in a mesh: ctx: 16 (over z, x, core), head: 2 (over y).
Axes of the slice: x: 2, y: 2, z: 4, core: 2. Of those that a mesh axis runs over, the one named last changes fastest.
Arguments:
- queries: bfloat16 [16, 256, 32, 128], P('ctx', 'head'), may hold values from -6 to 6
- keys: bfloat16 [16, 256, 4, 128], P('ctx', 'head'), may hold values from -6 to 6
- values: bfloat16 [16, 256, 4, 128], P('ctx', 'head'), may hold values from -6 to 6
Outputs:
- weighted: float32 [16, 256, 32, 128], P('ctx', None, 'head')
- row_max: float32 [32, 16, 256], P('head', 'ctx')
- row_sum: float32 [32, 16, 256], P('head', 'ctx')
All inputs are finite; a program needn't handle non-finite values.
Results may differ from a plain program's by a relative error of at most 0.0027.
Values may be sent and summed in bfloat16 or wider, within the bound.
No kernel may reach another device: no remote copies, remote signals or barrier semaphores. Data moves between devices by JAX's collectives and lax.ppermute only.
A program may use at most 64 MiB of HBM per device.

v0:
```python
import math

import jax
import jax.numpy as jnp
from jax import lax
from jax.sharding import PartitionSpec as P

QUERY_HEADS = 32
KEY_VALUE_HEADS = 4
WIN = 8


def shifted(block, axis, distance):
    devices = range(lax.axis_size(axis))
    route = [((i - distance) % len(devices), i) for i in devices]
    return lax.ppermute(block, axis, route)


def positions(source, row_halves, period_length):
    row_ids = jnp.arange(2 * row_halves, dtype=jnp.int32)
    return jnp.where(
        row_ids < row_halves,
        2 * source * row_halves + row_ids,
        (2 * period_length - 1 - 2 * source) * row_halves + row_ids - row_halves,
    )


def local(queries, keys, values):
    query_all, key_all, value_all = (
        lax.all_to_all(queries, "head", split_axis=2, concat_axis=1, tiled=True),
        lax.all_to_all(keys, "head", split_axis=2, concat_axis=1, tiled=True),
        lax.all_to_all(values, "head", split_axis=2, concat_axis=1, tiled=True),
    )
    query_zig = query_all[0]
    key_zig = key_all[0]
    value_zig = value_all[0]
    row_halves = query_zig.shape[0] // 2
    period_length = lax.axis_size("ctx")
    own_index = lax.axis_index("ctx")
    key_row_block, value_row_block = (key_zig, value_zig)
    distance = 1
    while distance < WIN:
        received = shifted((key_row_block, value_row_block), "ctx", distance)
        key_row_block = jnp.concatenate([key_row_block, received[0]], axis=0)
        value_row_block = jnp.concatenate([value_row_block, received[1]], axis=0)
        distance = distance * 2
    sources = (own_index - jnp.arange(WIN, dtype=jnp.int32)) % period_length
    pos_keys = jax.vmap(lambda source: positions(source, row_halves, period_length))(
        sources
    ).reshape(-1)
    pos_query = positions(own_index, row_halves, period_length)
    visible = pos_keys[None, :] <= pos_query[:, None]
    query_group_count = QUERY_HEADS // KEY_VALUE_HEADS
    score_scale = 1.0 / math.sqrt(query_zig.shape[2])

    def one_head(head_id):
        query_head = lax.dynamic_index_in_dim(query_zig, head_id, 1, keepdims=False)
        key_head = lax.dynamic_index_in_dim(
            key_row_block, head_id // query_group_count, 1, keepdims=False
        )
        value_head = lax.dynamic_index_in_dim(
            value_row_block, head_id // query_group_count, 1, keepdims=False
        )
        scores = (
            lax.dot_general(
                query_head, key_head, (((1,), (1,)), ((), ())), preferred_element_type=jnp.float32
            )
            * score_scale
        )
        scores = jnp.where(visible, scores, jnp.float32(-1e30))
        head_max = jnp.max(scores, axis=1)
        weights = jnp.where(visible, jnp.exp(scores - head_max[:, None]), jnp.float32(0.0))
        head_sum = jnp.sum(weights, axis=1)
        head_out = jnp.dot(
            weights.astype(jnp.bfloat16), value_head, preferred_element_type=jnp.float32
        )
        return (head_out, head_max, head_sum)

    per_head, stat_max, stat_sum = lax.map(
        one_head, jnp.arange(query_zig.shape[1], dtype=jnp.int32)
    )
    weighted = jnp.transpose(per_head, (1, 0, 2))[None]
    return (weighted, stat_max[:, None, :], stat_sum[:, None, :])


def solution(mesh):
    in_specs = (
        P("ctx", "head", None, None),
        P("ctx", "head", None, None),
        P("ctx", "head", None, None),
    )
    out_specs = (P("ctx", None, "head", None), P("head", "ctx", None), P("head", "ctx", None))
    return jax.shard_map(local, mesh=mesh, in_specs=in_specs, out_specs=out_specs, check_vma=False)
```

profile of v0, /device:TPU:1, one launch (start us, length us, event | category | flops | bytes accessed | tf_op | source)
XLA Modules:
  0.0 235.5 jit_solution(1571433598835135565)
XLA Ops:
  0.6 1.0 copy.18
  1.7 6.5 %all_to_all.45 = bf16[1,128,4,128]{3,1,0,2:T(8,128)(2,1)S(1)} all-to-all(bf16[1,128,4,128]{3,1,0,2:T(8,128)(2,1)S(1)} %copy.18), channel_id=1, replica_groups=mesh['ctx'=16,'head'=2] {'head'}, dimensions={2} | all-to-all | bytes 262144 | tf_op jit(solution)/shard_map/all_to_all | solution.py:32
  8.1 3.3 %collective-permute-start.3 = (bf16[256,2,128]{2,0,1:T(8,128)(2,1)S(1)}, bf16[256,2,128]{2,0,1:T(8,128)(2,1)S(1)}, u32[]{:S(2)}, u32[]{:S(2)}) collective-permute-start(bf16[256,2,128]{2,0,1:T(8,128)(2,1)S(1)} %bitcast.53), channel_id=1, source_target_pairs={{30,0},{0,2},{2,4},{4,6},{6,8},{8,10},{10,12},{12,14},{14,16},{16,... | collective-permute-start | bytes 393224 | tf_op jit(solution)/shard_map/ppermute | solution.py:16
  11.4 0.9 copy.16
  12.3 5.8 %all_to_all.46 = bf16[1,128,4,128]{3,1,0,2:T(8,128)(2,1)S(1)} all-to-all(bf16[1,128,4,128]{3,1,0,2:T(8,128)(2,1)S(1)} %copy.16), channel_id=1, replica_groups=mesh['ctx'=16,'head'=2] {'head'}, dimensions={2} | all-to-all | bytes 262144 | tf_op jit(solution)/shard_map/all_to_all | solution.py:31
  18.1 1.2 collective-permute-start
  19.3 1.4 collective-permute-start.4
  20.7 1.4 copy.14
  22.1 3.6 %all-to-all-start = ((bf16[1,128,32,128]{3,1,0,2:T(8,128)(2,1)}), bf16[1,128,32,128]{3,1,0,2:T(8,128)(2,1)S(1)}, u32[]{:S(2)}, u32[]{:S(2)}) async-start(bf16[1,128,32,128]{3,1,0,2:T(8,128)(2,1)} %copy.14), calls=%async_computation | async-start | bytes 2097152 | tf_op jit(solution)/shard_map/all_to_all | solution.py:30
  25.7 1.2 collective-permute-start.1
  27.0 3.3 %collective-permute-done.4 = bf16[512,2,128]{2,0,1:T(8,128)(2,1)S(1)} collective-permute-done((bf16[512,2,128]{2,0,1:T(8,128)(2,1)S(1)}, bf16[512,2,128]{2,0,1:T(8,128)(2,1)S(1)}, u32[]{:S(2)}, u32[]{:S(2)}) %collective-permute-start.4) | collective-permute-done | bytes 262176 | tf_op jit(solution)/shard_map/ppermute | solution.py:16
  30.3 0.8 pad_maximum_fusion.3
  31.1 5.3 %collective-permute-done.1 = bf16[512,2,128]{2,0,1:T(8,128)(2,1)S(1)} collective-permute-done((bf16[512,2,128]{2,0,1:T(8,128)(2,1)S(1)}, bf16[512,2,128]{2,0,1:T(8,128)(2,1)S(1)}, u32[]{:S(2)}, u32[]{:S(2)}) %collective-permute-start.1) | collective-permute-done | bytes 262176 | tf_op jit(solution)/shard_map/ppermute | solution.py:16
  36.4 0.9 pad_maximum_fusion.2
  37.4 2.5 %all-to-all-done = bf16[1,128,32,128]{3,1,0,2:T(8,128)(2,1)S(1)} async-done(((bf16[1,128,32,128]{3,1,0,2:T(8,128)(2,1)}), bf16[1,128,32,128]{3,1,0,2:T(8,128)(2,1)S(1)}, u32[]{:S(2)}, u32[]{:S(2)}) %all-to-all-start) | async-done | bytes 1048608 | tf_op jit(solution)/shard_map/all_to_all | solution.py:30
  40.0 6.4 %collective-permute-done.5 = bf16[1024,2,128]{2,0,1:T(8,128)(2,1)} collective-permute-done((bf16[1024,2,128]{2,0,1:T(8,128)(2,1)}, bf16[1024,2,128]{2,0,1:T(8,128)(2,1)}, u32[]{:S(2)}, u32[]{:S(2)}) %collective-permute-start.5) | collective-permute-done | bytes 524320 | tf_op jit(solution)/shard_map/ppermute | solution.py:16
  46.4 2.1 pad_maximum_fusion.1
  48.5 9.2 %collective-permute-done.2 = bf16[1024,2,128]{2,0,1:T(8,128)(2,1)} collective-permute-done((bf16[1024,2,128]{2,0,1:T(8,128)(2,1)}, bf16[1024,2,128]{2,0,1:T(8,128)(2,1)}, u32[]{:S(2)}, u32[]{:S(2)}) %collective-permute-start.2) | collective-permute-done | bytes 524320 | tf_op jit(solution)/shard_map/ppermute | solution.py:16
  57.7 1.2 pad_maximum_fusion
  58.9 175.4 %while.17 = (s32[]{:T(128)}, f32[16,256,128]{2,0,1:T(8,128)}, f32[16,256]{1,0:T(8,128)S(1)}, f32[16,256]{1,0:T(8,128)S(1)}, s32[16]{0:T(128)S(1)}, /*index=5*/bf...) while((s32[]{:T(128)}, f32[16,256,128]{2,0,1:T(8,128)}, ...), condition=%wide.region_3.4_spmd.clone, body=%wide.region_0.3_spmd.clone.sunk | while | flops 274726400 | bytes 7835034 | solution.py:79
  58.9 0.6 dynamic_slice.54
  64.5 0.6 fusion.26
  65.2 4.7 %dynamic_update_slice.26 = f32[16,256,128]{2,0,1:T(8,128)} dynamic-update-slice(f32[16,256,128]{2,0,1:T(8,128)} %get-tuple-element.253, f32[1,256,128]{2,0,1:T(1,128)S(1)} %bitcast.52, s32[]{:T(128)S(6)} %copy.31, s32[]{:T(128)} %constant.115.clone.1..sunk, s32[]{:T(128)} %constant.115.clone.1..sunk) | dynamic-update-slice | bytes 262148 | tf_op jit(solution)/shard_map/while/body/jit(dynamic_update_index_in_dim)/dynamic_update_slice | solution.py:79
  75.5 0.6 fusion.26
  76.1 4.7 %dynamic_update_slice.26 = f32[16,256,128]{2,0,1:T(8,128)} dynamic-update-slice(f32[16,256,128]{2,0,1:T(8,128)} %get-tuple-element.253, f32[1,256,128]{2,0,1:T(1,128)S(1)} %bitcast.52, s32[]{:T(128)S(6)} %copy.31, s32[]{:T(128)} %constant.115.clone.1..sunk, s32[]{:T(128)} %constant.115.clone.1..sunk) | dynamic-update-slice | bytes 262148 | tf_op jit(solution)/shard_map/while/body/jit(dynamic_update_index_in_dim)/dynamic_update_slice | solution.py:79
  86.4 0.6 fusion.26
  87.1 4.7 %dynamic_update_slice.26 = f32[16,256,128]{2,0,1:T(8,128)} dynamic-update-slice(f32[16,256,128]{2,0,1:T(8,128)} %get-tuple-element.253, f32[1,256,128]{2,0,1:T(1,128)S(1)} %bitcast.52, s32[]{:T(128)S(6)} %copy.31, s32[]{:T(128)} %constant.115.clone.1..sunk, s32[]{:T(128)} %constant.115.clone.1..sunk) | dynamic-update-slice | bytes 262148 | tf_op jit(solution)/shard_map/while/body/jit(dynamic_update_index_in_dim)/dynamic_update_slice | solution.py:79
  98.1 4.7 %dynamic_update_slice.26 = f32[16,256,128]{2,0,1:T(8,128)} dynamic-update-slice(f32[16,256,128]{2,0,1:T(8,128)} %get-tuple-element.253, f32[1,256,128]{2,0,1:T(1,128)S(1)} %bitcast.52, s32[]{:T(128)S(6)} %copy.31, s32[]{:T(128)} %constant.115.clone.1..sunk, s32[]{:T(128)} %constant.115.clone.1..sunk) | dynamic-update-slice | bytes 262148 | tf_op jit(solution)/shard_map/while/body/jit(dynamic_update_index_in_dim)/dynamic_update_slice | solution.py:79
  108.4 0.6 fusion.26
  109.0 4.7 %dynamic_update_slice.26 = f32[16,256,128]{2,0,1:T(8,128)} dynamic-update-slice(f32[16,256,128]{2,0,1:T(8,128)} %get-tuple-element.253, f32[1,256,128]{2,0,1:T(1,128)S(1)} %bitcast.52, s32[]{:T(128)S(6)} %copy.31, s32[]{:T(128)} %constant.115.clone.1..sunk, s32[]{:T(128)} %constant.115.clone.1..sunk) | dynamic-update-slice | bytes 262148 | tf_op jit(solution)/shard_map/while/body/jit(dynamic_update_index_in_dim)/dynamic_update_slice | solution.py:79
  120.0 4.7 %dynamic_update_slice.26 = f32[16,256,128]{2,0,1:T(8,128)} dynamic-update-slice(f32[16,256,128]{2,0,1:T(8,128)} %get-tuple-element.253, f32[1,256,128]{2,0,1:T(1,128)S(1)} %bitcast.52, s32[]{:T(128)S(6)} %copy.31, s32[]{:T(128)} %constant.115.clone.1..sunk, s32[]{:T(128)} %constant.115.clone.1..sunk) | dynamic-update-slice | bytes 262148 | tf_op jit(solution)/shard_map/while/body/jit(dynamic_update_index_in_dim)/dynamic_update_slice | solution.py:79
  130.3 0.6 fusion.26
  131.0 4.7 %dynamic_update_slice.26 = f32[16,256,128]{2,0,1:T(8,128)} dynamic-update-slice(f32[16,256,128]{2,0,1:T(8,128)} %get-tuple-element.253, f32[1,256,128]{2,0,1:T(1,128)S(1)} %bitcast.52, s32[]{:T(128)S(6)} %copy.31, s32[]{:T(128)} %constant.115.clone.1..sunk, s32[]{:T(128)} %constant.115.clone.1..sunk) | dynamic-update-slice | bytes 262148 | tf_op jit(solution)/shard_map/while/body/jit(dynamic_update_index_in_dim)/dynamic_update_slice | solution.py:79
  141.9 4.7 %dynamic_update_slice.26 = f32[16,256,128]{2,0,1:T(8,128)} dynamic-update-slice(f32[16,256,128]{2,0,1:T(8,128)} %get-tuple-element.253, f32[1,256,128]{2,0,1:T(1,128)S(1)} %bitcast.52, s32[]{:T(128)S(6)} %copy.31, s32[]{:T(128)} %constant.115.clone.1..sunk, s32[]{:T(128)} %constant.115.clone.1..sunk) | dynamic-update-slice | bytes 262148 | tf_op jit(solution)/shard_map/while/body/jit(dynamic_update_index_in_dim)/dynamic_update_slice | solution.py:79
  152.2 0.6 fusion.26
  152.9 4.7 %dynamic_update_slice.26 = f32[16,256,128]{2,0,1:T(8,128)} dynamic-update-slice(f32[16,256,128]{2,0,1:T(8,128)} %get-tuple-element.253, f32[1,256,128]{2,0,1:T(1,128)S(1)} %bitcast.52, s32[]{:T(128)S(6)} %copy.31, s32[]{:T(128)} %constant.115.clone.1..sunk, s32[]{:T(128)} %constant.115.clone.1..sunk) | dynamic-update-slice | bytes 262148 | tf_op jit(solution)/shard_map/while/body/jit(dynamic_update_index_in_dim)/dynamic_update_slice | solution.py:79
  163.9 4.7 %dynamic_update_slice.26 = f32[16,256,128]{2,0,1:T(8,128)} dynamic-update-slice(f32[16,256,128]{2,0,1:T(8,128)} %get-tuple-element.253, f32[1,256,128]{2,0,1:T(1,128)S(1)} %bitcast.52, s32[]{:T(128)S(6)} %copy.31, s32[]{:T(128)} %constant.115.clone.1..sunk, s32[]{:T(128)} %constant.115.clone.1..sunk) | dynamic-update-slice | bytes 262148 | tf_op jit(solution)/shard_map/while/body/jit(dynamic_update_index_in_dim)/dynamic_update_slice | solution.py:79
  174.1 0.6 fusion.26
  174.8 4.7 %dynamic_update_slice.26 = f32[16,256,128]{2,0,1:T(8,128)} dynamic-update-slice(f32[16,256,128]{2,0,1:T(8,128)} %get-tuple-element.253, f32[1,256,128]{2,0,1:T(1,128)S(1)} %bitcast.52, s32[]{:T(128)S(6)} %copy.31, s32[]{:T(128)} %constant.115.clone.1..sunk, s32[]{:T(128)} %constant.115.clone.1..sunk) | dynamic-update-slice | bytes 262148 | tf_op jit(solution)/shard_map/while/body/jit(dynamic_update_index_in_dim)/dynamic_update_slice | solution.py:79
  185.8 4.7 %dynamic_update_slice.26 = f32[16,256,128]{2,0,1:T(8,128)} dynamic-update-slice(f32[16,256,128]{2,0,1:T(8,128)} %get-tuple-element.253, f32[1,256,128]{2,0,1:T(1,128)S(1)} %bitcast.52, s32[]{:T(128)S(6)} %copy.31, s32[]{:T(128)} %constant.115.clone.1..sunk, s32[]{:T(128)} %constant.115.clone.1..sunk) | dynamic-update-slice | bytes 262148 | tf_op jit(solution)/shard_map/while/body/jit(dynamic_update_index_in_dim)/dynamic_update_slice | solution.py:79
  196.1 0.6 fusion.26
  196.8 4.7 %dynamic_update_slice.26 = f32[16,256,128]{2,0,1:T(8,128)} dynamic-update-slice(f32[16,256,128]{2,0,1:T(8,128)} %get-tuple-element.253, f32[1,256,128]{2,0,1:T(1,128)S(1)} %bitcast.52, s32[]{:T(128)S(6)} %copy.31, s32[]{:T(128)} %constant.115.clone.1..sunk, s32[]{:T(128)} %constant.115.clone.1..sunk) | dynamic-update-slice | bytes 262148 | tf_op jit(solution)/shard_map/while/body/jit(dynamic_update_index_in_dim)/dynamic_update_slice | solution.py:79
  207.7 4.7 %dynamic_update_slice.26 = f32[16,256,128]{2,0,1:T(8,128)} dynamic-update-slice(f32[16,256,128]{2,0,1:T(8,128)} %get-tuple-element.253, f32[1,256,128]{2,0,1:T(1,128)S(1)} %bitcast.52, s32[]{:T(128)S(6)} %copy.31, s32[]{:T(128)} %constant.115.clone.1..sunk, s32[]{:T(128)} %constant.115.clone.1..sunk) | dynamic-update-slice | bytes 262148 | tf_op jit(solution)/shard_map/while/body/jit(dynamic_update_index_in_dim)/dynamic_update_slice | solution.py:79
  218.0 0.6 fusion.26
  218.7 4.7 %dynamic_update_slice.26 = f32[16,256,128]{2,0,1:T(8,128)} dynamic-update-slice(f32[16,256,128]{2,0,1:T(8,128)} %get-tuple-element.253, f32[1,256,128]{2,0,1:T(1,128)S(1)} %bitcast.52, s32[]{:T(128)S(6)} %copy.31, s32[]{:T(128)} %constant.115.clone.1..sunk, s32[]{:T(128)} %constant.115.clone.1..sunk) | dynamic-update-slice | bytes 262148 | tf_op jit(solution)/shard_map/while/body/jit(dynamic_update_index_in_dim)/dynamic_update_slice | solution.py:79
  229.6 4.7 %dynamic_update_slice.26 = f32[16,256,128]{2,0,1:T(8,128)} dynamic-update-slice(f32[16,256,128]{2,0,1:T(8,128)} %get-tuple-element.253, f32[1,256,128]{2,0,1:T(1,128)S(1)} %bitcast.52, s32[]{:T(128)S(6)} %copy.31, s32[]{:T(128)} %constant.115.clone.1..sunk, s32[]{:T(128)} %constant.115.clone.1..sunk) | dynamic-update-slice | bytes 262148 | tf_op jit(solution)/shard_map/while/body/jit(dynamic_update_index_in_dim)/dynamic_update_slice | solution.py:79
  234.3 0.6 broadcast_in_dim.59
  234.9 0.6 broadcast_in_dim.58
  (110 shorter events, 32.6 us)
Async XLA Ops:
  0.6 20.1 %copy-start = (bf16[1,128,32,128]{3,2,1,0:T(8,128)(2,1)S(1)}, bf16[1,128,32,128]{3,2,1,0:T(8,128)(2,1)}, u32[]{:S(2)}) copy-start(bf16[1,128,32,128]{3,2,1,0:T(8,128)(2,1)} %param.5) | copy-start | bytes 3145732
  8.1 11.2 %collective-permute-start.3 = (bf16[256,2,128]{2,0,1:T(8,128)(2,1)S(1)}, bf16[256,2,128]{2,0,1:T(8,128)(2,1)S(1)}, u32[]{:S(2)}, u32[]{:S(2)}) collective-permute-start(bf16[256,2,128]{2,0,1:T(8,128)(2,1)S(1)} %bitcast.53), channel_id=1, source_target_pairs={{30,0},{0,2},{2,4},{4,6},{6,8},{8,10},{10,12},{12,14},{14,16},{16,... | collective-permute-start | bytes 393224 | tf_op jit(solution)/shard_map/ppermute | solution.py:16
  18.1 7.6 %collective-permute-start = (bf16[256,2,128]{2,0,1:T(8,128)(2,1)S(1)}, bf16[256,2,128]{2,0,1:T(8,128)(2,1)S(1)}, u32[]{:S(2)}, u32[]{:S(2)}) collective-permute-start(bf16[256,2,128]{2,0,1:T(8,128)(2,1)S(1)} %bitcast.57), channel_id=1, source_target_pairs={{30,0},{0,2},{2,4},{4,6},{6,8},{8,10},{10,12},{12,14},{14,16},{16,... | collective-permute-start | bytes 393224 | tf_op jit(solution)/shard_map/ppermute | solution.py:16
  19.3 11.0 %collective-permute-start.4 = (bf16[512,2,128]{2,0,1:T(8,128)(2,1)S(1)}, bf16[512,2,128]{2,0,1:T(8,128)(2,1)S(1)}, u32[]{:S(2)}, u32[]{:S(2)}) collective-permute-start(bf16[512,2,128]{2,0,1:T(8,128)(2,1)S(1)} %pad_maximum_fusion.5), channel_id=1, source_target_pairs={{28,0},{30,2},{0,4},{2,6},{4,8},{6,10},{8,12},{10,14},{12,16},{14,... | collective-permute-start | bytes 786440 | tf_op jit(solution)/shard_map/ppermute | solution.py:16
  22.1 17.8 %all-to-all-start = ((bf16[1,128,32,128]{3,1,0,2:T(8,128)(2,1)}), bf16[1,128,32,128]{3,1,0,2:T(8,128)(2,1)S(1)}, u32[]{:S(2)}, u32[]{:S(2)}) async-start(bf16[1,128,32,128]{3,1,0,2:T(8,128)(2,1)} %copy.14), calls=%async_computation | async-start | bytes 2097152 | tf_op jit(solution)/shard_map/all_to_all | solution.py:30
  25.7 10.7 %collective-permute-start.1 = (bf16[512,2,128]{2,0,1:T(8,128)(2,1)S(1)}, bf16[512,2,128]{2,0,1:T(8,128)(2,1)S(1)}, u32[]{:S(2)}, u32[]{:S(2)}) collective-permute-start(bf16[512,2,128]{2,0,1:T(8,128)(2,1)S(1)} %pad_maximum_fusion.4), channel_id=1, source_target_pairs={{28,0},{30,2},{0,4},{2,6},{4,8},{6,10},{8,12},{10,14},{12,16},{14,... | collective-permute-start | bytes 786440 | tf_op jit(solution)/shard_map/ppermute | solution.py:16
  31.1 15.3 %collective-permute-start.5 = (bf16[1024,2,128]{2,0,1:T(8,128)(2,1)}, bf16[1024,2,128]{2,0,1:T(8,128)(2,1)}, u32[]{:S(2)}, u32[]{:S(2)}) collective-permute-start(bf16[1024,2,128]{2,0,1:T(8,128)(2,1)} %pad_maximum_fusion.3), channel_id=1, source_target_pairs={{24,0},{26,2},{28,4},{30,6},{0,8},{2,10},{4,12},{6,14},{8,16},{10,... | collective-permute-start | bytes 1572872 | tf_op jit(solution)/shard_map/ppermute | solution.py:16
  36.4 12.1 %copy-start.2 = (bf16[512,2,128]{2,0,1:T(8,128)(2,1)}, bf16[512,2,128]{2,0,1:T(8,128)(2,1)S(1)}, u32[]{:S(2)}) copy-start(bf16[512,2,128]{2,0,1:T(8,128)(2,1)S(1)} %collective-permute-done.1) | copy-start | bytes 786436
  37.3 20.4 %collective-permute-start.2 = (bf16[1024,2,128]{2,0,1:T(8,128)(2,1)}, bf16[1024,2,128]{2,0,1:T(8,128)(2,1)}, u32[]{:S(2)}, u32[]{:S(2)}) collective-permute-start(bf16[1024,2,128]{2,0,1:T(8,128)(2,1)} %pad_maximum_fusion.2), channel_id=1, source_target_pairs={{24,0},{26,2},{28,4},{30,6},{0,8},{2,10},{4,12},{6,14},{8,16},{10,... | collective-permute-start | bytes 1572872 | tf_op jit(solution)/shard_map/ppermute | solution.py:16
  48.5 10.3 %copy-start.1 = (bf16[2048,2,128]{2,0,1:T(8,128)(2,1)S(1)}, bf16[2048,2,128]{2,0,1:T(8,128)(2,1)}, u32[]{:S(2)}) copy-start(bf16[2048,2,128]{2,0,1:T(8,128)(2,1)} %pad_maximum_fusion.1) | copy-start | bytes 3145732
where the time goes:
time: 239 us; the launch traced here: 236 us
  local copies, waits for them, and re-layouts  89.9 us (38%)
  loops' own time  62.7 us (26%)
  waiting for transfers between devices  26.7 us (11%)
  matrix products  18.4 us (8%)
  other arithmetic  14.2 us (6%)
  blocking collectives  12.2 us (5%)
  starting transfers between devices  10.6 us (4%)
    dynamic_update_slice x48, local copies, waits for them, and re-layouts, local(): lax.map(one_head, jnp.arange(query_zig.shape[1], dtype=jnp.int32))  75.9 us
    another operation x1, loops' own time, local(): lax.map(one_head, jnp.arange(query_zig.shape[1], dtype=jnp.int32))  62.7 us
    ppermute x6, waiting for transfers between devices, shifted(): return lax.ppermute(block, axis, route)  24.2 us
    dot_general x16, matrix products, one_head(): jnp.dot(weights.astype(jnp.bfloat16), value_head, preferred_element_type=...  9.36 us
    dynamic_slice x16, local copies, waits for them, and re-layouts, local(): lax.map(one_head, jnp.arange(query_zig.shape[1], dtype=jnp.int32))  9.32 us
    reduce_sum x16, other arithmetic, one_head(): head_sum = jnp.sum(weights, axis=1)  9.11 us
    dot_general x16, matrix products, one_head(): lax.dot_general(query_head, key_head, (((1,), (1,)), ((), ())), preferred...  8.99 us
    ppermute x6, starting transfers between devices, shifted(): return lax.ppermute(block, axis, route)  7.05 us
  transfers between devices with their start and end apart: 7, of which 5 were waited for; matrix products, arithmetic and copies ran while one was open for 3% of the time, Pallas kernels for 0%

commit v1 on v0

v1 whole, which is shorter than its diff:
```python
import functools
import math

import jax
import jax.numpy as jnp
from jax import lax
from jax.experimental import pallas as pl
from jax.experimental.pallas import tpu as pltpu
from jax.sharding import PartitionSpec as P

QUERY_HEADS = 32
KEY_VALUE_HEADS = 4
WIN = 8
LAYER = 4
GROUP = QUERY_HEADS // KEY_VALUE_HEADS
BF16 = jnp.bfloat16
F32 = jnp.float32
VMEM_LIMIT = 56 * 2**20
NEG = -1e30


def pack_kernel(count, *refs):
    q_ref, k_ref, v_ref = refs[:3]
    q_outs, kv_outs = refs[3 : 3 + count], refs[3 + count :]
    rows, kv_heads = k_ref.shape[1:3]
    per = kv_heads // count
    h = lax.axis_index("head")
    k = k_ref[0].astype(F32)
    v = v_ref[0].astype(F32)
    for head in range(kv_heads):
        kh = k[:, head, :].astype(BF16)
        vh = v[:, head, :].astype(BF16)
        slot = lax.rem(head // per - h + count, count)
        for d in range(count):

            @pl.when(slot == d)
            def _():
                kv_outs[d][0, head % per] = kh
                kv_outs[d][1, head % per] = vh

    for head in range(kv_heads):
        slot = lax.rem(head // per - h + count, count)
        qh = q_ref[0, :, head * GROUP : (head + 1) * GROUP, :].astype(F32)
        qh = qh.reshape(rows * GROUP, qh.shape[-1]).astype(BF16)
        for d in range(count):

            @pl.when(slot == d)
            def _():
                q_outs[d][head % per] = qh


def pack(queries, keys, values, count):
    rows, width = keys.shape[1], keys.shape[3]
    per = keys.shape[2] // count
    q_shape = jax.ShapeDtypeStruct((per, rows * GROUP, width), BF16)
    kv_shape = jax.ShapeDtypeStruct((2, per, rows, width), BF16)
    outs = pl.pallas_call(
        functools.partial(pack_kernel, count),
        out_shape=(q_shape,) * count + (kv_shape,) * count,
        in_specs=[pl.BlockSpec(memory_space=pltpu.VMEM)] * 3,
        out_specs=[pl.BlockSpec(memory_space=pltpu.VMEM)] * (2 * count),
        compiler_params=pltpu.CompilerParams(vmem_limit_bytes=VMEM_LIMIT),
    )(queries, keys, values)
    return list(outs[:count]), list(outs[count:])


def attend_kernel(n, count, offsets, step_chunks, block, *refs):
    total = len(offsets) * count
    q_hbm, kv_hbm = refs[:count], refs[count : count + total]
    out_ref, max_ref, sum_ref, qbuf, kbuf, vbuf, mbuf, lbuf, qsem, ksem = refs[count + total :]
    per, rows, width = kv_hbm[0].shape[1:]
    half = count * rows // 2
    m_rows = rows * GROUP
    span = step_chunks * rows
    p = lax.axis_index("ctx")
    h = lax.axis_index("head")
    factor = math.log2(math.e) / math.sqrt(width)

    def start_of(pair, chunk):
        r = chunk * rows
        return jnp.where(r < half, 2 * pair * half + r, (2 * n - 2 - 2 * pair) * half + r)

    for s in range(count):
        pltpu.make_async_copy(q_hbm[s], qbuf.at[s], qsem.at[s]).start()
    chunks = []
    for a, offset in enumerate(offsets):
        pair = lax.rem(p - offset(p) + n, n)
        for d in range(count):
            chunks.append(start_of(pair, lax.rem(h - d + count, count)))
    plans = []
    for s in range(count):
        start_q = start_of(p, lax.rem(h - s + count, count))
        seen = jnp.int32(1)
        plan = []
        for c in [s] + [c for c in range(total) if c != s]:
            visible = None if c == s else chunks[c] < start_q
            at = jnp.int32(0) if c == s else seen
            if c != s:
                seen = seen + visible.astype(jnp.int32)
            plan.append((c, visible, at))
        plans.append((plan, seen))

    def copies(s, c, at):
        to = pl.ds(pl.multiple_of(at * rows, rows), rows)
        return (
            pltpu.make_async_copy(kv_hbm[c].at[0], kbuf.at[s, :, to, :], ksem.at[s, c, 0]),
            pltpu.make_async_copy(kv_hbm[c].at[1], vbuf.at[s, :, to, :], ksem.at[s, c, 1]),
        )

    def each(s, act):
        for c, visible, at in plans[s][0]:
            if visible is None:
                act(copies(s, c, at))
            else:

                @pl.when(visible)
                def _():
                    act(copies(s, c, at))

    for s in range(count):
        vbuf[s, :, :span, :] = jnp.zeros((per, span, width), BF16)
    for s in range(count):
        each(s, lambda pair: [x.start() for x in pair])

    for s in range(count):
        q_chunk = lax.rem(h - s + count, count)
        seen = plans[s][1]
        first = lax.rem(seen - 1, step_chunks) + 1
        steps = (seen - first) // step_chunks
        row0 = pl.multiple_of(q_chunk * rows, rows)
        pltpu.make_async_copy(q_hbm[s], qbuf.at[s], qsem.at[s]).wait()
        each(s, lambda pair: [x.wait() for x in pair])
        for g in range(per):

            def out_at(b):
                return (
                    0,
                    pl.ds(row0 + b * (block // GROUP), block // GROUP),
                    slice(g * GROUP, (g + 1) * GROUP),
                    slice(None),
                )

            k = kbuf[s, g, 0:span, :]
            v = vbuf[s, g, 0:span, :]
            for b in range(m_rows // block):
                at = slice(b * block, (b + 1) * block)
                score = lax.dot_general(
                    qbuf[s, g, at, :], k, (((1,), (1,)), ((), ())), preferred_element_type=F32
                )
                col = lax.broadcasted_iota(jnp.int32, (block, span), 1)
                row = (lax.broadcasted_iota(jnp.int32, (block, span), 0) + b * block) // GROUP
                limit = jnp.where(col < rows, row, first * rows - 1)
                score = jnp.where(col <= limit, score, NEG)
                top = jnp.max(score, axis=1, keepdims=True)
                prob = jnp.exp2((score - top) * factor)
                mbuf[at, :] = jnp.broadcast_to(top, (block, 128))
                lbuf[at, :] = sum(prob[:, t : t + 128] for t in range(0, span, 128))
                got = jnp.dot(prob.astype(BF16), v, preferred_element_type=F32)
                out_ref[out_at(b)] = got.reshape(block // GROUP, GROUP, width)

            def step(t, _):
                where = pl.ds(pl.multiple_of((first + t * step_chunks) * rows, rows), span)
                k = kbuf[s, g, where, :]
                v = vbuf[s, g, where, :]
                for b in range(m_rows // block):
                    at = slice(b * block, (b + 1) * block)
                    score = lax.dot_general(
                        qbuf[s, g, at, :], k, (((1,), (1,)), ((), ())), preferred_element_type=F32
                    )
                    old = mbuf[at, :]
                    top = jnp.maximum(old, jnp.max(score, axis=1, keepdims=True))
                    shrink = jnp.exp2((old - top) * factor)
                    probs = [
                        jnp.exp2((score[:, t : t + 128] - top) * factor)
                        for t in range(0, span, 128)
                    ]
                    mbuf[at, :] = top
                    lbuf[at, :] = lbuf[at, :] * shrink + sum(probs)
                    prob = jnp.concatenate([x.astype(BF16) for x in probs], axis=1)
                    got = jnp.dot(prob, v, preferred_element_type=F32)
                    held = out_ref[out_at(b)].reshape(block, width)
                    out_ref[out_at(b)] = (held * shrink + got).reshape(
                        block // GROUP, GROUP, width
                    )
                return 0

            lax.fori_loop(0, steps, step, 0)

            def to_lanes(x):
                x = x.reshape(rows, GROUP, 128)[:, :, :rows]
                a = lax.broadcasted_iota(jnp.int32, (rows, GROUP, rows), 0)
                b = lax.broadcasted_iota(jnp.int32, (rows, GROUP, rows), 2)
                return jnp.sum(jnp.where(a == b, x, 0.0), axis=0)

            tops = to_lanes(mbuf[...]) * (1.0 / math.sqrt(width))
            sums = jnp.sum(lbuf[...], axis=1, keepdims=True)
            sums = to_lanes(jnp.broadcast_to(sums, (m_rows, 128)))
            for d in range(count):

                @pl.when(q_chunk == d)
                def _():
                    max_ref[g * GROUP : (g + 1) * GROUP, 0, d * rows : (d + 1) * rows] = tops
                    sum_ref[g * GROUP : (g + 1) * GROUP, 0, d * rows : (d + 1) * rows] = sums


def attend(q_list, kv_list, offsets, n):
    count = len(q_list)
    per, m_rows, width = q_list[0].shape
    rows = m_rows // GROUP
    step_chunks = 512 // rows
    longest = (len(kv_list) + step_chunks) * rows
    total = len(kv_list)
    return pl.pallas_call(
        functools.partial(attend_kernel, n, count, offsets, step_chunks, min(512, m_rows)),
        out_shape=(
            jax.ShapeDtypeStruct((1, count * rows, per * GROUP, width), F32),
            jax.ShapeDtypeStruct((per * GROUP, 1, count * rows), F32),
            jax.ShapeDtypeStruct((per * GROUP, 1, count * rows), F32),
        ),
        in_specs=[pl.BlockSpec(memory_space=pl.ANY)] * (count + total),
        out_specs=[pl.BlockSpec(memory_space=pltpu.VMEM)] * 3,
        scratch_shapes=[
            pltpu.VMEM((count, per, m_rows, width), BF16),
            pltpu.VMEM((count, per, longest, width), BF16),
            pltpu.VMEM((count, per, longest, width), BF16),
            pltpu.VMEM((m_rows, 128), F32),
            pltpu.VMEM((m_rows, 128), F32),
            pltpu.SemaphoreType.DMA((count,)),
            pltpu.SemaphoreType.DMA((count, total, 2)),
        ],
        compiler_params=pltpu.CompilerParams(vmem_limit_bytes=VMEM_LIMIT),
    )(*q_list, *kv_list)


def along(block, axis, target):
    size = lax.axis_size(axis)
    return lax.ppermute(block, axis, [(i, target(i) % size) for i in range(size)])


def local(queries, keys, values):
    n = lax.axis_size("ctx")
    count = lax.axis_size("head")
    q_out, kv_out = pack(queries, keys, values, count)
    swap = lambda x, d: along(x, "head", lambda i: i + d)
    own = [kv_out[0]] + [swap(kv_out[d], d) for d in range(1, count)]
    q_in = [q_out[0]] + [swap(q_out[d], d) for d in range(1, count)]

    layer = LAYER
    ctx = lambda xs, target: [along(x, "ctx", target) for x in xs]
    up = ctx(own, lambda i: i + layer)
    wide = ctx(own, lambda i: i + 2 if i & 2 == 0 else i + layer + 2)
    near = ctx(own, lambda i: i + 1 if i & 1 == 0 else i + 2 * layer - 1)
    up_x = ctx(up, lambda i: i ^ 2)
    up_c = ctx(up, lambda i: i ^ 1)
    up_xc = ctx(up_x, lambda i: i ^ 1)
    wide_c = ctx(wide, lambda i: i ^ 1)

    def flip(p, bit):
        return jnp.where(lax.rem(p // bit, 2) == 1, bit, -bit)

    wide_at = lambda p: jnp.where(lax.rem(p // 2, 2) == 1, 2, layer + 2)
    near_at = lambda p: jnp.where(lax.rem(p, 2) == 1, 1, 2 * layer - 1)
    offsets = [
        lambda p: 0,
        lambda p: layer,
        wide_at,
        near_at,
        lambda p: layer + flip(p, 2),
        lambda p: layer + flip(p, 1),
        lambda p: layer + flip(p, 1) + flip(p, 2),
        lambda p: flip(p, 1) + wide_at(p),
    ]
    blocks = own + up + wide + near + up_x + up_c + up_xc + wide_c
    return attend(q_in, blocks, offsets, n)


def solution(mesh):
    in_specs = (
        P("ctx", "head", None, None),
        P("ctx", "head", None, None),
        P("ctx", "head", None, None),
    )
    out_specs = (P("ctx", None, "head", None), P("head", "ctx", None), P("head", "ctx", None))
    return jax.shard_map(local, mesh=mesh, in_specs=in_specs, out_specs=out_specs, check_vma=False)
```

time: 239 us -> 59 us (0.25); the launches traced: 236 us -> 58.4 us
  local copies, waits for them, and re-layouts: 89.9 us -> 0.78 us
  loops' own time: 62.7 us -> 0 us
  Pallas kernels: 0 us -> 18.5 us
  matrix products: 18.4 us -> 0 us
  other arithmetic: 14.2 us -> 0 us
  blocking collectives: 12.2 us -> 0 us
    dynamic_update_slice x48 -> x0, local copies, waits for them, and re-layouts: 75.9 us -> none  [local(): lax.map(one_head, jnp.arange(query_zig.shape[1], dtype=jnp.int32))]
    another operation x1 -> x0, loops' own time: 62.7 us -> none  [local(): lax.map(one_head, jnp.arange(query_zig.shape[1], dtype=jnp.int32))]
    pallas_call x0 -> x2, Pallas kernels: none -> 18.5 us  [the longest x1 15.3 us: attend(): pl.pallas_call(functools.partial(attend_kernel, n, count, offsets, step_c...]
    dot_general x32 -> x0, matrix products: 18.4 us -> none  [the longest x16 9.36 us: one_head(): jnp.dot(weights.astype(jnp.bfloat16), value_head, preferred_element_type=...]
    all_to_all x2 -> x0, blocking collectives: 12.2 us -> none  [the longest x1 6.46 us: local(): lax.all_to_all(values, 'head', split_axis=2, concat_axis=1, tiled=True)]
    dynamic_slice x16 -> x0, local copies, waits for them, and re-layouts: 9.32 us -> none  [local(): lax.map(one_head, jnp.arange(query_zig.shape[1], dtype=jnp.int32))]
    reduce_sum x16 -> x0, other arithmetic: 9.11 us -> none  [one_head(): head_sum = jnp.sum(weights, axis=1)]
    ppermute x6 -> x16, starting transfers between devices: 7.05 us -> 12.1 us  [along(): lax.ppermute(block, axis, [(i, target(i) % size) for i in range(size)])]
  transfers between devices with their start and end apart: 7 -> 16, of which waited for: 5 -> 6; matrix products, arithmetic and copies ran while one was open for 3% -> 0% of each run, Pallas kernels for 0% -> 0%
where the time goes in v1:
time: 59 us; the launch traced here: 58.4 us
  waiting for transfers between devices  26.2 us (44%)
  Pallas kernels  18.5 us (31%)
  starting transfers between devices  12.1 us (21%)
  between operations  0.84 us (1%)
  local copies, waits for them, and re-layouts  0.78 us (1%)
    ppermute x16, waiting for transfers between devices, along(): lax.ppermute(block, axis, [(i, target(i) % size) for i in range(size)])  26.2 us
    pallas_call x1, Pallas kernels, attend(): pl.pallas_call(functools.partial(attend_kernel, n, count, offsets, step_c...  15.3 us
    ppermute x16, starting transfers between devices, along(): lax.ppermute(block, axis, [(i, target(i) % size) for i in range(size)])  12.1 us
    pallas_call x1, Pallas kernels, pack(): pl.pallas_call(functools.partial(pack_kernel, count), out_shape=(q_shape,...  3.18 us
  transfers between devices with their start and end apart: 16, of which 6 were waited for; matrix products, arithmetic and copies ran while one was open for 0% of the time, Pallas kernels for 0%

profile of v1, /device:TPU:1, one launch (start us, length us, event | category | flops | bytes accessed | tf_op | source)
XLA Modules:
  0.0 58.4 jit_solution(9465928549355606022)
XLA Ops:
  0.6 3.2 %shard_map.58 = (bf16[2,1024,128]{2,1,0:T(8,128)(2,1)}, bf16[2,1024,128]{2,1,0:T(8,128)(2,1)}, bf16[2,2,128,128]{3,2,1,0:T(8,128)(2,1)}, bf16[2,2,128,128]{3,2,1,0:T(8,128)(2,1)}) custom-call(bf16[1,128,32,128]{3,2,1,0:T(8,128)(2,1)} %refs_0_.1, bf16[1,128,4,128]{3,2,1,0:T(4,128)(2,1)} %refs_1_.1, bf16[1,128,4,128]{3,2,1,0:T(4,128)(2,1)} %refs_2_.1), custom_call_target="tpu_custom_call" | custom-call | tf_op jit(solution)/shard_map/pallas_call | solution.py:57
  3.8 2.1 %collective-permute-start.1 = (bf16[2,2,128,128]{3,2,1,0:T(8,128)(2,1)}, bf16[2,2,128,128]{3,2,1,0:T(8,128)(2,1)S(1)}, u32[]{:S(2)}, u32[]{:S(2)}) collective-permute-start(bf16[2,2,128,128]{3,2,1,0:T(8,128)(2,1)} %get-tuple-element.10), channel_id=1, source_target_pairs={{0,1},{1,0},{2,3},{3,2},{4,5},{5,4},{6,7},{7,6},{8,9},{9,8},{10,11... | collective-permute-start | bytes 393224 | tf_op jit(solution)/shard_map/ppermute | solution.py:237
  5.9 3.1 %collective-permute-start.6 = (bf16[2,2,128,128]{3,2,1,0:T(8,128)(2,1)}, bf16[2,2,128,128]{3,2,1,0:T(8,128)(2,1)S(1)}, u32[]{:S(2)}, u32[]{:S(2)}) collective-permute-start(bf16[2,2,128,128]{3,2,1,0:T(8,128)(2,1)} %get-tuple-element.9.refs_2_), channel_id=1, source_target_pairs={{0,2},{2,16},{4,6},{6,20},{8,10},{10,24},{12,14},{14,28},{16,18},{... | collective-permute-start | bytes 393224 | tf_op jit(solution)/shard_map/ppermute | solution.py:237
  9.0 1.2 %collective-permute-start.4 = (bf16[2,2,128,128]{3,2,1,0:T(8,128)(2,1)}, bf16[2,2,128,128]{3,2,1,0:T(8,128)(2,1)S(1)}, u32[]{:S(2)}, u32[]{:S(2)}) collective-permute-start(bf16[2,2,128,128]{3,2,1,0:T(8,128)(2,1)} %get-tuple-element.9.refs_2_), channel_id=1, source_target_pairs={{0,4},{2,6},{4,16},{6,18},{8,12},{10,14},{12,24},{14,26},{16,20},{... | collective-permute-start | bytes 393224 | tf_op jit(solution)/shard_map/ppermute | solution.py:237
  10.2 0.2 collective-permute-start
  10.5 1.3 %collective-permute-start.2 = (bf16[2,2,128,128]{3,2,1,0:T(8,128)(2,1)}, bf16[2,2,128,128]{3,2,1,0:T(8,128)(2,1)S(1)}, u32[]{:S(2)}, u32[]{:S(2)}) collective-permute-start(bf16[2,2,128,128]{3,2,1,0:T(8,128)(2,1)} %get-tuple-element.9.refs_2_), channel_id=1, source_target_pairs={{0,8},{2,10},{4,12},{6,14},{8,16},{10,18},{12,20},{14,22},{16,24},... | collective-permute-start | bytes 393224 | tf_op jit(solution)/shard_map/ppermute | solution.py:237
  11.8 0.0 collective-permute-done.1.refs_3_
  11.8 1.2 %collective-permute-start.7 = (bf16[2,2,128,128]{3,2,1,0:T(8,128)(2,1)S(1)}, bf16[2,2,128,128]{3,2,1,0:T(8,128)(2,1)S(1)}, u32[]{:S(2)}, u32[]{:S(2)}) collective-permute-start(bf16[2,2,128,128]{3,2,1,0:T(8,128)(2,1)S(1)} %collective-permute-done.1.refs_3_), channel_id=1, source_target_pairs={{0,2},{2,16},{4,6},{6,20},{8,10},{10,24},{12,14},{14,28},{16,18},{... | collective-permute-start | bytes 393224 | tf_op jit(solution)/shard_map/ppermute | solution.py:237
  13.0 0.0 collective-permute-done.6.refs_8_
  13.0 1.2 %collective-permute-start.5 = (bf16[2,2,128,128]{3,2,1,0:T(8,128)(2,1)S(1)}, bf16[2,2,128,128]{3,2,1,0:T(8,128)(2,1)S(1)}, u32[]{:S(2)}, u32[]{:S(2)}) collective-permute-start(bf16[2,2,128,128]{3,2,1,0:T(8,128)(2,1)S(1)} %collective-permute-done.1.refs_3_), channel_id=1, source_target_pairs={{0,4},{2,6},{4,16},{6,18},{8,12},{10,14},{12,24},{14,26},{16,20},{... | collective-permute-start | bytes 393224 | tf_op jit(solution)/shard_map/ppermute | solution.py:237
  14.2 15.1 %collective-permute-done.4.refs_6_ = bf16[2,2,128,128]{3,2,1,0:T(8,128)(2,1)S(1)} collective-permute-done((bf16[2,2,128,128]{3,2,1,0:T(8,128)(2,1)}, bf16[2,2,128,128]{3,2,1,0:T(8,128)(2,1)S(1)}, u32[]{:S(2)}, u32[]{:S(2)}) %collective-permute-start.4) | collective-permute-done | bytes 131104 | tf_op jit(solution)/shard_map/ppermute | solution.py:237
  29.2 0.0 collective-permute-start.3
  29.2 0.0 collective-permute-done.2.refs_4_
  29.3 0.1 collective-permute-start.14
  29.3 0.0 collective-permute-done.7.refs_9_
  29.4 0.5 collective-permute-start.10
  29.8 4.1 %collective-permute-done.5.refs_7_ = bf16[2,2,128,128]{3,2,1,0:T(8,128)(2,1)S(1)} collective-permute-done((bf16[2,2,128,128]{3,2,1,0:T(8,128)(2,1)S(1)}, bf16[2,2,128,128]{3,2,1,0:T(8,128)(2,1)S(1)}, u32[]{:S(2)}, u32[]{:S(2)}) %collective-permute-start.5) | collective-permute-done | bytes 131104 | tf_op jit(solution)/shard_map/ppermute | solution.py:237
  33.9 0.0 collective-permute-start.8
  33.9 1.3 %collective-permute-done.3.refs_5_ = bf16[2,2,128,128]{3,2,1,0:T(8,128)(2,1)S(1)} collective-permute-done((bf16[2,2,128,128]{3,2,1,0:T(8,128)(2,1)S(1)}, bf16[2,2,128,128]{3,2,1,0:T(8,128)(2,1)S(1)}, u32[]{:S(2)}, u32[]{:S(2)}) %collective-permute-start.3) | collective-permute-done | bytes 131104 | tf_op jit(solution)/shard_map/ppermute | solution.py:237
  35.3 0.1 collective-permute-start.9
  35.4 0.0 collective-permute-done.14.refs_16_
  35.4 0.0 collective-permute-start.11
  35.4 0.0 collective-permute-done.10.refs_12_
  35.4 0.5 collective-permute-start.15
  35.9 1.8 %collective-permute-done.8.refs_10_ = bf16[2,2,128,128]{3,2,1,0:T(8,128)(2,1)S(1)} collective-permute-done((bf16[2,2,128,128]{3,2,1,0:T(8,128)(2,1)S(1)}, bf16[2,2,128,128]{3,2,1,0:T(8,128)(2,1)S(1)}, u32[]{:S(2)}, u32[]{:S(2)}) %collective-permute-start.8) | collective-permute-done | bytes 131104 | tf_op jit(solution)/shard_map/ppermute | solution.py:237
  37.8 0.0 collective-permute-start.12
  37.8 2.9 %collective-permute-done.9.refs_11_ = bf16[2,2,128,128]{3,2,1,0:T(8,128)(2,1)S(1)} collective-permute-done((bf16[2,2,128,128]{3,2,1,0:T(8,128)(2,1)S(1)}, bf16[2,2,128,128]{3,2,1,0:T(8,128)(2,1)S(1)}, u32[]{:S(2)}, u32[]{:S(2)}) %collective-permute-start.9) | collective-permute-done | bytes 131104 | tf_op jit(solution)/shard_map/ppermute | solution.py:237
  40.7 0.6 collective-permute-start.13
  41.3 0.0 collective-permute-done.15.refs_17_
  41.3 0.0 collective-permute-done.11.refs_13_
  41.3 0.0 collective-permute-done.12.refs_14_
  41.3 0.9 %collective-permute-done.13.refs_15_ = bf16[2,2,128,128]{3,2,1,0:T(8,128)(2,1)S(1)} collective-permute-done((bf16[2,2,128,128]{3,2,1,0:T(8,128)(2,1)S(1)}, bf16[2,2,128,128]{3,2,1,0:T(8,128)(2,1)S(1)}, u32[]{:S(2)}, u32[]{:S(2)}) %collective-permute-start.13) | collective-permute-done | bytes 131104 | tf_op jit(solution)/shard_map/ppermute | solution.py:237
  42.2 0.0 collective-permute-done.refs_1_
  42.3 0.0 copy-done.2
  42.3 0.0 copy-done.3
  42.3 0.0 copy-done.4
  42.3 0.0 copy-done.5
  42.3 0.0 copy-done.6
  42.3 0.0 copy-done.7
  42.3 0.0 copy-done.8
  42.3 0.0 copy-done.9
  42.3 0.0 copy-done.10
  42.3 0.0 copy-done.11
  42.4 0.0 copy-done.13
  42.4 0.0 copy-done.12
  42.4 0.5 copy-done.15
  42.9 0.2 copy-done
  43.1 15.3 %shard_map.59 = (f32[1,256,16,128]{3,2,1,0:T(8,128)}, f32[16,1,256]{2,1,0:T(1,128)}, f32[16,1,256]{2,1,0:T(1,128)}) custom-call(bf16[2,1024,128]{2,1,0:T(8,128)(2,1)} %get-tuple-element.7.refs_0_, bf16[2,1024,128]{2,1,0:T(8,128)(2,1)} %copy-done, bf16[2,2,128,128]{3,2,1,0:T(8,128)(2,1)} %get-tuple-element.9.refs_2_, bf16[2,2,128,128]{3,2,1,0:T(8,128)(2,1)} %copy-done.1, ...), custom_call_target="tpu_custom_call" | custom-call | tf_op jit(solution)/shard_map/pallas_call | solution.py:213
  (18 shorter events, 0.0 us)
Async XLA Ops:
  3.8 8.0 %collective-permute-start.1 = (bf16[2,2,128,128]{3,2,1,0:T(8,128)(2,1)}, bf16[2,2,128,128]{3,2,1,0:T(8,128)(2,1)S(1)}, u32[]{:S(2)}, u32[]{:S(2)}) collective-permute-start(bf16[2,2,128,128]{3,2,1,0:T(8,128)(2,1)} %get-tuple-element.10), channel_id=1, source_target_pairs={{0,1},{1,0},{2,3},{3,2},{4,5},{5,4},{6,7},{7,6},{8,9},{9,8},{10,11... | collective-permute-start | bytes 393224 | tf_op jit(solution)/shard_map/ppermute | solution.py:237
  5.9 7.1 %collective-permute-start.6 = (bf16[2,2,128,128]{3,2,1,0:T(8,128)(2,1)}, bf16[2,2,128,128]{3,2,1,0:T(8,128)(2,1)S(1)}, u32[]{:S(2)}, u32[]{:S(2)}) collective-permute-start(bf16[2,2,128,128]{3,2,1,0:T(8,128)(2,1)} %get-tuple-element.9.refs_2_), channel_id=1, source_target_pairs={{0,2},{2,16},{4,6},{6,20},{8,10},{10,24},{12,14},{14,28},{16,18},{... | collective-permute-start | bytes 393224 | tf_op jit(solution)/shard_map/ppermute | solution.py:237
  9.0 20.2 %collective-permute-start.4 = (bf16[2,2,128,128]{3,2,1,0:T(8,128)(2,1)}, bf16[2,2,128,128]{3,2,1,0:T(8,128)(2,1)S(1)}, u32[]{:S(2)}, u32[]{:S(2)}) collective-permute-start(bf16[2,2,128,128]{3,2,1,0:T(8,128)(2,1)} %get-tuple-element.9.refs_2_), channel_id=1, source_target_pairs={{0,4},{2,6},{4,16},{6,18},{8,12},{10,14},{12,24},{14,26},{16,20},{... | collective-permute-start | bytes 393224 | tf_op jit(solution)/shard_map/ppermute | solution.py:237
  10.2 32.0 %collective-permute-start = (bf16[2,1024,128]{2,1,0:T(8,128)(2,1)}, bf16[2,1024,128]{2,1,0:T(8,128)(2,1)S(1)}, u32[]{:S(2)}, u32[]{:S(2)}) collective-permute-start(bf16[2,1024,128]{2,1,0:T(8,128)(2,1)} %get-tuple-element.8), channel_id=1, source_target_pairs={{0,1},{1,0},{2,3},{3,2},{4,5},{5,4},{6,7},{7,6},{8,9},{9,8},{10,11... | collective-permute-start | bytes 1572872 | tf_op jit(solution)/shard_map/ppermute | solution.py:237
  10.5 18.8 %collective-permute-start.2 = (bf16[2,2,128,128]{3,2,1,0:T(8,128)(2,1)}, bf16[2,2,128,128]{3,2,1,0:T(8,128)(2,1)S(1)}, u32[]{:S(2)}, u32[]{:S(2)}) collective-permute-start(bf16[2,2,128,128]{3,2,1,0:T(8,128)(2,1)} %get-tuple-element.9.refs_2_), channel_id=1, source_target_pairs={{0,8},{2,10},{4,12},{6,14},{8,16},{10,18},{12,20},{14,22},{16,24},... | collective-permute-start | bytes 393224 | tf_op jit(solution)/shard_map/ppermute | solution.py:237
  11.8 30.5 %copy-start.1 = (bf16[2,2,128,128]{3,2,1,0:T(8,128)(2,1)}, bf16[2,2,128,128]{3,2,1,0:T(8,128)(2,1)S(1)}, u32[]{:S(2)}) copy-start(bf16[2,2,128,128]{3,2,1,0:T(8,128)(2,1)S(1)} %collective-permute-done.1.refs_3_) | copy-start | bytes 393220
  11.8 17.6 %collective-permute-start.7 = (bf16[2,2,128,128]{3,2,1,0:T(8,128)(2,1)S(1)}, bf16[2,2,128,128]{3,2,1,0:T(8,128)(2,1)S(1)}, u32[]{:S(2)}, u32[]{:S(2)}) collective-permute-start(bf16[2,2,128,128]{3,2,1,0:T(8,128)(2,1)S(1)} %collective-permute-done.1.refs_3_), channel_id=1, source_target_pairs={{0,2},{2,16},{4,6},{6,20},{8,10},{10,24},{12,14},{14,28},{16,18},{... | collective-permute-start | bytes 393224 | tf_op jit(solution)/shard_map/ppermute | solution.py:237
  13.0 29.3 %copy-start.2 = (bf16[2,2,128,128]{3,2,1,0:T(8,128)(2,1)}, bf16[2,2,128,128]{3,2,1,0:T(8,128)(2,1)S(1)}, u32[]{:S(2)}) copy-start(bf16[2,2,128,128]{3,2,1,0:T(8,128)(2,1)S(1)} %collective-permute-done.6.refs_8_) | copy-start | bytes 393220
  13.0 21.0 %collective-permute-start.5 = (bf16[2,2,128,128]{3,2,1,0:T(8,128)(2,1)S(1)}, bf16[2,2,128,128]{3,2,1,0:T(8,128)(2,1)S(1)}, u32[]{:S(2)}, u32[]{:S(2)}) collective-permute-start(bf16[2,2,128,128]{3,2,1,0:T(8,128)(2,1)S(1)} %collective-permute-done.1.refs_3_), channel_id=1, source_target_pairs={{0,4},{2,6},{4,16},{6,18},{8,12},{10,14},{12,24},{14,26},{16,20},{... | collective-permute-start | bytes 393224 | tf_op jit(solution)/shard_map/ppermute | solution.py:237
  29.2 13.0 %copy-start.3 = (bf16[2,2,128,128]{3,2,1,0:T(8,128)(2,1)}, bf16[2,2,128,128]{3,2,1,0:T(8,128)(2,1)S(1)}, u32[]{:S(2)}) copy-start(bf16[2,2,128,128]{3,2,1,0:T(8,128)(2,1)S(1)} %collective-permute-done.4.refs_6_) | copy-start | bytes 393220
  29.2 6.0 %collective-permute-start.3 = (bf16[2,2,128,128]{3,2,1,0:T(8,128)(2,1)S(1)}, bf16[2,2,128,128]{3,2,1,0:T(8,128)(2,1)S(1)}, u32[]{:S(2)}, u32[]{:S(2)}) collective-permute-start(bf16[2,2,128,128]{3,2,1,0:T(8,128)(2,1)S(1)} %collective-permute-done.1.refs_3_), channel_id=1, source_target_pairs={{0,8},{2,10},{4,12},{6,14},{8,16},{10,18},{12,20},{14,22},{16,24},... | collective-permute-start | bytes 393224 | tf_op jit(solution)/shard_map/ppermute | solution.py:237
  29.2 13.0 %copy-start.4 = (bf16[2,2,128,128]{3,2,1,0:T(8,128)(2,1)}, bf16[2,2,128,128]{3,2,1,0:T(8,128)(2,1)S(1)}, u32[]{:S(2)}) copy-start(bf16[2,2,128,128]{3,2,1,0:T(8,128)(2,1)S(1)} %collective-permute-done.2.refs_4_) | copy-start | bytes 393220
  29.3 6.2 %collective-permute-start.14 = (bf16[2,2,128,128]{3,2,1,0:T(8,128)(2,1)S(1)}, bf16[2,2,128,128]{3,2,1,0:T(8,128)(2,1)S(1)}, u32[]{:S(2)}, u32[]{:S(2)}) collective-permute-start(bf16[2,2,128,128]{3,2,1,0:T(8,128)(2,1)S(1)} %collective-permute-done.4.refs_6_), channel_id=1, source_target_pairs={{0,2},{2,0},{4,6},{6,4},{8,10},{10,8},{12,14},{14,12},{16,18},{18,... | collective-permute-start | bytes 393224 | tf_op jit(solution)/shard_map/ppermute | solution.py:237
  29.3 12.9 %copy-start.5 = (bf16[2,2,128,128]{3,2,1,0:T(8,128)(2,1)}, bf16[2,2,128,128]{3,2,1,0:T(8,128)(2,1)S(1)}, u32[]{:S(2)}) copy-start(bf16[2,2,128,128]{3,2,1,0:T(8,128)(2,1)S(1)} %collective-permute-done.7.refs_9_) | copy-start | bytes 393220
  29.4 6.1 %collective-permute-start.10 = (bf16[2,2,128,128]{3,2,1,0:T(8,128)(2,1)S(1)}, bf16[2,2,128,128]{3,2,1,0:T(8,128)(2,1)S(1)}, u32[]{:S(2)}, u32[]{:S(2)}) collective-permute-start(bf16[2,2,128,128]{3,2,1,0:T(8,128)(2,1)S(1)} %collective-permute-done.2.refs_4_), channel_id=1, source_target_pairs={{0,2},{2,0},{4,6},{6,4},{8,10},{10,8},{12,14},{14,12},{16,18},{18,... | collective-permute-start | bytes 393224 | tf_op jit(solution)/shard_map/ppermute | solution.py:237
  33.9 8.4 %copy-start.6 = (bf16[2,2,128,128]{3,2,1,0:T(8,128)(2,1)}, bf16[2,2,128,128]{3,2,1,0:T(8,128)(2,1)S(1)}, u32[]{:S(2)}) copy-start(bf16[2,2,128,128]{3,2,1,0:T(8,128)(2,1)S(1)} %collective-permute-done.5.refs_7_) | copy-start | bytes 393220
  33.9 3.8 %collective-permute-start.8 = (bf16[2,2,128,128]{3,2,1,0:T(8,128)(2,1)S(1)}, bf16[2,2,128,128]{3,2,1,0:T(8,128)(2,1)S(1)}, u32[]{:S(2)}, u32[]{:S(2)}) collective-permute-start(bf16[2,2,128,128]{3,2,1,0:T(8,128)(2,1)S(1)} %collective-permute-done.2.refs_4_), channel_id=1, source_target_pairs={{0,4},{2,6},{4,0},{6,2},{8,12},{10,14},{12,8},{14,10},{16,20},{18,... | collective-permute-start | bytes 393224 | tf_op jit(solution)/shard_map/ppermute | solution.py:237
  35.3 7.0 %copy-start.7 = (bf16[2,2,128,128]{3,2,1,0:T(8,128)(2,1)}, bf16[2,2,128,128]{3,2,1,0:T(8,128)(2,1)S(1)}, u32[]{:S(2)}) copy-start(bf16[2,2,128,128]{3,2,1,0:T(8,128)(2,1)S(1)} %collective-permute-done.3.refs_5_) | copy-start | bytes 393220
  35.3 5.4 %collective-permute-start.9 = (bf16[2,2,128,128]{3,2,1,0:T(8,128)(2,1)S(1)}, bf16[2,2,128,128]{3,2,1,0:T(8,128)(2,1)S(1)}, u32[]{:S(2)}, u32[]{:S(2)}) collective-permute-start(bf16[2,2,128,128]{3,2,1,0:T(8,128)(2,1)S(1)} %collective-permute-done.3.refs_5_), channel_id=1, source_target_pairs={{0,4},{2,6},{4,0},{6,2},{8,12},{10,14},{12,8},{14,10},{16,20},{18,... | collective-permute-start | bytes 393224 | tf_op jit(solution)/shard_map/ppermute | solution.py:237
  35.4 6.9 %copy-start.8 = (bf16[2,2,128,128]{3,2,1,0:T(8,128)(2,1)}, bf16[2,2,128,128]{3,2,1,0:T(8,128)(2,1)S(1)}, u32[]{:S(2)}) copy-start(bf16[2,2,128,128]{3,2,1,0:T(8,128)(2,1)S(1)} %collective-permute-done.14.refs_16_) | copy-start | bytes 393220
  35.4 5.8 %collective-permute-start.11 = (bf16[2,2,128,128]{3,2,1,0:T(8,128)(2,1)S(1)}, bf16[2,2,128,128]{3,2,1,0:T(8,128)(2,1)S(1)}, u32[]{:S(2)}, u32[]{:S(2)}) collective-permute-start(bf16[2,2,128,128]{3,2,1,0:T(8,128)(2,1)S(1)} %collective-permute-done.3.refs_5_), channel_id=1, source_target_pairs={{0,2},{2,0},{4,6},{6,4},{8,10},{10,8},{12,14},{14,12},{16,18},{18,... | collective-permute-start | bytes 393224 | tf_op jit(solution)/shard_map/ppermute | solution.py:237
  35.4 6.9 %copy-start.9 = (bf16[2,2,128,128]{3,2,1,0:T(8,128)(2,1)}, bf16[2,2,128,128]{3,2,1,0:T(8,128)(2,1)S(1)}, u32[]{:S(2)}) copy-start(bf16[2,2,128,128]{3,2,1,0:T(8,128)(2,1)S(1)} %collective-permute-done.10.refs_12_) | copy-start | bytes 393220
  35.4 5.8 %collective-permute-start.15 = (bf16[2,2,128,128]{3,2,1,0:T(8,128)(2,1)S(1)}, bf16[2,2,128,128]{3,2,1,0:T(8,128)(2,1)S(1)}, u32[]{:S(2)}, u32[]{:S(2)}) collective-permute-start(bf16[2,2,128,128]{3,2,1,0:T(8,128)(2,1)S(1)} %collective-permute-done.5.refs_7_), channel_id=1, source_target_pairs={{0,2},{2,0},{4,6},{6,4},{8,10},{10,8},{12,14},{14,12},{16,18},{18,... | collective-permute-start | bytes 393224 | tf_op jit(solution)/shard_map/ppermute | solution.py:237
  37.8 4.6 %copy-start.10 = (bf16[2,2,128,128]{3,2,1,0:T(8,128)(2,1)}, bf16[2,2,128,128]{3,2,1,0:T(8,128)(2,1)S(1)}, u32[]{:S(2)}) copy-start(bf16[2,2,128,128]{3,2,1,0:T(8,128)(2,1)S(1)} %collective-permute-done.8.refs_10_) | copy-start | bytes 393220
  37.8 3.5 %collective-permute-start.12 = (bf16[2,2,128,128]{3,2,1,0:T(8,128)(2,1)S(1)}, bf16[2,2,128,128]{3,2,1,0:T(8,128)(2,1)S(1)}, u32[]{:S(2)}, u32[]{:S(2)}) collective-permute-start(bf16[2,2,128,128]{3,2,1,0:T(8,128)(2,1)S(1)} %collective-permute-done.8.refs_10_), channel_id=1, source_target_pairs={{0,2},{2,0},{4,6},{6,4},{8,10},{10,8},{12,14},{14,12},{16,18},{18,... | collective-permute-start | bytes 393224 | tf_op jit(solution)/shard_map/ppermute | solution.py:237
  40.7 1.7 %copy-start.11 = (bf16[2,2,128,128]{3,2,1,0:T(8,128)(2,1)}, bf16[2,2,128,128]{3,2,1,0:T(8,128)(2,1)S(1)}, u32[]{:S(2)}) copy-start(bf16[2,2,128,128]{3,2,1,0:T(8,128)(2,1)S(1)} %collective-permute-done.9.refs_11_) | copy-start | bytes 393220
  40.7 1.6 %collective-permute-start.13 = (bf16[2,2,128,128]{3,2,1,0:T(8,128)(2,1)S(1)}, bf16[2,2,128,128]{3,2,1,0:T(8,128)(2,1)S(1)}, u32[]{:S(2)}, u32[]{:S(2)}) collective-permute-start(bf16[2,2,128,128]{3,2,1,0:T(8,128)(2,1)S(1)} %collective-permute-done.9.refs_11_), channel_id=1, source_target_pairs={{0,2},{2,0},{4,6},{6,4},{8,10},{10,8},{12,14},{14,12},{16,18},{18,... | collective-permute-start | bytes 393224 | tf_op jit(solution)/shard_map/ppermute | solution.py:237
  41.3 1.1 %copy-start.13 = (bf16[2,2,128,128]{3,2,1,0:T(8,128)(2,1)}, bf16[2,2,128,128]{3,2,1,0:T(8,128)(2,1)S(1)}, u32[]{:S(2)}) copy-start(bf16[2,2,128,128]{3,2,1,0:T(8,128)(2,1)S(1)} %collective-permute-done.15.refs_17_) | copy-start | bytes 393220
  41.3 1.1 %copy-start.12 = (bf16[2,2,128,128]{3,2,1,0:T(8,128)(2,1)}, bf16[2,2,128,128]{3,2,1,0:T(8,128)(2,1)S(1)}, u32[]{:S(2)}) copy-start(bf16[2,2,128,128]{3,2,1,0:T(8,128)(2,1)S(1)} %collective-permute-done.11.refs_13_) | copy-start | bytes 393220
  41.3 1.1 %copy-start.14 = (bf16[2,2,128,128]{3,2,1,0:T(8,128)(2,1)}, bf16[2,2,128,128]{3,2,1,0:T(8,128)(2,1)S(1)}, u32[]{:S(2)}) copy-start(bf16[2,2,128,128]{3,2,1,0:T(8,128)(2,1)S(1)} %collective-permute-done.12.refs_14_) | copy-start | bytes 393220
  42.2 0.6 %copy-start.15 = (bf16[2,2,128,128]{3,2,1,0:T(8,128)(2,1)}, bf16[2,2,128,128]{3,2,1,0:T(8,128)(2,1)S(1)}, u32[]{:S(2)}) copy-start(bf16[2,2,128,128]{3,2,1,0:T(8,128)(2,1)S(1)} %collective-permute-done.13.refs_15_) | copy-start | bytes 393220
  42.2 0.9 %copy-start = (bf16[2,1024,128]{2,1,0:T(8,128)(2,1)}, bf16[2,1024,128]{2,1,0:T(8,128)(2,1)S(1)}, u32[]{:S(2)}) copy-start(bf16[2,1024,128]{2,1,0:T(8,128)(2,1)S(1)} %collective-permute-done.refs_1_) | copy-start | bytes 1572868

commit v2 on v1

--- a/solution.py
+++ b/solution.py
@@ -19,55 +19,57 @@
 NEG = -1e30
 
 
-def pack_kernel(count, *refs):
-    q_ref, k_ref, v_ref = refs[:3]
-    q_outs, kv_outs = refs[3 : 3 + count], refs[3 + count :]
-    rows, kv_heads = k_ref.shape[1:3]
-    per = kv_heads // count
-    h = lax.axis_index("head")
+def slot_of(head, per, count):
+    return lax.rem(head // per - lax.axis_index("head") + count, count)
+
+
+def pack_kv_kernel(k_ref, v_ref, *outs):
+    count = len(outs)
+    per = k_ref.shape[2] // count
     k = k_ref[0].astype(F32)
     v = v_ref[0].astype(F32)
-    for head in range(kv_heads):
+    for head in range(k_ref.shape[2]):
         kh = k[:, head, :].astype(BF16)
         vh = v[:, head, :].astype(BF16)
-        slot = lax.rem(head // per - h + count, count)
         for d in range(count):
 
-            @pl.when(slot == d)
+            @pl.when(slot_of(head, per, count) == d)
             def _():
-                kv_outs[d][0, head % per] = kh
-                kv_outs[d][1, head % per] = vh
-
-    for head in range(kv_heads):
-        slot = lax.rem(head // per - h + count, count)
+                outs[d][0, head % per] = kh
+                outs[d][1, head % per] = vh
+
+
+def pack_q_kernel(q_ref, *outs):
+    count = len(outs)
+    rows, heads, width = q_ref.shape[1:]
+    per = heads // GROUP // count
+    for head in range(heads // GROUP):
         qh = q_ref[0, :, head * GROUP : (head + 1) * GROUP, :].astype(F32)
-        qh = qh.reshape(rows * GROUP, qh.shape[-1]).astype(BF16)
+        qh = qh.reshape(rows * GROUP, width).astype(BF16)
         for d in range(count):
 
-            @pl.when(slot == d)
+            @pl.when(slot_of(head, per, count) == d)
             def _():
-                q_outs[d][head % per] = qh
-
-
-def pack(queries, keys, values, count):
-    rows, width = keys.shape[1], keys.shape[3]
-    per = keys.shape[2] // count
-    q_shape = jax.ShapeDtypeStruct((per, rows * GROUP, width), BF16)
-    kv_shape = jax.ShapeDtypeStruct((2, per, rows, width), BF16)
-    outs = pl.pallas_call(
-        functools.partial(pack_kernel, count),
-        out_shape=(q_shape,) * count + (kv_shape,) * count,
-        in_specs=[pl.BlockSpec(memory_space=pltpu.VMEM)] * 3,
-        out_specs=[pl.BlockSpec(memory_space=pltpu.VMEM)] * (2 * count),
+                outs[d][head % per] = qh
+
+
+def pack(kernel, shape, count, *arrays):
+    return pl.pallas_call(
+        kernel,
+        out_shape=(jax.ShapeDtypeStruct(shape, BF16),) * count,
+        in_specs=[pl.BlockSpec(memory_space=pltpu.VMEM)] * len(arrays),
+        out_specs=[pl.BlockSpec(memory_space=pltpu.VMEM)] * count,
         compiler_params=pltpu.CompilerParams(vmem_limit_bytes=VMEM_LIMIT),
-    )(queries, keys, values)
-    return list(outs[:count]), list(outs[count:])
-
-
-def attend_kernel(n, count, offsets, step_chunks, block, *refs):
+    )(*arrays)
+
+
+def attend_kernel(n, count, singles, offsets, step_chunks, block, *refs):
     total = len(offsets) * count
-    q_hbm, kv_hbm = refs[:count], refs[count : count + total]
-    out_ref, max_ref, sum_ref, qbuf, kbuf, vbuf, mbuf, lbuf, qsem, ksem = refs[count + total :]
+    merged = len(offsets) - singles // count
+    q_hbm, refs = refs[:count], refs[count:]
+    kv_hbm, refs = list(refs[:singles]), refs[singles:]
+    kv_hbm += [refs[a].at[d] for a in range(merged) for d in range(count)]
+    out_ref, max_ref, sum_ref, qbuf, kbuf, vbuf, mbuf, lbuf, qsem, ksem = refs[merged:]
     per, rows, width = kv_hbm[0].shape[1:]
     half = count * rows // 2
     m_rows = rows * GROUP
@@ -203,21 +205,21 @@
                     sum_ref[g * GROUP : (g + 1) * GROUP, 0, d * rows : (d + 1) * rows] = sums
 
 
-def attend(q_list, kv_list, offsets, n):
+def attend(q_list, kv_list, merged, offsets, n):
     count = len(q_list)
     per, m_rows, width = q_list[0].shape
     rows = m_rows // GROUP
     step_chunks = 512 // rows
-    longest = (len(kv_list) + step_chunks) * rows
-    total = len(kv_list)
+    total = len(offsets) * count
+    longest = (total + step_chunks) * rows
     return pl.pallas_call(
-        functools.partial(attend_kernel, n, count, offsets, step_chunks, min(512, m_rows)),
+        functools.partial(attend_kernel, n, count, len(kv_list), offsets, step_chunks, min(512, m_rows)),
         out_shape=(
             jax.ShapeDtypeStruct((1, count * rows, per * GROUP, width), F32),
             jax.ShapeDtypeStruct((per * GROUP, 1, count * rows), F32),
             jax.ShapeDtypeStruct((per * GROUP, 1, count * rows), F32),
         ),
-        in_specs=[pl.BlockSpec(memory_space=pl.ANY)] * (count + total),
+        in_specs=[pl.BlockSpec(memory_space=pl.ANY)] * (count + len(kv_list) + len(merged)),
         out_specs=[pl.BlockSpec(memory_space=pltpu.VMEM)] * 3,
         scratch_shapes=[
             pltpu.VMEM((count, per, m_rows, width), BF16),
@@ -229,7 +231,7 @@
             pltpu.SemaphoreType.DMA((count, total, 2)),
         ],
         compiler_params=pltpu.CompilerParams(vmem_limit_bytes=VMEM_LIMIT),
-    )(*q_list, *kv_list)
+    )(*q_list, *kv_list, *merged)
 
 
 def along(block, axis, target):
@@ -240,38 +242,43 @@
 def local(queries, keys, values):
     n = lax.axis_size("ctx")
     count = lax.axis_size("head")
-    q_out, kv_out = pack(queries, keys, values, count)
+    rows, kv_heads, width = keys.shape[1:]
+    per = kv_heads // count
+    me = lax.axis_index("ctx")
     swap = lambda x, d: along(x, "head", lambda i: i + d)
-    own = [kv_out[0]] + [swap(kv_out[d], d) for d in range(1, count)]
-    q_in = [q_out[0]] + [swap(q_out[d], d) for d in range(1, count)]
+    ctx = lambda xs, target: [along(x, "ctx", target) for x in xs]
+
+    kv = pack(pack_kv_kernel, (2, per, rows, width), count, keys, values)
+    own = [kv[0]] + [swap(kv[d], d) for d in range(1, count)]
+    q = pack(pack_q_kernel, (per, rows * GROUP, width), count, queries)
+    q = [q[0]] + [swap(q[d], d) for d in range(1, count)]
 
     layer = LAYER
-    ctx = lambda xs, target: [along(x, "ctx", target) for x in xs]
     up = ctx(own, lambda i: i + layer)
-    wide = ctx(own, lambda i: i + 2 if i & 2 == 0 else i + layer + 2)
-    near = ctx(own, lambda i: i + 1 if i & 1 == 0 else i + 2 * layer - 1)
-    up_x = ctx(up, lambda i: i ^ 2)
-    up_c = ctx(up, lambda i: i ^ 1)
-    up_xc = ctx(up_x, lambda i: i ^ 1)
-    wide_c = ctx(wide, lambda i: i ^ 1)
-
-    def flip(p, bit):
-        return jnp.where(lax.rem(p // bit, 2) == 1, bit, -bit)
-
-    wide_at = lambda p: jnp.where(lax.rem(p // 2, 2) == 1, 2, layer + 2)
-    near_at = lambda p: jnp.where(lax.rem(p, 2) == 1, 1, 2 * layer - 1)
+    far = ctx(up, lambda i: i + layer // 2)
+    odd = ctx(up, lambda i: i + layer - 1 if i & 1 else i + 1)
+    column = lax.rem(me // 2, 2) == 0
+    side = jnp.concatenate([jnp.where(column, a, b)[None] for a, b in zip(own, up)])
+    side = along(side, "ctx", lambda i: i ^ 2)
+    core = lax.rem(me, 2) == 0
+    next_to = jnp.concatenate([jnp.where(core, a, b)[None] for a, b in zip(own, up)])
+    next_to = along(next_to, "ctx", lambda i: i ^ 1)
+    far_c = ctx(far, lambda i: i ^ 1)
+    side_c = along(side, "ctx", lambda i: i ^ 1)
+
+    bit = lambda p, even, other: jnp.where(lax.rem(p, 2) == 0, even, other)
     offsets = [
         lambda p: 0,
         lambda p: layer,
-        wide_at,
-        near_at,
-        lambda p: layer + flip(p, 2),
-        lambda p: layer + flip(p, 1),
-        lambda p: layer + flip(p, 1) + flip(p, 2),
-        lambda p: flip(p, 1) + wide_at(p),
+        lambda p: layer + 2,
+        lambda p: bit(p, layer + 3, layer + 1),
+        lambda p: bit(p, layer + 1, layer + 3),
+        lambda p: 2,
+        lambda p: bit(p, 3, 1),
+        lambda p: bit(p, 1, 3),
     ]
-    blocks = own + up + wide + near + up_x + up_c + up_xc + wide_c
-    return attend(q_in, blocks, offsets, n)
+    blocks = own + up + far + odd + far_c
+    return attend(q, blocks, [side, next_to, side_c], offsets, n)
 
 
 def solution(mesh):

time: 59 us -> 50.7 us (0.86)
  waiting for transfers between devices: 26.2 us -> 13.3 us
  starting transfers between devices: 12.1 us -> 14 us
  Pallas kernels: 18.5 us -> 20.1 us
  other arithmetic: 0 us -> 1.05 us
    ppermute x16 -> x13, waiting for transfers between devices: 26.2 us -> 13.3 us  [along(): lax.ppermute(block, axis, [(i, target(i) % size) for i in range(size)])]
    ppermute x16 -> x13, starting transfers between devices: 12.1 us -> 14 us  [along(): lax.ppermute(block, axis, [(i, target(i) % size) for i in range(size)])]
    pallas_call x2 -> x3, Pallas kernels: 18.5 us -> 20.1 us  [the longest x1 15.4 us: attend(): pl.pallas_call(functools.partial(attend_kernel, n, count, len(kv_list), o...]
    broadcast_in_dim x0 -> x2, other arithmetic: none -> 0.99 us  [local(): jnp.where(core, a, b)[None]]
  transfers between devices with their start and end apart: 16 -> 13, of which waited for: 6 -> 6; matrix products, arithmetic and copies ran while one was open for 0% -> 2% of each run, Pallas kernels for 0% -> 5%
where the time goes in v2:
time: 50.7 us; the launch traced here: 50.1 us
  Pallas kernels  20.1 us (40%)
  starting transfers between devices  14 us (28%)
  waiting for transfers between devices  13.3 us (26%)
  other arithmetic  1.05 us (2%)
  local copies, waits for them, and re-layouts  0.94 us (2%)
  between operations  0.77 us (2%)
    pallas_call x1, Pallas kernels, attend(): pl.pallas_call(functools.partial(attend_kernel, n, count, len(kv_list), o...  15.4 us
    ppermute x13, starting transfers between devices, along(): lax.ppermute(block, axis, [(i, target(i) % size) for i in range(size)])  14 us
    ppermute x13, waiting for transfers between devices, along(): lax.ppermute(block, axis, [(i, target(i) % size) for i in range(size)])  13.3 us
    pallas_call x2, Pallas kernels, pack(): pl.pallas_call(kernel, out_shape=(jax.ShapeDtypeStruct(shape, BF16),) * c...  4.69 us
  transfers between devices with their start and end apart: 13, of which 6 were waited for; matrix products, arithmetic and copies ran while one was open for 2% of the time, Pallas kernels for 5%

profile of v2, /device:TPU:1, one launch (start us, length us, event | category | flops | bytes accessed | tf_op | source)
XLA Modules:
  0.0 50.1 jit_solution(18378427416411235174)
XLA Ops:
  0.6 2.2 %shard_map.59 = (bf16[2,2,128,128]{3,2,1,0:T(8,128)(2,1)}, bf16[2,2,128,128]{3,2,1,0:T(8,128)(2,1)}) custom-call(bf16[1,128,4,128]{3,2,1,0:T(4,128)(2,1)} %k_ref.1, bf16[1,128,4,128]{3,2,1,0:T(4,128)(2,1)} %v_ref.1), custom_call_target="tpu_custom_call" | custom-call | tf_op jit(solution)/shard_map/pallas_call | solution.py:57
  2.8 2.1 %collective-permute-start.1 = (bf16[2,2,128,128]{3,2,1,0:T(8,128)(2,1)}, bf16[2,2,128,128]{3,2,1,0:T(8,128)(2,1)S(1)}, u32[]{:S(2)}, u32[]{:S(2)}) collective-permute-start(bf16[2,2,128,128]{3,2,1,0:T(8,128)(2,1)} %get-tuple-element.10), channel_id=1, source_target_pairs={{0,1},{1,0},{2,3},{3,2},{4,5},{5,4},{6,7},{7,6},{8,9},{9,8},{10,11... | collective-permute-start | bytes 393224 | tf_op jit(solution)/shard_map/ppermute | solution.py:239
  4.9 1.3 %collective-permute-start.2 = (bf16[2,2,128,128]{3,2,1,0:T(8,128)(2,1)}, bf16[2,2,128,128]{3,2,1,0:T(8,128)(2,1)S(1)}, u32[]{:S(2)}, u32[]{:S(2)}) collective-permute-start(bf16[2,2,128,128]{3,2,1,0:T(8,128)(2,1)} %get-tuple-element.9.refs_2_), channel_id=1, source_target_pairs={{0,8},{2,10},{4,12},{6,14},{8,16},{10,18},{12,20},{14,22},{16,24},... | collective-permute-start | bytes 393224 | tf_op jit(solution)/shard_map/ppermute | solution.py:239
  6.2 2.5 %shard_map.58 = (bf16[2,1024,128]{2,1,0:T(8,128)(2,1)}, bf16[2,1024,128]{2,1,0:T(8,128)(2,1)}) custom-call(bf16[1,128,32,128]{3,2,1,0:T(8,128)(2,1)} %q_ref.1), custom_call_target="tpu_custom_call" | custom-call | tf_op jit(solution)/shard_map/pallas_call | solution.py:57
  8.7 0.2 collective-permute-start
  8.9 0.0 collective-permute-done.1.refs_3_
  8.9 0.0 copy-start
  8.9 1.3 %collective-permute-start.3 = (bf16[2,2,128,128]{3,2,1,0:T(8,128)(2,1)S(1)}, bf16[2,2,128,128]{3,2,1,0:T(8,128)(2,1)S(1)}, u32[]{:S(2)}, u32[]{:S(2)}) collective-permute-start(bf16[2,2,128,128]{3,2,1,0:T(8,128)(2,1)S(1)} %collective-permute-done.1.refs_3_), channel_id=1, source_target_pairs={{0,8},{2,10},{4,12},{6,14},{8,16},{10,18},{12,20},{14,22},{16,24},... | collective-permute-start | bytes 393224 | tf_op jit(solution)/shard_map/ppermute | solution.py:239
  10.2 0.6 %collective-permute-done.2.refs_4_ = bf16[2,2,128,128]{3,2,1,0:T(8,128)(2,1)S(1)} collective-permute-done((bf16[2,2,128,128]{3,2,1,0:T(8,128)(2,1)}, bf16[2,2,128,128]{3,2,1,0:T(8,128)(2,1)S(1)}, u32[]{:S(2)}, u32[]{:S(2)}) %collective-permute-start.2) | collective-permute-done | bytes 131104 | tf_op jit(solution)/shard_map/ppermute | solution.py:239
  10.8 0.0 copy-start.1
  10.8 1.0 %select_bitcast_fusion.1 = (bf16[1,2,2,128,128]{4,3,2,1,0:T(8,128)(2,1)S(1)}, bf16[1,2,2,128,128]{4,3,2,1,0:T(8,128)(2,1)S(1)}) fusion(bf16[2,2,128,128]{3,2,1,0:T(8,128)(2,1)} %get-tuple-element.9.refs_2_, bf16[2,2,128,128]{3,2,1,0:T(8,128)(2,1)S(1)} %collective-permute-done.2.refs_4_, pred[]{:T(512)S(6)} %eq.7, pred[]{:T(512)S(6)} %eq.6), kind=kLoop, calls=%fused_computation.3 | loop fusion | flops 131072 | bytes 524290 | tf_op jit(solution)/shard_map/broadcast_in_dim | solution.py:264
  11.8 2.8 %collective-permute-done.3.refs_5_ = bf16[2,2,128,128]{3,2,1,0:T(8,128)(2,1)S(1)} collective-permute-done((bf16[2,2,128,128]{3,2,1,0:T(8,128)(2,1)S(1)}, bf16[2,2,128,128]{3,2,1,0:T(8,128)(2,1)S(1)}, u32[]{:S(2)}, u32[]{:S(2)}) %collective-permute-start.3) | collective-permute-done | bytes 131104 | tf_op jit(solution)/shard_map/ppermute | solution.py:239
  14.5 0.0 copy-start.2
  14.6 1.3 %collective-permute-start.10 = (bf16[2,2,2,128,128]{4,3,2,1,0:T(8,128)(2,1)S(1)}, bf16[2,2,2,128,128]{4,3,2,1,0:T(8,128)(2,1)S(1)}, u32[]{:S(2)}, u32[]{:S(2)}) collective-permute-start(bf16[2,2,2,128,128]{4,3,2,1,0:T(8,128)(2,1)S(1)} %pad_maximum_fusion), channel_id=1, source_target_pairs={{0,4},{2,6},{4,0},{6,2},{8,12},{10,14},{12,8},{14,10},{16,20},{18,... | collective-permute-start | bytes 786440 | tf_op jit(solution)/shard_map/ppermute | solution.py:239
  15.9 2.3 %collective-permute-start.6 = (bf16[2,2,128,128]{3,2,1,0:T(8,128)(2,1)S(1)}, bf16[2,2,128,128]{3,2,1,0:T(8,128)(2,1)S(1)}, u32[]{:S(2)}, u32[]{:S(2)}) collective-permute-start(bf16[2,2,128,128]{3,2,1,0:T(8,128)(2,1)S(1)} %collective-permute-done.2.refs_4_), channel_id=1, source_target_pairs={{0,2},{2,8},{4,6},{6,12},{8,10},{10,16},{12,14},{14,20},{16,18},{1... | collective-permute-start | bytes 393224 | tf_op jit(solution)/shard_map/ppermute | solution.py:239
  18.2 0.3 collective-permute-start.4
  18.5 0.3 collective-permute-start.7
  18.8 1.3 %collective-permute-done.6.refs_8_ = bf16[2,2,128,128]{3,2,1,0:T(8,128)(2,1)S(1)} collective-permute-done((bf16[2,2,128,128]{3,2,1,0:T(8,128)(2,1)S(1)}, bf16[2,2,128,128]{3,2,1,0:T(8,128)(2,1)S(1)}, u32[]{:S(2)}, u32[]{:S(2)}) %collective-permute-start.6) | collective-permute-done | bytes 131104 | tf_op jit(solution)/shard_map/ppermute | solution.py:239
  20.2 0.9 %collective-permute-start.5 = (bf16[2,2,128,128]{3,2,1,0:T(8,128)(2,1)S(1)}, bf16[2,2,128,128]{3,2,1,0:T(8,128)(2,1)S(1)}, u32[]{:S(2)}, u32[]{:S(2)}) collective-permute-start(bf16[2,2,128,128]{3,2,1,0:T(8,128)(2,1)S(1)} %collective-permute-done.3.refs_5_), channel_id=1, source_target_pairs={{0,4},{2,6},{4,8},{6,10},{8,12},{10,14},{12,16},{14,18},{16,20},{1... | collective-permute-start | bytes 393224 | tf_op jit(solution)/shard_map/ppermute | solution.py:239
  21.1 6.2 %collective-permute-done.4.refs_6_ = bf16[2,2,128,128]{3,2,1,0:T(8,128)(2,1)S(1)} collective-permute-done((bf16[2,2,128,128]{3,2,1,0:T(8,128)(2,1)S(1)}, bf16[2,2,128,128]{3,2,1,0:T(8,128)(2,1)S(1)}, u32[]{:S(2)}, u32[]{:S(2)}) %collective-permute-start.4) | collective-permute-done | bytes 131104 | tf_op jit(solution)/shard_map/ppermute | solution.py:239
  27.2 0.7 %collective-permute-start.11 = (bf16[2,2,2,128,128]{4,3,2,1,0:T(8,128)(2,1)S(1)}, bf16[2,2,2,128,128]{4,3,2,1,0:T(8,128)(2,1)S(1)}, u32[]{:S(2)}, u32[]{:S(2)}) collective-permute-start(bf16[2,2,2,128,128]{4,3,2,1,0:T(8,128)(2,1)S(1)} %pad_maximum_fusion.1), channel_id=1, source_target_pairs={{0,2},{2,0},{4,6},{6,4},{8,10},{10,8},{12,14},{14,12},{16,18},{18,... | collective-permute-start | bytes 786440 | tf_op jit(solution)/shard_map/ppermute | solution.py:239
  28.0 0.0 collective-permute-done.10.refs_12_
  28.0 0.1 collective-permute-start.12
  28.0 0.0 collective-permute-done.7.refs_9_
  28.0 0.4 collective-permute-start.8
  28.5 1.4 %collective-permute-done.5.refs_7_ = bf16[2,2,128,128]{3,2,1,0:T(8,128)(2,1)S(1)} collective-permute-done((bf16[2,2,128,128]{3,2,1,0:T(8,128)(2,1)S(1)}, bf16[2,2,128,128]{3,2,1,0:T(8,128)(2,1)S(1)}, u32[]{:S(2)}, u32[]{:S(2)}) %collective-permute-start.5) | collective-permute-done | bytes 131104 | tf_op jit(solution)/shard_map/ppermute | solution.py:239
  29.9 2.8 %collective-permute-start.9 = (bf16[2,2,128,128]{3,2,1,0:T(8,128)(2,1)S(1)}, bf16[2,2,128,128]{3,2,1,0:T(8,128)(2,1)S(1)}, u32[]{:S(2)}, u32[]{:S(2)}) collective-permute-start(bf16[2,2,128,128]{3,2,1,0:T(8,128)(2,1)S(1)} %collective-permute-done.5.refs_7_), channel_id=1, source_target_pairs={{0,2},{2,0},{4,6},{6,4},{8,10},{10,8},{12,14},{14,12},{16,18},{18,... | collective-permute-start | bytes 393224 | tf_op jit(solution)/shard_map/ppermute | solution.py:239
  32.7 0.0 collective-permute-done.8.refs_10_
  32.7 1.0 %collective-permute-done.9.refs_11_ = bf16[2,2,128,128]{3,2,1,0:T(8,128)(2,1)S(1)} collective-permute-done((bf16[2,2,128,128]{3,2,1,0:T(8,128)(2,1)S(1)}, bf16[2,2,128,128]{3,2,1,0:T(8,128)(2,1)S(1)}, u32[]{:S(2)}, u32[]{:S(2)}) %collective-permute-start.9) | collective-permute-done | bytes 131104 | tf_op jit(solution)/shard_map/ppermute | solution.py:239
  33.7 0.0 collective-permute-done.11.refs_13_
  33.7 0.0 collective-permute-done.refs_1_
  33.7 0.0 copy-start.3
  33.7 0.0 collective-permute-done.12.refs_14_
  33.7 0.0 copy-start.6
  33.7 0.0 copy-done
  33.7 0.0 copy-done.1
  33.7 0.0 copy-done.2
  33.7 0.0 copy-done.7
  33.7 0.0 copy-done.8
  33.8 0.0 copy-done.4
  33.8 0.0 copy-done.9
  33.8 0.0 copy-done.10
  33.8 0.0 copy-done.11
  33.8 0.5 %copy-done.12 = bf16[2,2,128,128]{3,2,1,0:T(8,128)(2,1)} copy-done((bf16[2,2,128,128]{3,2,1,0:T(8,128)(2,1)}, bf16[2,2,128,128]{3,2,1,0:T(8,128)(2,1)S(1)}, u32[]{:S(2)}) %copy-start.12) | copy-done | bytes 131096
  34.3 0.1 copy-done.5
  34.4 0.2 copy-done.3
  34.6 0.1 copy-done.6
  34.7 15.4 %shard_map.60 = (f32[1,256,16,128]{3,2,1,0:T(8,128)}, f32[16,1,256]{2,1,0:T(1,128)}, f32[16,1,256]{2,1,0:T(1,128)}) custom-call(bf16[2,1024,128]{2,1,0:T(8,128)(2,1)} %get-tuple-element.7.refs_0_, bf16[2,1024,128]{2,1,0:T(8,128)(2,1)} %copy-done.3, bf16[2,2,128,128]{3,2,1,0:T(8,128)(2,1)} %get-tuple-element.9.refs_2_, bf16[2,2,128,128]{3,2,1,0:T(8,128)(2,1)} %copy-done, ...), custom_call_target="tpu_custom_call" | custom-call | tf_op jit(solution)/shard_map/pallas_call | solution.py:215
  (11 shorter events, 0.1 us)
Async XLA Ops:
  2.8 6.1 %collective-permute-start.1 = (bf16[2,2,128,128]{3,2,1,0:T(8,128)(2,1)}, bf16[2,2,128,128]{3,2,1,0:T(8,128)(2,1)S(1)}, u32[]{:S(2)}, u32[]{:S(2)}) collective-permute-start(bf16[2,2,128,128]{3,2,1,0:T(8,128)(2,1)} %get-tuple-element.10), channel_id=1, source_target_pairs={{0,1},{1,0},{2,3},{3,2},{4,5},{5,4},{6,7},{7,6},{8,9},{9,8},{10,11... | collective-permute-start | bytes 393224 | tf_op jit(solution)/shard_map/ppermute | solution.py:239
  4.9 5.9 %collective-permute-start.2 = (bf16[2,2,128,128]{3,2,1,0:T(8,128)(2,1)}, bf16[2,2,128,128]{3,2,1,0:T(8,128)(2,1)S(1)}, u32[]{:S(2)}, u32[]{:S(2)}) collective-permute-start(bf16[2,2,128,128]{3,2,1,0:T(8,128)(2,1)} %get-tuple-element.9.refs_2_), channel_id=1, source_target_pairs={{0,8},{2,10},{4,12},{6,14},{8,16},{10,18},{12,20},{14,22},{16,24},... | collective-permute-start | bytes 393224 | tf_op jit(solution)/shard_map/ppermute | solution.py:239
  8.7 25.0 %collective-permute-start = (bf16[2,1024,128]{2,1,0:T(8,128)(2,1)}, bf16[2,1024,128]{2,1,0:T(8,128)(2,1)S(1)}, u32[]{:S(2)}, u32[]{:S(2)}) collective-permute-start(bf16[2,1024,128]{2,1,0:T(8,128)(2,1)} %get-tuple-element.8), channel_id=1, source_target_pairs={{0,1},{1,0},{2,3},{3,2},{4,5},{5,4},{6,7},{7,6},{8,9},{9,8},{10,11... | collective-permute-start | bytes 1572872 | tf_op jit(solution)/shard_map/ppermute | solution.py:239
  8.9 24.8 %copy-start = (bf16[2,2,128,128]{3,2,1,0:T(8,128)(2,1)}, bf16[2,2,128,128]{3,2,1,0:T(8,128)(2,1)S(1)}, u32[]{:S(2)}) copy-start(bf16[2,2,128,128]{3,2,1,0:T(8,128)(2,1)S(1)} %collective-permute-done.1.refs_3_) | copy-start | bytes 393220
  8.9 5.6 %collective-permute-start.3 = (bf16[2,2,128,128]{3,2,1,0:T(8,128)(2,1)S(1)}, bf16[2,2,128,128]{3,2,1,0:T(8,128)(2,1)S(1)}, u32[]{:S(2)}, u32[]{:S(2)}) collective-permute-start(bf16[2,2,128,128]{3,2,1,0:T(8,128)(2,1)S(1)} %collective-permute-done.1.refs_3_), channel_id=1, source_target_pairs={{0,8},{2,10},{4,12},{6,14},{8,16},{10,18},{12,20},{14,22},{16,24},... | collective-permute-start | bytes 393224 | tf_op jit(solution)/shard_map/ppermute | solution.py:239
  10.8 22.9 %copy-start.1 = (bf16[2,2,128,128]{3,2,1,0:T(8,128)(2,1)}, bf16[2,2,128,128]{3,2,1,0:T(8,128)(2,1)S(1)}, u32[]{:S(2)}) copy-start(bf16[2,2,128,128]{3,2,1,0:T(8,128)(2,1)S(1)} %collective-permute-done.2.refs_4_) | copy-start | bytes 393220
  14.5 19.2 %copy-start.2 = (bf16[2,2,128,128]{3,2,1,0:T(8,128)(2,1)}, bf16[2,2,128,128]{3,2,1,0:T(8,128)(2,1)S(1)}, u32[]{:S(2)}) copy-start(bf16[2,2,128,128]{3,2,1,0:T(8,128)(2,1)S(1)} %collective-permute-done.3.refs_5_) | copy-start | bytes 393220
  14.6 13.4 %collective-permute-start.10 = (bf16[2,2,2,128,128]{4,3,2,1,0:T(8,128)(2,1)S(1)}, bf16[2,2,2,128,128]{4,3,2,1,0:T(8,128)(2,1)S(1)}, u32[]{:S(2)}, u32[]{:S(2)}) collective-permute-start(bf16[2,2,2,128,128]{4,3,2,1,0:T(8,128)(2,1)S(1)} %pad_maximum_fusion), channel_id=1, source_target_pairs={{0,4},{2,6},{4,0},{6,2},{8,12},{10,14},{12,8},{14,10},{16,20},{18,... | collective-permute-start | bytes 786440 | tf_op jit(solution)/shard_map/ppermute | solution.py:239
  15.9 4.3 %collective-permute-start.6 = (bf16[2,2,128,128]{3,2,1,0:T(8,128)(2,1)S(1)}, bf16[2,2,128,128]{3,2,1,0:T(8,128)(2,1)S(1)}, u32[]{:S(2)}, u32[]{:S(2)}) collective-permute-start(bf16[2,2,128,128]{3,2,1,0:T(8,128)(2,1)S(1)} %collective-permute-done.2.refs_4_), channel_id=1, source_target_pairs={{0,2},{2,8},{4,6},{6,12},{8,10},{10,16},{12,14},{14,20},{16,18},{1... | collective-permute-start | bytes 393224 | tf_op jit(solution)/shard_map/ppermute | solution.py:239
  18.2 9.0 %collective-permute-start.4 = (bf16[2,2,128,128]{3,2,1,0:T(8,128)(2,1)S(1)}, bf16[2,2,128,128]{3,2,1,0:T(8,128)(2,1)S(1)}, u32[]{:S(2)}, u32[]{:S(2)}) collective-permute-start(bf16[2,2,128,128]{3,2,1,0:T(8,128)(2,1)S(1)} %collective-permute-done.2.refs_4_), channel_id=1, source_target_pairs={{0,4},{2,6},{4,8},{6,10},{8,12},{10,14},{12,16},{14,18},{16,20},{1... | collective-permute-start | bytes 393224 | tf_op jit(solution)/shard_map/ppermute | solution.py:239
  18.5 9.5 %collective-permute-start.7 = (bf16[2,2,128,128]{3,2,1,0:T(8,128)(2,1)S(1)}, bf16[2,2,128,128]{3,2,1,0:T(8,128)(2,1)S(1)}, u32[]{:S(2)}, u32[]{:S(2)}) collective-permute-start(bf16[2,2,128,128]{3,2,1,0:T(8,128)(2,1)S(1)} %collective-permute-done.3.refs_5_), channel_id=1, source_target_pairs={{0,2},{2,8},{4,6},{6,12},{8,10},{10,16},{12,14},{14,20},{16,18},{1... | collective-permute-start | bytes 393224 | tf_op jit(solution)/shard_map/ppermute | solution.py:239
  20.1 13.6 %copy-start.7 = (bf16[2,2,128,128]{3,2,1,0:T(8,128)(2,1)}, bf16[2,2,128,128]{3,2,1,0:T(8,128)(2,1)S(1)}, u32[]{:S(2)}) copy-start(bf16[2,2,128,128]{3,2,1,0:T(8,128)(2,1)S(1)} %collective-permute-done.6.refs_8_) | copy-start | bytes 393220
  20.2 9.8 %collective-permute-start.5 = (bf16[2,2,128,128]{3,2,1,0:T(8,128)(2,1)S(1)}, bf16[2,2,128,128]{3,2,1,0:T(8,128)(2,1)S(1)}, u32[]{:S(2)}, u32[]{:S(2)}) collective-permute-start(bf16[2,2,128,128]{3,2,1,0:T(8,128)(2,1)S(1)} %collective-permute-done.3.refs_5_), channel_id=1, source_target_pairs={{0,4},{2,6},{4,8},{6,10},{8,12},{10,14},{12,16},{14,18},{16,20},{1... | collective-permute-start | bytes 393224 | tf_op jit(solution)/shard_map/ppermute | solution.py:239
  27.2 6.5 %copy-start.8 = (bf16[2,2,128,128]{3,2,1,0:T(8,128)(2,1)}, bf16[2,2,128,128]{3,2,1,0:T(8,128)(2,1)S(1)}, u32[]{:S(2)}) copy-start(bf16[2,2,128,128]{3,2,1,0:T(8,128)(2,1)S(1)} %collective-permute-done.4.refs_6_) | copy-start | bytes 393220
  27.2 6.4 %collective-permute-start.11 = (bf16[2,2,2,128,128]{4,3,2,1,0:T(8,128)(2,1)S(1)}, bf16[2,2,2,128,128]{4,3,2,1,0:T(8,128)(2,1)S(1)}, u32[]{:S(2)}, u32[]{:S(2)}) collective-permute-start(bf16[2,2,2,128,128]{4,3,2,1,0:T(8,128)(2,1)S(1)} %pad_maximum_fusion.1), channel_id=1, source_target_pairs={{0,2},{2,0},{4,6},{6,4},{8,10},{10,8},{12,14},{14,12},{16,18},{18,... | collective-permute-start | bytes 786440 | tf_op jit(solution)/shard_map/ppermute | solution.py:239
  28.0 5.8 %copy-start.4 = (bf16[2,2,2,128,128]{4,3,2,1,0:T(8,128)(2,1)}, bf16[2,2,2,128,128]{4,3,2,1,0:T(8,128)(2,1)S(1)}, u32[]{:S(2)}) copy-start(bf16[2,2,2,128,128]{4,3,2,1,0:T(8,128)(2,1)S(1)} %collective-permute-done.10.refs_12_) | copy-start | bytes 786436
  28.0 5.7 %collective-permute-start.12 = (bf16[2,2,2,128,128]{4,3,2,1,0:T(8,128)(2,1)S(1)}, bf16[2,2,2,128,128]{4,3,2,1,0:T(8,128)(2,1)S(1)}, u32[]{:S(2)}, u32[]{:S(2)}) collective-permute-start(bf16[2,2,2,128,128]{4,3,2,1,0:T(8,128)(2,1)S(1)} %collective-permute-done.10.refs_12_), channel_id=1, source_target_pairs={{0,2},{2,0},{4,6},{6,4},{8,10},{10,8},{12,14},{14,12},{16,18},{18,... | collective-permute-start | bytes 786440 | tf_op jit(solution)/shard_map/ppermute | solution.py:239
  28.0 5.7 %copy-start.9 = (bf16[2,2,128,128]{3,2,1,0:T(8,128)(2,1)}, bf16[2,2,128,128]{3,2,1,0:T(8,128)(2,1)S(1)}, u32[]{:S(2)}) copy-start(bf16[2,2,128,128]{3,2,1,0:T(8,128)(2,1)S(1)} %collective-permute-done.7.refs_9_) | copy-start | bytes 393220
  28.0 4.6 %collective-permute-start.8 = (bf16[2,2,128,128]{3,2,1,0:T(8,128)(2,1)S(1)}, bf16[2,2,128,128]{3,2,1,0:T(8,128)(2,1)S(1)}, u32[]{:S(2)}, u32[]{:S(2)}) collective-permute-start(bf16[2,2,128,128]{3,2,1,0:T(8,128)(2,1)S(1)} %collective-permute-done.4.refs_6_), channel_id=1, source_target_pairs={{0,2},{2,0},{4,6},{6,4},{8,10},{10,8},{12,14},{14,12},{16,18},{18,... | collective-permute-start | bytes 393224 | tf_op jit(solution)/shard_map/ppermute | solution.py:239
  29.9 3.9 %copy-start.10 = (bf16[2,2,128,128]{3,2,1,0:T(8,128)(2,1)}, bf16[2,2,128,128]{3,2,1,0:T(8,128)(2,1)S(1)}, u32[]{:S(2)}) copy-start(bf16[2,2,128,128]{3,2,1,0:T(8,128)(2,1)S(1)} %collective-permute-done.5.refs_7_) | copy-start | bytes 393220
  29.9 3.8 %collective-permute-start.9 = (bf16[2,2,128,128]{3,2,1,0:T(8,128)(2,1)S(1)}, bf16[2,2,128,128]{3,2,1,0:T(8,128)(2,1)S(1)}, u32[]{:S(2)}, u32[]{:S(2)}) collective-permute-start(bf16[2,2,128,128]{3,2,1,0:T(8,128)(2,1)S(1)} %collective-permute-done.5.refs_7_), channel_id=1, source_target_pairs={{0,2},{2,0},{4,6},{6,4},{8,10},{10,8},{12,14},{14,12},{16,18},{18,... | collective-permute-start | bytes 393224 | tf_op jit(solution)/shard_map/ppermute | solution.py:239
  32.7 1.1 %copy-start.11 = (bf16[2,2,128,128]{3,2,1,0:T(8,128)(2,1)}, bf16[2,2,128,128]{3,2,1,0:T(8,128)(2,1)S(1)}, u32[]{:S(2)}) copy-start(bf16[2,2,128,128]{3,2,1,0:T(8,128)(2,1)S(1)} %collective-permute-done.8.refs_10_) | copy-start | bytes 393220
  33.7 0.6 %copy-start.12 = (bf16[2,2,128,128]{3,2,1,0:T(8,128)(2,1)}, bf16[2,2,128,128]{3,2,1,0:T(8,128)(2,1)S(1)}, u32[]{:S(2)}) copy-start(bf16[2,2,128,128]{3,2,1,0:T(8,128)(2,1)S(1)} %collective-permute-done.9.refs_11_) | copy-start | bytes 393220
  33.7 0.7 %copy-start.5 = (bf16[2,2,2,128,128]{4,3,2,1,0:T(8,128)(2,1)}, bf16[2,2,2,128,128]{4,3,2,1,0:T(8,128)(2,1)S(1)}, u32[]{:S(2)}) copy-start(bf16[2,2,2,128,128]{4,3,2,1,0:T(8,128)(2,1)S(1)} %collective-permute-done.11.refs_13_) | copy-start | bytes 786436
  33.7 1.0 %copy-start.3 = (bf16[2,1024,128]{2,1,0:T(8,128)(2,1)}, bf16[2,1024,128]{2,1,0:T(8,128)(2,1)S(1)}, u32[]{:S(2)}) copy-start(bf16[2,1024,128]{2,1,0:T(8,128)(2,1)S(1)} %collective-permute-done.refs_1_) | copy-start | bytes 1572868
  33.7 1.0 %copy-start.6 = (bf16[2,2,2,128,128]{4,3,2,1,0:T(8,128)(2,1)}, bf16[2,2,2,128,128]{4,3,2,1,0:T(8,128)(2,1)S(1)}, u32[]{:S(2)}) copy-start(bf16[2,2,2,128,128]{4,3,2,1,0:T(8,128)(2,1)S(1)} %collective-permute-done.12.refs_14_) | copy-start | bytes 786436

commit v3 on v2

v3 whole, which is shorter than its diff:
```python
import functools
import math

import jax
import jax.numpy as jnp
from jax import lax
from jax.experimental import pallas as pl
from jax.experimental.pallas import tpu as pltpu
from jax.sharding import PartitionSpec as P

QUERY_HEADS = 32
KEY_VALUE_HEADS = 4
WIN = 8
LAYER = 4
GROUP = QUERY_HEADS // KEY_VALUE_HEADS
BF16 = jnp.bfloat16
F32 = jnp.float32
VMEM_LIMIT = 56 * 2**20
NEG = -1e30
SPAN = 512
BLOCK = 128
AHEAD = 0


def slot_of(head, per, count):
    return lax.rem(head // per - lax.axis_index("head") + count, count)


def pack_kv_kernel(k_ref, v_ref, *outs):
    count = len(outs)
    per = k_ref.shape[2] // count
    k = k_ref[0].astype(F32)
    v = v_ref[0].astype(F32)
    for head in range(k_ref.shape[2]):
        kh = k[:, head, :].astype(BF16)
        vh = v[:, head, :].astype(BF16)
        for d in range(count):

            @pl.when(slot_of(head, per, count) == d)
            def _():
                outs[d][0, head % per] = kh
                outs[d][1, head % per] = vh


def pack_q_kernel(q_ref, *outs):
    count = len(outs)
    rows, heads, width = q_ref.shape[1:]
    per = heads // GROUP // count
    for head in range(heads // GROUP):
        qh = q_ref[0, :, head * GROUP : (head + 1) * GROUP, :].astype(F32)
        qh = qh.reshape(rows * GROUP, width).astype(BF16)
        for d in range(count):

            @pl.when(slot_of(head, per, count) == d)
            def _():
                outs[d][head % per] = qh


def pack(kernel, shape, count, *arrays):
    return pl.pallas_call(
        kernel,
        out_shape=(jax.ShapeDtypeStruct(shape, BF16),) * count,
        in_specs=[pl.BlockSpec(memory_space=pltpu.VMEM)] * len(arrays),
        out_specs=[pl.BlockSpec(memory_space=pltpu.VMEM)] * count,
        compiler_params=pltpu.CompilerParams(vmem_limit_bytes=VMEM_LIMIT),
    )(*arrays)


def attend_kernel(n, count, singles, offsets, step_chunks, block, *refs):
    total = len(offsets) * count
    merged = len(offsets) - singles // count
    q_hbm, refs = refs[:count], refs[count:]
    kv_hbm, refs = refs[: singles + merged], refs[singles + merged :]
    out_hbm, max_ref, sum_ref, qbuf, kvbuf, acc, mbuf, lbuf, order, qsem, ksem, osem = refs
    per, m_rows, width = q_hbm[0].shape
    rows = m_rows // GROUP
    half = count * rows // 2
    span = step_chunks * rows
    p = lax.axis_index("ctx")
    h = lax.axis_index("head")
    factor = math.log2(math.e) / math.sqrt(width)

    loads = [pltpu.make_async_copy(q_hbm[s], qbuf.at[s], qsem.at[s]) for s in range(count)]
    for i, ref in enumerate(kv_hbm):
        if i < singles:
            to = kvbuf.at[i]
        else:
            to = kvbuf.at[pl.ds(singles + (i - singles) * count, count)]
        loads.append(pltpu.make_async_copy(ref, to, ksem.at[i]))
    for load in loads:
        load.start()

    def start_of(pair, chunk):
        r = chunk * rows
        return jnp.where(r < half, 2 * pair * half + r, (2 * n - 2 - 2 * pair) * half + r)

    chunk_of = [lax.rem(h - d + count, count) for d in range(count)]
    starts = []
    for offset in offsets:
        pair = lax.rem(p - offset(p) + n, n)
        starts += [start_of(pair, chunk) for chunk in chunk_of]
    firsts, steps = [], []
    for s in range(count):
        for t in range(step_chunks):
            order[s, t] = s
        seen = jnp.int32(1)
        for c in range(total):
            if c != s:
                visible = (starts[c] < starts[s]).astype(jnp.int32)
                order[s, seen] = lax.select(visible == 1, c, s)
                seen = seen + visible
        first = lax.rem(seen - 1, step_chunks) + 1
        firsts.append(first)
        steps.append((seen - first) // step_chunks)

    def keys_at(s, g, begin):
        at = [order[s, begin + t] for t in range(step_chunks)]
        return jnp.concatenate([kvbuf[i, 0, g] for i in at], axis=0)

    def values_at(s, g, begin):
        at = [order[s, begin + t] for t in range(step_chunks)]
        v = jnp.concatenate([kvbuf[i, 1, g] for i in at], axis=0)
        return jnp.concatenate([v, jnp.ones((span, 128), BF16)], axis=1)

    def score_of(s, g, b, k):
        q = qbuf[s, g, b * block : (b + 1) * block, :]
        return lax.dot_general(q, k, (((1,), (1,)), ((), ())), preferred_element_type=F32)

    def acc_at(s, g, b):
        row = b * (block // GROUP)
        return s, slice(row, row + block // GROUP), slice(g * GROUP, (g + 1) * GROUP)

    def tiles(x):
        return [x[:, t : t + 128] for t in range(0, span, 128)]

    def first_block(s, g, b, score, v):
        at = slice(b * block, (b + 1) * block)
        shape = (block // GROUP, GROUP, 128)
        row = lax.broadcasted_iota(jnp.int32, shape, 0) + b * (block // GROUP)
        col = lax.broadcasted_iota(jnp.int32, shape, 2)
        parts = []
        for t, x in enumerate(tiles(score)):
            x = x.reshape(shape)
            if t * 128 >= rows and rows % 128 == 0:
                x = jnp.where(t * 128 < firsts[s] * rows, x, NEG)
            else:
                seen = col + t * 128 < firsts[s] * rows
                if t * 128 < rows:
                    seen &= (col + t * 128 <= row) | (col + t * 128 >= rows)
                x = jnp.where(seen, x, NEG)
            parts.append(x.reshape(block, 128))
        top = jnp.max(functools.reduce(jnp.maximum, parts), axis=1, keepdims=True)
        prob = jnp.concatenate(
            [jnp.exp2((x - top) * factor).astype(BF16) for x in parts], axis=1
        )
        got = jnp.dot(prob, v, preferred_element_type=F32)
        mbuf[s, g, at, :] = jnp.broadcast_to(top, (block, 128))
        lbuf[s, g, at, :] = got[:, width:]
        acc[acc_at(s, g, b)] = got[:, :width].reshape(block // GROUP, GROUP, width)

    def next_block(s, g, b, score, v):
        at = slice(b * block, (b + 1) * block)
        parts = tiles(score)
        old = mbuf[s, g, at, :]
        top = jnp.maximum(
            old, jnp.max(functools.reduce(jnp.maximum, parts), axis=1, keepdims=True)
        )
        shrink = jnp.exp2((old - top) * factor)
        prob = jnp.concatenate(
            [jnp.exp2((x - top) * factor).astype(BF16) for x in parts], axis=1
        )
        got = jnp.dot(prob, v, preferred_element_type=F32)
        mbuf[s, g, at, :] = top
        lbuf[s, g, at, :] = lbuf[s, g, at, :] * shrink + got[:, width:]
        held = acc[acc_at(s, g, b)].reshape(block, width)
        acc[acc_at(s, g, b)] = (held * shrink + got[:, :width]).reshape(
            block // GROUP, GROUP, width
        )

    def run(work, begin, finish):
        scores, keys, vals = {}, {}, {}
        for i in range(len(work) + AHEAD):
            if i < len(work):
                s, g, b = work[i]
                if (s, g) not in keys:
                    keys[s, g] = keys_at(s, g, begin)
                scores[i] = score_of(s, g, b, keys[s, g])
            if i >= AHEAD:
                s, g, b = work[i - AHEAD]
                if (s, g) not in vals:
                    vals[s, g] = values_at(s, g, begin)
                finish(s, g, b, scores.pop(i - AHEAD), vals[s, g])

    def to_lanes(x):
        x = x.reshape(rows, GROUP, 128)[:, :, :rows]
        a = lax.broadcasted_iota(jnp.int32, (rows, GROUP, rows), 0)
        b = lax.broadcasted_iota(jnp.int32, (rows, GROUP, rows), 2)
        return jnp.sum(jnp.where(a == b, x, 0.0), axis=0)

    for load in loads:
        load.wait()
    blocks = [(g, b) for g in range(per) for b in range(m_rows // block)]
    run([(s, g, b) for s in range(count) for g, b in blocks], 0, first_block)
    saves = []
    for s in range(count):

        def step(t, _):
            run([(s, g, b) for g, b in blocks], firsts[s] + t * step_chunks, next_block)
            return 0

        lax.fori_loop(0, steps[s], step, 0)
        row0 = pl.multiple_of(chunk_of[s] * rows, rows)
        saves.append(
            pltpu.make_async_copy(acc.at[s], out_hbm.at[0, pl.ds(row0, rows)], osem.at[s])
        )
        saves[-1].start()
        for g in range(per):
            tops = to_lanes(mbuf[s, g]) * (1.0 / math.sqrt(width))
            sums = to_lanes(lbuf[s, g])
            for d in range(count):

                @pl.when(chunk_of[s] == d)
                def _():
                    max_ref[g * GROUP : (g + 1) * GROUP, 0, d * rows : (d + 1) * rows] = tops
                    sum_ref[g * GROUP : (g + 1) * GROUP, 0, d * rows : (d + 1) * rows] = sums
    for save in saves:
        save.wait()


def attend(q_list, kv_list, merged, offsets, n):
    count = len(q_list)
    per, m_rows, width = q_list[0].shape
    rows = m_rows // GROUP
    total = len(offsets) * count
    step_chunks = SPAN // rows
    loads = len(kv_list) + len(merged)
    return pl.pallas_call(
        functools.partial(
            attend_kernel, n, count, len(kv_list), offsets, step_chunks, min(BLOCK, m_rows)
        ),
        out_shape=(
            jax.ShapeDtypeStruct((1, count * rows, per * GROUP, width), F32),
            jax.ShapeDtypeStruct((per * GROUP, 1, count * rows), F32),
            jax.ShapeDtypeStruct((per * GROUP, 1, count * rows), F32),
        ),
        in_specs=[pl.BlockSpec(memory_space=pl.ANY)] * (count + loads),
        out_specs=[pl.BlockSpec(memory_space=pl.ANY)]
        + [pl.BlockSpec(memory_space=pltpu.VMEM)] * 2,
        scratch_shapes=[
            pltpu.VMEM((count, per, m_rows, width), BF16),
            pltpu.VMEM((total, 2, per, rows, width), BF16),
            pltpu.VMEM((count, rows, per * GROUP, width), F32),
            pltpu.VMEM((count, per, m_rows, 128), F32),
            pltpu.VMEM((count, per, m_rows, 128), F32),
            pltpu.SMEM((count, total + 1 + step_chunks), jnp.int32),
            pltpu.SemaphoreType.DMA((count,)),
            pltpu.SemaphoreType.DMA((loads,)),
            pltpu.SemaphoreType.DMA((count,)),
        ],
        compiler_params=pltpu.CompilerParams(vmem_limit_bytes=VMEM_LIMIT),
    )(*q_list, *kv_list, *merged)


def along(block, axis, target):
    size = lax.axis_size(axis)
    return lax.ppermute(block, axis, [(i, target(i) % size) for i in range(size)])


def local(queries, keys, values):
    n = lax.axis_size("ctx")
    count = lax.axis_size("head")
    rows, kv_heads, width = keys.shape[1:]
    per = kv_heads // count
    me = lax.axis_index("ctx")
    swap = lambda x, d: along(x, "head", lambda i: i + d)
    ctx = lambda xs, target: [along(x, "ctx", target) for x in xs]

    kv = pack(pack_kv_kernel, (2, per, rows, width), count, keys, values)
    own = [kv[0]] + [swap(kv[d], d) for d in range(1, count)]
    q = pack(pack_q_kernel, (per, rows * GROUP, width), count, queries)
    q = [q[0]] + [swap(q[d], d) for d in range(1, count)]

    layer = LAYER
    up = ctx(own, lambda i: i + layer)
    far = ctx(up, lambda i: i + layer // 2)
    odd = ctx(up, lambda i: i + layer - 1 if i & 1 else i + 1)
    column = lax.rem(me // 2, 2) == 0
    side = jnp.concatenate([jnp.where(column, a, b)[None] for a, b in zip(own, up)])
    side = along(side, "ctx", lambda i: i ^ 2)
    core = lax.rem(me, 2) == 0
    next_to = jnp.concatenate([jnp.where(core, a, b)[None] for a, b in zip(own, up)])
    next_to = along(next_to, "ctx", lambda i: i ^ 1)
    far_c = ctx(far, lambda i: i ^ 1)
    side_c = along(side, "ctx", lambda i: i ^ 1)

    bit = lambda p, even, other: jnp.where(lax.rem(p, 2) == 0, even, other)
    offsets = [
        lambda p: 0,
        lambda p: layer,
        lambda p: layer + 2,
        lambda p: bit(p, layer + 3, layer + 1),
        lambda p: bit(p, layer + 1, layer + 3),
        lambda p: 2,
        lambda p: bit(p, 3, 1),
        lambda p: bit(p, 1, 3),
    ]
    blocks = own + up + far + odd + far_c
    return attend(q, blocks, [side, next_to, side_c], offsets, n)


def solution(mesh):
    in_specs = (
        P("ctx", "head", None, None),
        P("ctx", "head", None, None),
        P("ctx", "head", None, None),
    )
    out_specs = (P("ctx", None, "head", None), P("head", "ctx", None), P("head", "ctx", None))
    return jax.shard_map(local, mesh=mesh, in_specs=in_specs, out_specs=out_specs, check_vma=False)
```

time: 50.7 us -> 46.5 us (0.917)
  Pallas kernels: 20.1 us -> 15.9 us
    pallas_call x1, Pallas kernels: 15.4 us -> 11.2 us  [attend(): pl.pallas_call(functools.partial(attend_kernel, n, count, len(kv_list), o...]
where the time goes in v3:
time: 46.5 us; the launch traced here: 45.9 us
  Pallas kernels  15.9 us (34%)
  starting transfers between devices  14 us (30%)
  waiting for transfers between devices  13.3 us (29%)
  other arithmetic  1.05 us (2%)
  local copies, waits for them, and re-layouts  0.94 us (2%)
  between operations  0.77 us (2%)
    ppermute x13, starting transfers between devices, along(): lax.ppermute(block, axis, [(i, target(i) % size) for i in range(size)])  14 us
    ppermute x13, waiting for transfers between devices, along(): lax.ppermute(block, axis, [(i, target(i) % size) for i in range(size)])  13.3 us
    pallas_call x1, Pallas kernels, attend(): pl.pallas_call(functools.partial(attend_kernel, n, count, len(kv_list), o...  11.2 us
    pallas_call x2, Pallas kernels, pack(): pl.pallas_call(kernel, out_shape=(jax.ShapeDtypeStruct(shape, BF16),) * c...  4.69 us
    broadcast_in_dim x2, other arithmetic, local(): jnp.where(core, a, b)[None]  0.99 us
    unnamed x26, local copies, waits for them, and re-layouts  0.94 us
  transfers between devices with their start and end apart: 13, of which 6 were waited for; matrix products, arithmetic and copies ran while one was open for 2% of the time, Pallas kernels for 5%

profile of v3, /device:TPU:1, one launch (start us, length us, event | category | flops | bytes accessed | tf_op | source)
XLA Modules:
  0.0 45.9 jit_solution(10223817401571795229)
XLA Ops:
  0.6 2.2 %shard_map.59 = (bf16[2,2,128,128]{3,2,1,0:T(8,128)(2,1)}, bf16[2,2,128,128]{3,2,1,0:T(8,128)(2,1)}) custom-call(bf16[1,128,4,128]{3,2,1,0:T(4,128)(2,1)} %k_ref.1, bf16[1,128,4,128]{3,2,1,0:T(4,128)(2,1)} %v_ref.1), custom_call_target="tpu_custom_call" | custom-call | tf_op jit(solution)/shard_map/pallas_call | solution.py:60
  2.8 2.1 %collective-permute-start.1 = (bf16[2,2,128,128]{3,2,1,0:T(8,128)(2,1)}, bf16[2,2,128,128]{3,2,1,0:T(8,128)(2,1)S(1)}, u32[]{:S(2)}, u32[]{:S(2)}) collective-permute-start(bf16[2,2,128,128]{3,2,1,0:T(8,128)(2,1)} %get-tuple-element.10), channel_id=1, source_target_pairs={{0,1},{1,0},{2,3},{3,2},{4,5},{5,4},{6,7},{7,6},{8,9},{9,8},{10,11... | collective-permute-start | bytes 393224 | tf_op jit(solution)/shard_map/ppermute | solution.py:266
  4.9 1.3 %collective-permute-start.2 = (bf16[2,2,128,128]{3,2,1,0:T(8,128)(2,1)}, bf16[2,2,128,128]{3,2,1,0:T(8,128)(2,1)S(1)}, u32[]{:S(2)}, u32[]{:S(2)}) collective-permute-start(bf16[2,2,128,128]{3,2,1,0:T(8,128)(2,1)} %get-tuple-element.9.refs_2_), channel_id=1, source_target_pairs={{0,8},{2,10},{4,12},{6,14},{8,16},{10,18},{12,20},{14,22},{16,24},... | collective-permute-start | bytes 393224 | tf_op jit(solution)/shard_map/ppermute | solution.py:266
  6.2 2.5 %shard_map.58 = (bf16[2,1024,128]{2,1,0:T(8,128)(2,1)}, bf16[2,1024,128]{2,1,0:T(8,128)(2,1)}) custom-call(bf16[1,128,32,128]{3,2,1,0:T(8,128)(2,1)} %q_ref.1), custom_call_target="tpu_custom_call" | custom-call | tf_op jit(solution)/shard_map/pallas_call | solution.py:60
  8.7 0.2 collective-permute-start
  8.9 0.0 collective-permute-done.1.refs_3_
  8.9 0.0 copy-start
  8.9 1.3 %collective-permute-start.3 = (bf16[2,2,128,128]{3,2,1,0:T(8,128)(2,1)S(1)}, bf16[2,2,128,128]{3,2,1,0:T(8,128)(2,1)S(1)}, u32[]{:S(2)}, u32[]{:S(2)}) collective-permute-start(bf16[2,2,128,128]{3,2,1,0:T(8,128)(2,1)S(1)} %collective-permute-done.1.refs_3_), channel_id=1, source_target_pairs={{0,8},{2,10},{4,12},{6,14},{8,16},{10,18},{12,20},{14,22},{16,24},... | collective-permute-start | bytes 393224 | tf_op jit(solution)/shard_map/ppermute | solution.py:266
  10.2 0.6 %collective-permute-done.2.refs_4_ = bf16[2,2,128,128]{3,2,1,0:T(8,128)(2,1)S(1)} collective-permute-done((bf16[2,2,128,128]{3,2,1,0:T(8,128)(2,1)}, bf16[2,2,128,128]{3,2,1,0:T(8,128)(2,1)S(1)}, u32[]{:S(2)}, u32[]{:S(2)}) %collective-permute-start.2) | collective-permute-done | bytes 131104 | tf_op jit(solution)/shard_map/ppermute | solution.py:266
  10.8 0.0 copy-start.1
  10.8 1.0 %select_bitcast_fusion.1 = (bf16[1,2,2,128,128]{4,3,2,1,0:T(8,128)(2,1)S(1)}, bf16[1,2,2,128,128]{4,3,2,1,0:T(8,128)(2,1)S(1)}) fusion(bf16[2,2,128,128]{3,2,1,0:T(8,128)(2,1)} %get-tuple-element.9.refs_2_, bf16[2,2,128,128]{3,2,1,0:T(8,128)(2,1)S(1)} %collective-permute-done.2.refs_4_, pred[]{:T(512)S(6)} %eq.7, pred[]{:T(512)S(6)} %eq.6), kind=kLoop, calls=%fused_computation.3 | loop fusion | flops 131072 | bytes 524290 | tf_op jit(solution)/shard_map/broadcast_in_dim | solution.py:291
  11.8 2.8 %collective-permute-done.3.refs_5_ = bf16[2,2,128,128]{3,2,1,0:T(8,128)(2,1)S(1)} collective-permute-done((bf16[2,2,128,128]{3,2,1,0:T(8,128)(2,1)S(1)}, bf16[2,2,128,128]{3,2,1,0:T(8,128)(2,1)S(1)}, u32[]{:S(2)}, u32[]{:S(2)}) %collective-permute-start.3) | collective-permute-done | bytes 131104 | tf_op jit(solution)/shard_map/ppermute | solution.py:266
  14.5 0.0 copy-start.2
  14.6 1.3 %collective-permute-start.10 = (bf16[2,2,2,128,128]{4,3,2,1,0:T(8,128)(2,1)S(1)}, bf16[2,2,2,128,128]{4,3,2,1,0:T(8,128)(2,1)S(1)}, u32[]{:S(2)}, u32[]{:S(2)}) collective-permute-start(bf16[2,2,2,128,128]{4,3,2,1,0:T(8,128)(2,1)S(1)} %pad_maximum_fusion), channel_id=1, source_target_pairs={{0,4},{2,6},{4,0},{6,2},{8,12},{10,14},{12,8},{14,10},{16,20},{18,... | collective-permute-start | bytes 786440 | tf_op jit(solution)/shard_map/ppermute | solution.py:266
  15.9 2.3 %collective-permute-start.6 = (bf16[2,2,128,128]{3,2,1,0:T(8,128)(2,1)S(1)}, bf16[2,2,128,128]{3,2,1,0:T(8,128)(2,1)S(1)}, u32[]{:S(2)}, u32[]{:S(2)}) collective-permute-start(bf16[2,2,128,128]{3,2,1,0:T(8,128)(2,1)S(1)} %collective-permute-done.2.refs_4_), channel_id=1, source_target_pairs={{0,2},{2,8},{4,6},{6,12},{8,10},{10,16},{12,14},{14,20},{16,18},{1... | collective-permute-start | bytes 393224 | tf_op jit(solution)/shard_map/ppermute | solution.py:266
  18.2 0.3 collective-permute-start.4
  18.5 0.3 collective-permute-start.7
  18.8 1.3 %collective-permute-done.6.refs_8_ = bf16[2,2,128,128]{3,2,1,0:T(8,128)(2,1)S(1)} collective-permute-done((bf16[2,2,128,128]{3,2,1,0:T(8,128)(2,1)S(1)}, bf16[2,2,128,128]{3,2,1,0:T(8,128)(2,1)S(1)}, u32[]{:S(2)}, u32[]{:S(2)}) %collective-permute-start.6) | collective-permute-done | bytes 131104 | tf_op jit(solution)/shard_map/ppermute | solution.py:266
  20.2 0.9 %collective-permute-start.5 = (bf16[2,2,128,128]{3,2,1,0:T(8,128)(2,1)S(1)}, bf16[2,2,128,128]{3,2,1,0:T(8,128)(2,1)S(1)}, u32[]{:S(2)}, u32[]{:S(2)}) collective-permute-start(bf16[2,2,128,128]{3,2,1,0:T(8,128)(2,1)S(1)} %collective-permute-done.3.refs_5_), channel_id=1, source_target_pairs={{0,4},{2,6},{4,8},{6,10},{8,12},{10,14},{12,16},{14,18},{16,20},{1... | collective-permute-start | bytes 393224 | tf_op jit(solution)/shard_map/ppermute | solution.py:266
  21.1 6.2 %collective-permute-done.4.refs_6_ = bf16[2,2,128,128]{3,2,1,0:T(8,128)(2,1)S(1)} collective-permute-done((bf16[2,2,128,128]{3,2,1,0:T(8,128)(2,1)S(1)}, bf16[2,2,128,128]{3,2,1,0:T(8,128)(2,1)S(1)}, u32[]{:S(2)}, u32[]{:S(2)}) %collective-permute-start.4) | collective-permute-done | bytes 131104 | tf_op jit(solution)/shard_map/ppermute | solution.py:266
  27.2 0.7 %collective-permute-start.11 = (bf16[2,2,2,128,128]{4,3,2,1,0:T(8,128)(2,1)S(1)}, bf16[2,2,2,128,128]{4,3,2,1,0:T(8,128)(2,1)S(1)}, u32[]{:S(2)}, u32[]{:S(2)}) collective-permute-start(bf16[2,2,2,128,128]{4,3,2,1,0:T(8,128)(2,1)S(1)} %pad_maximum_fusion.1), channel_id=1, source_target_pairs={{0,2},{2,0},{4,6},{6,4},{8,10},{10,8},{12,14},{14,12},{16,18},{18,... | collective-permute-start | bytes 786440 | tf_op jit(solution)/shard_map/ppermute | solution.py:266
  28.0 0.0 collective-permute-done.10.refs_12_
  28.0 0.1 collective-permute-start.12
  28.0 0.0 collective-permute-done.7.refs_9_
  28.0 0.4 collective-permute-start.8
  28.5 1.4 %collective-permute-done.5.refs_7_ = bf16[2,2,128,128]{3,2,1,0:T(8,128)(2,1)S(1)} collective-permute-done((bf16[2,2,128,128]{3,2,1,0:T(8,128)(2,1)S(1)}, bf16[2,2,128,128]{3,2,1,0:T(8,128)(2,1)S(1)}, u32[]{:S(2)}, u32[]{:S(2)}) %collective-permute-start.5) | collective-permute-done | bytes 131104 | tf_op jit(solution)/shard_map/ppermute | solution.py:266
  29.9 2.8 %collective-permute-start.9 = (bf16[2,2,128,128]{3,2,1,0:T(8,128)(2,1)S(1)}, bf16[2,2,128,128]{3,2,1,0:T(8,128)(2,1)S(1)}, u32[]{:S(2)}, u32[]{:S(2)}) collective-permute-start(bf16[2,2,128,128]{3,2,1,0:T(8,128)(2,1)S(1)} %collective-permute-done.5.refs_7_), channel_id=1, source_target_pairs={{0,2},{2,0},{4,6},{6,4},{8,10},{10,8},{12,14},{14,12},{16,18},{18,... | collective-permute-start | bytes 393224 | tf_op jit(solution)/shard_map/ppermute | solution.py:266
  32.7 0.0 collective-permute-done.8.refs_10_
  32.7 1.0 %collective-permute-done.9.refs_11_ = bf16[2,2,128,128]{3,2,1,0:T(8,128)(2,1)S(1)} collective-permute-done((bf16[2,2,128,128]{3,2,1,0:T(8,128)(2,1)S(1)}, bf16[2,2,128,128]{3,2,1,0:T(8,128)(2,1)S(1)}, u32[]{:S(2)}, u32[]{:S(2)}) %collective-permute-start.9) | collective-permute-done | bytes 131104 | tf_op jit(solution)/shard_map/ppermute | solution.py:266
  33.7 0.0 collective-permute-done.11.refs_13_
  33.7 0.0 collective-permute-done.refs_1_
  33.7 0.0 copy-start.3
  33.7 0.0 collective-permute-done.12.refs_14_
  33.7 0.0 copy-start.6
  33.7 0.0 copy-done
  33.7 0.0 copy-done.1
  33.7 0.0 copy-done.2
  33.7 0.0 copy-done.7
  33.7 0.0 copy-done.8
  33.8 0.0 copy-done.4
  33.8 0.0 copy-done.9
  33.8 0.0 copy-done.10
  33.8 0.0 copy-done.11
  33.8 0.5 %copy-done.12 = bf16[2,2,128,128]{3,2,1,0:T(8,128)(2,1)} copy-done((bf16[2,2,128,128]{3,2,1,0:T(8,128)(2,1)}, bf16[2,2,128,128]{3,2,1,0:T(8,128)(2,1)S(1)}, u32[]{:S(2)}) %copy-start.12) | copy-done | bytes 131096
  34.3 0.1 copy-done.5
  34.4 0.2 copy-done.3
  34.6 0.1 copy-done.6
  34.7 11.2 %shard_map.60 = (f32[1,256,16,128]{3,2,1,0:T(8,128)}, f32[16,1,256]{2,1,0:T(1,128)}, f32[16,1,256]{2,1,0:T(1,128)}) custom-call(bf16[2,1024,128]{2,1,0:T(8,128)(2,1)} %get-tuple-element.7.refs_0_, bf16[2,1024,128]{2,1,0:T(8,128)(2,1)} %copy-done.3, bf16[2,2,128,128]{3,2,1,0:T(8,128)(2,1)} %get-tuple-element.9.refs_2_, bf16[2,2,128,128]{3,2,1,0:T(8,128)(2,1)} %copy-done, ...), custom_call_target="tpu_custom_call" | custom-call | tf_op jit(solution)/shard_map/pallas_call | solution.py:237
  (11 shorter events, 0.1 us)
Async XLA Ops:
  2.8 6.1 %collective-permute-start.1 = (bf16[2,2,128,128]{3,2,1,0:T(8,128)(2,1)}, bf16[2,2,128,128]{3,2,1,0:T(8,128)(2,1)S(1)}, u32[]{:S(2)}, u32[]{:S(2)}) collective-permute-start(bf16[2,2,128,128]{3,2,1,0:T(8,128)(2,1)} %get-tuple-element.10), channel_id=1, source_target_pairs={{0,1},{1,0},{2,3},{3,2},{4,5},{5,4},{6,7},{7,6},{8,9},{9,8},{10,11... | collective-permute-start | bytes 393224 | tf_op jit(solution)/shard_map/ppermute | solution.py:266
  4.9 5.9 %collective-permute-start.2 = (bf16[2,2,128,128]{3,2,1,0:T(8,128)(2,1)}, bf16[2,2,128,128]{3,2,1,0:T(8,128)(2,1)S(1)}, u32[]{:S(2)}, u32[]{:S(2)}) collective-permute-start(bf16[2,2,128,128]{3,2,1,0:T(8,128)(2,1)} %get-tuple-element.9.refs_2_), channel_id=1, source_target_pairs={{0,8},{2,10},{4,12},{6,14},{8,16},{10,18},{12,20},{14,22},{16,24},... | collective-permute-start | bytes 393224 | tf_op jit(solution)/shard_map/ppermute | solution.py:266
  8.7 25.0 %collective-permute-start = (bf16[2,1024,128]{2,1,0:T(8,128)(2,1)}, bf16[2,1024,128]{2,1,0:T(8,128)(2,1)S(1)}, u32[]{:S(2)}, u32[]{:S(2)}) collective-permute-start(bf16[2,1024,128]{2,1,0:T(8,128)(2,1)} %get-tuple-element.8), channel_id=1, source_target_pairs={{0,1},{1,0},{2,3},{3,2},{4,5},{5,4},{6,7},{7,6},{8,9},{9,8},{10,11... | collective-permute-start | bytes 1572872 | tf_op jit(solution)/shard_map/ppermute | solution.py:266
  8.9 24.8 %copy-start = (bf16[2,2,128,128]{3,2,1,0:T(8,128)(2,1)}, bf16[2,2,128,128]{3,2,1,0:T(8,128)(2,1)S(1)}, u32[]{:S(2)}) copy-start(bf16[2,2,128,128]{3,2,1,0:T(8,128)(2,1)S(1)} %collective-permute-done.1.refs_3_) | copy-start | bytes 393220
  8.9 5.6 %collective-permute-start.3 = (bf16[2,2,128,128]{3,2,1,0:T(8,128)(2,1)S(1)}, bf16[2,2,128,128]{3,2,1,0:T(8,128)(2,1)S(1)}, u32[]{:S(2)}, u32[]{:S(2)}) collective-permute-start(bf16[2,2,128,128]{3,2,1,0:T(8,128)(2,1)S(1)} %collective-permute-done.1.refs_3_), channel_id=1, source_target_pairs={{0,8},{2,10},{4,12},{6,14},{8,16},{10,18},{12,20},{14,22},{16,24},... | collective-permute-start | bytes 393224 | tf_op jit(solution)/shard_map/ppermute | solution.py:266
  10.8 22.9 %copy-start.1 = (bf16[2,2,128,128]{3,2,1,0:T(8,128)(2,1)}, bf16[2,2,128,128]{3,2,1,0:T(8,128)(2,1)S(1)}, u32[]{:S(2)}) copy-start(bf16[2,2,128,128]{3,2,1,0:T(8,128)(2,1)S(1)} %collective-permute-done.2.refs_4_) | copy-start | bytes 393220
  14.5 19.2 %copy-start.2 = (bf16[2,2,128,128]{3,2,1,0:T(8,128)(2,1)}, bf16[2,2,128,128]{3,2,1,0:T(8,128)(2,1)S(1)}, u32[]{:S(2)}) copy-start(bf16[2,2,128,128]{3,2,1,0:T(8,128)(2,1)S(1)} %collective-permute-done.3.refs_5_) | copy-start | bytes 393220
  14.6 13.4 %collective-permute-start.10 = (bf16[2,2,2,128,128]{4,3,2,1,0:T(8,128)(2,1)S(1)}, bf16[2,2,2,128,128]{4,3,2,1,0:T(8,128)(2,1)S(1)}, u32[]{:S(2)}, u32[]{:S(2)}) collective-permute-start(bf16[2,2,2,128,128]{4,3,2,1,0:T(8,128)(2,1)S(1)} %pad_maximum_fusion), channel_id=1, source_target_pairs={{0,4},{2,6},{4,0},{6,2},{8,12},{10,14},{12,8},{14,10},{16,20},{18,... | collective-permute-start | bytes 786440 | tf_op jit(solution)/shard_map/ppermute | solution.py:266
  15.9 4.3 %collective-permute-start.6 = (bf16[2,2,128,128]{3,2,1,0:T(8,128)(2,1)S(1)}, bf16[2,2,128,128]{3,2,1,0:T(8,128)(2,1)S(1)}, u32[]{:S(2)}, u32[]{:S(2)}) collective-permute-start(bf16[2,2,128,128]{3,2,1,0:T(8,128)(2,1)S(1)} %collective-permute-done.2.refs_4_), channel_id=1, source_target_pairs={{0,2},{2,8},{4,6},{6,12},{8,10},{10,16},{12,14},{14,20},{16,18},{1... | collective-permute-start | bytes 393224 | tf_op jit(solution)/shard_map/ppermute | solution.py:266
  18.2 9.0 %collective-permute-start.4 = (bf16[2,2,128,128]{3,2,1,0:T(8,128)(2,1)S(1)}, bf16[2,2,128,128]{3,2,1,0:T(8,128)(2,1)S(1)}, u32[]{:S(2)}, u32[]{:S(2)}) collective-permute-start(bf16[2,2,128,128]{3,2,1,0:T(8,128)(2,1)S(1)} %collective-permute-done.2.refs_4_), channel_id=1, source_target_pairs={{0,4},{2,6},{4,8},{6,10},{8,12},{10,14},{12,16},{14,18},{16,20},{1... | collective-permute-start | bytes 393224 | tf_op jit(solution)/shard_map/ppermute | solution.py:266
  18.5 9.5 %collective-permute-start.7 = (bf16[2,2,128,128]{3,2,1,0:T(8,128)(2,1)S(1)}, bf16[2,2,128,128]{3,2,1,0:T(8,128)(2,1)S(1)}, u32[]{:S(2)}, u32[]{:S(2)}) collective-permute-start(bf16[2,2,128,128]{3,2,1,0:T(8,128)(2,1)S(1)} %collective-permute-done.3.refs_5_), channel_id=1, source_target_pairs={{0,2},{2,8},{4,6},{6,12},{8,10},{10,16},{12,14},{14,20},{16,18},{1... | collective-permute-start | bytes 393224 | tf_op jit(solution)/shard_map/ppermute | solution.py:266
  20.1 13.6 %copy-start.7 = (bf16[2,2,128,128]{3,2,1,0:T(8,128)(2,1)}, bf16[2,2,128,128]{3,2,1,0:T(8,128)(2,1)S(1)}, u32[]{:S(2)}) copy-start(bf16[2,2,128,128]{3,2,1,0:T(8,128)(2,1)S(1)} %collective-permute-done.6.refs_8_) | copy-start | bytes 393220
  20.2 9.8 %collective-permute-start.5 = (bf16[2,2,128,128]{3,2,1,0:T(8,128)(2,1)S(1)}, bf16[2,2,128,128]{3,2,1,0:T(8,128)(2,1)S(1)}, u32[]{:S(2)}, u32[]{:S(2)}) collective-permute-start(bf16[2,2,128,128]{3,2,1,0:T(8,128)(2,1)S(1)} %collective-permute-done.3.refs_5_), channel_id=1, source_target_pairs={{0,4},{2,6},{4,8},{6,10},{8,12},{10,14},{12,16},{14,18},{16,20},{1... | collective-permute-start | bytes 393224 | tf_op jit(solution)/shard_map/ppermute | solution.py:266
  27.2 6.5 %copy-start.8 = (bf16[2,2,128,128]{3,2,1,0:T(8,128)(2,1)}, bf16[2,2,128,128]{3,2,1,0:T(8,128)(2,1)S(1)}, u32[]{:S(2)}) copy-start(bf16[2,2,128,128]{3,2,1,0:T(8,128)(2,1)S(1)} %collective-permute-done.4.refs_6_) | copy-start | bytes 393220
  27.2 6.4 %collective-permute-start.11 = (bf16[2,2,2,128,128]{4,3,2,1,0:T(8,128)(2,1)S(1)}, bf16[2,2,2,128,128]{4,3,2,1,0:T(8,128)(2,1)S(1)}, u32[]{:S(2)}, u32[]{:S(2)}) collective-permute-start(bf16[2,2,2,128,128]{4,3,2,1,0:T(8,128)(2,1)S(1)} %pad_maximum_fusion.1), channel_id=1, source_target_pairs={{0,2},{2,0},{4,6},{6,4},{8,10},{10,8},{12,14},{14,12},{16,18},{18,... | collective-permute-start | bytes 786440 | tf_op jit(solution)/shard_map/ppermute | solution.py:266
  28.0 5.8 %copy-start.4 = (bf16[2,2,2,128,128]{4,3,2,1,0:T(8,128)(2,1)}, bf16[2,2,2,128,128]{4,3,2,1,0:T(8,128)(2,1)S(1)}, u32[]{:S(2)}) copy-start(bf16[2,2,2,128,128]{4,3,2,1,0:T(8,128)(2,1)S(1)} %collective-permute-done.10.refs_12_) | copy-start | bytes 786436
  28.0 5.7 %collective-permute-start.12 = (bf16[2,2,2,128,128]{4,3,2,1,0:T(8,128)(2,1)S(1)}, bf16[2,2,2,128,128]{4,3,2,1,0:T(8,128)(2,1)S(1)}, u32[]{:S(2)}, u32[]{:S(2)}) collective-permute-start(bf16[2,2,2,128,128]{4,3,2,1,0:T(8,128)(2,1)S(1)} %collective-permute-done.10.refs_12_), channel_id=1, source_target_pairs={{0,2},{2,0},{4,6},{6,4},{8,10},{10,8},{12,14},{14,12},{16,18},{18,... | collective-permute-start | bytes 786440 | tf_op jit(solution)/shard_map/ppermute | solution.py:266
  28.0 5.7 %copy-start.9 = (bf16[2,2,128,128]{3,2,1,0:T(8,128)(2,1)}, bf16[2,2,128,128]{3,2,1,0:T(8,128)(2,1)S(1)}, u32[]{:S(2)}) copy-start(bf16[2,2,128,128]{3,2,1,0:T(8,128)(2,1)S(1)} %collective-permute-done.7.refs_9_) | copy-start | bytes 393220
  28.0 4.6 %collective-permute-start.8 = (bf16[2,2,128,128]{3,2,1,0:T(8,128)(2,1)S(1)}, bf16[2,2,128,128]{3,2,1,0:T(8,128)(2,1)S(1)}, u32[]{:S(2)}, u32[]{:S(2)}) collective-permute-start(bf16[2,2,128,128]{3,2,1,0:T(8,128)(2,1)S(1)} %collective-permute-done.4.refs_6_), channel_id=1, source_target_pairs={{0,2},{2,0},{4,6},{6,4},{8,10},{10,8},{12,14},{14,12},{16,18},{18,... | collective-permute-start | bytes 393224 | tf_op jit(solution)/shard_map/ppermute | solution.py:266
  29.9 3.9 %copy-start.10 = (bf16[2,2,128,128]{3,2,1,0:T(8,128)(2,1)}, bf16[2,2,128,128]{3,2,1,0:T(8,128)(2,1)S(1)}, u32[]{:S(2)}) copy-start(bf16[2,2,128,128]{3,2,1,0:T(8,128)(2,1)S(1)} %collective-permute-done.5.refs_7_) | copy-start | bytes 393220
  29.9 3.8 %collective-permute-start.9 = (bf16[2,2,128,128]{3,2,1,0:T(8,128)(2,1)S(1)}, bf16[2,2,128,128]{3,2,1,0:T(8,128)(2,1)S(1)}, u32[]{:S(2)}, u32[]{:S(2)}) collective-permute-start(bf16[2,2,128,128]{3,2,1,0:T(8,128)(2,1)S(1)} %collective-permute-done.5.refs_7_), channel_id=1, source_target_pairs={{0,2},{2,0},{4,6},{6,4},{8,10},{10,8},{12,14},{14,12},{16,18},{18,... | collective-permute-start | bytes 393224 | tf_op jit(solution)/shard_map/ppermute | solution.py:266
  32.7 1.1 %copy-start.11 = (bf16[2,2,128,128]{3,2,1,0:T(8,128)(2,1)}, bf16[2,2,128,128]{3,2,1,0:T(8,128)(2,1)S(1)}, u32[]{:S(2)}) copy-start(bf16[2,2,128,128]{3,2,1,0:T(8,128)(2,1)S(1)} %collective-permute-done.8.refs_10_) | copy-start | bytes 393220
  33.7 0.6 %copy-start.12 = (bf16[2,2,128,128]{3,2,1,0:T(8,128)(2,1)}, bf16[2,2,128,128]{3,2,1,0:T(8,128)(2,1)S(1)}, u32[]{:S(2)}) copy-start(bf16[2,2,128,128]{3,2,1,0:T(8,128)(2,1)S(1)} %collective-permute-done.9.refs_11_) | copy-start | bytes 393220
  33.7 0.7 %copy-start.5 = (bf16[2,2,2,128,128]{4,3,2,1,0:T(8,128)(2,1)}, bf16[2,2,2,128,128]{4,3,2,1,0:T(8,128)(2,1)S(1)}, u32[]{:S(2)}) copy-start(bf16[2,2,2,128,128]{4,3,2,1,0:T(8,128)(2,1)S(1)} %collective-permute-done.11.refs_13_) | copy-start | bytes 786436
  33.7 1.0 %copy-start.3 = (bf16[2,1024,128]{2,1,0:T(8,128)(2,1)}, bf16[2,1024,128]{2,1,0:T(8,128)(2,1)S(1)}, u32[]{:S(2)}) copy-start(bf16[2,1024,128]{2,1,0:T(8,128)(2,1)S(1)} %collective-permute-done.refs_1_) | copy-start | bytes 1572868
  33.7 1.0 %copy-start.6 = (bf16[2,2,2,128,128]{4,3,2,1,0:T(8,128)(2,1)}, bf16[2,2,2,128,128]{4,3,2,1,0:T(8,128)(2,1)S(1)}, u32[]{:S(2)}) copy-start(bf16[2,2,2,128,128]{4,3,2,1,0:T(8,128)(2,1)S(1)} %collective-permute-done.12.refs_14_) | copy-start | bytes 786436

commit v4 on v3

v4 whole, which is shorter than its diff:
```python
import functools
import math

import jax
import jax.numpy as jnp
from jax import lax
from jax.experimental import pallas as pl
from jax.experimental.pallas import tpu as pltpu
from jax.sharding import PartitionSpec as P

QUERY_HEADS = 32
KEY_VALUE_HEADS = 4
WIN = 8
LAYER = 4
GROUP = QUERY_HEADS // KEY_VALUE_HEADS
BF16 = jnp.bfloat16
F32 = jnp.float32
VMEM_LIMIT = 20 * 2**20
NEG = -1e30
SPAN = 512
BLOCK = 128
COST = 10**9
PACK_LIMIT = 56 * 2**20


def slot_of(head, per, count):
    return lax.rem(head // per - lax.axis_index("head") + count, count)


def place(outs, head, per, at, x):
    for d in range(len(outs)):

        @pl.when(slot_of(head, per, len(outs)) == d)
        def _():
            outs[d][at + (head % per,)] = x


def pack_kv_kernel(k_hbm, v_hbm, *refs):
    outs, (flat, wide, sems) = refs[:-3], refs[-3:]
    rows, heads, width = k_hbm.shape[1:]
    loads = [
        pltpu.make_async_copy(ref.at[0], flat.at[i], sems.at[i])
        for i, ref in enumerate((k_hbm, v_hbm))
    ]
    for load in loads:
        load.start()
    for i in range(2):
        loads[i].wait()
        wide.at[i].reshape(rows, 8, width)[:, :heads, :] = flat[i].astype(F32)
        for head in range(heads):
            x = wide[i, pl.ds(head, rows, stride=8), :].astype(BF16)
            place(outs, head, heads // len(outs), (i,), x)


def pack_kv(keys, values, count):
    rows, heads, width = keys.shape[1:]
    shape = jax.ShapeDtypeStruct((2, heads // count, rows, width), BF16)
    return pl.pallas_call(
        pack_kv_kernel,
        out_shape=(shape,) * count,
        in_specs=[pl.BlockSpec(memory_space=pl.ANY)] * 2,
        out_specs=[pl.BlockSpec(memory_space=pltpu.VMEM)] * count,
        scratch_shapes=[
            pltpu.VMEM((2, rows, heads, width), BF16),
            pltpu.VMEM((2, rows * 8, width), F32),
            pltpu.SemaphoreType.DMA((2,)),
        ],
        compiler_params=pltpu.CompilerParams(vmem_limit_bytes=PACK_LIMIT),
    )(keys, values)


def pack_q_kernel(q_ref, *outs):
    rows, heads, width = q_ref.shape[1:]
    for head in range(heads // GROUP):
        x = q_ref[0, :, head * GROUP : (head + 1) * GROUP, :].astype(F32)
        x = x.reshape(rows * GROUP, width).astype(BF16)
        place(outs, head, heads // GROUP // len(outs), (), x)


def pack_q(queries, count):
    rows, heads, width = queries.shape[1:]
    shape = jax.ShapeDtypeStruct((heads // GROUP // count, rows * GROUP, width), BF16)
    return pl.pallas_call(
        pack_q_kernel,
        out_shape=(shape,) * count,
        in_specs=[pl.BlockSpec(memory_space=pltpu.VMEM)],
        out_specs=[pl.BlockSpec(memory_space=pltpu.VMEM)] * count,
        compiler_params=pltpu.CompilerParams(vmem_limit_bytes=VMEM_LIMIT),
    )(queries)


def attend_kernel(n, count, slots, singles, offsets, block, begin, end, *refs):
    total = len(offsets) * count
    here = len(slots)
    loads_n = singles + (total - singles) // count
    q_hbm, refs = refs[:here], refs[here:]
    kv_hbm, refs = refs[:loads_n], refs[loads_n:]
    if not begin:
        refs = refs[3 * here :]
    if end:
        out_hbm, max_ref, sum_ref = refs[:3]
        refs = refs[3:]
    acc, mbuf, lbuf = refs[:here], refs[here : 2 * here], refs[2 * here : 3 * here]
    qbuf, kvbuf, order, qsem, ksem, osem = refs[3 * here :]
    per, m_rows, width = q_hbm[0].shape
    rows = m_rows // GROUP
    half = count * rows // 2
    small, large = SPAN // 2 // rows, SPAN // rows
    p = lax.axis_index("ctx")
    h = lax.axis_index("head")
    factor = math.log2(math.e) / math.sqrt(width)

    loads = [pltpu.make_async_copy(q_hbm[s], qbuf.at[s], qsem.at[s]) for s in range(here)]
    for i, ref in enumerate(kv_hbm):
        if i < singles:
            to = kvbuf.at[i]
        else:
            to = kvbuf.at[pl.ds(singles + (i - singles) * count, count)]
        loads.append(pltpu.make_async_copy(ref, to, ksem.at[i]))
    for load in loads:
        load.start()

    def start_of(pair, chunk):
        r = chunk * rows
        return jnp.where(r < half, 2 * pair * half + r, (2 * n - 2 - 2 * pair) * half + r)

    chunk_of = [lax.rem(h - d + count, count) for d in range(count)]
    starts = []
    for offset in offsets:
        pair = lax.rem(p - offset(p) + n, n)
        starts += [start_of(pair, chunk) for chunk in chunk_of]
    seen = []
    for s, slot in enumerate(slots):
        mine = start_of(p, chunk_of[slot])
        found = jnp.int32(0)
        if begin:
            order[s, 0] = slot
            found = jnp.int32(1)
        for c in range(total):
            if not begin or c != slot:
                order[s, found] = c
                found = found + (starts[c] < mine).astype(jnp.int32)
        for t in range(large):
            order[s, found + t] = 0
        seen.append(found)

    def chunks_at(kind, s, g, at, chunks):
        return jnp.concatenate(
            [kvbuf[order[s, at + t], kind, g] for t in range(chunks)], axis=0
        )

    def tiles(x):
        return [x[:, t : t + 128] for t in range(0, x.shape[1], 128)]

    def one(s, g, b, k, v, at, diagonal, partial):
        where = slice(b * block, (b + 1) * block)
        row = b * (block // GROUP)
        acc_at = slice(row, row + block // GROUP), slice(g * GROUP, (g + 1) * GROUP)
        score = lax.dot_general(
            qbuf[s, g, where, :], k, (((1,), (1,)), ((), ())), preferred_element_type=F32
        )
        parts = tiles(score)
        if diagonal or partial:
            shape = (block // GROUP, GROUP, 128)
            col = lax.broadcasted_iota(jnp.int32, shape, 2)
            row = lax.broadcasted_iota(jnp.int32, shape, 0) + row
            left = (seen[s] - at) * rows
            for t, x in enumerate(parts):
                x = x.reshape(shape)
                if rows % 128 == 0 and (t * 128 >= rows or not diagonal):
                    if t or diagonal:
                        x = jnp.where(t * 128 < left, x, NEG)
                else:
                    ok = col + t * 128 < left
                    if diagonal and t * 128 < rows:
                        ok &= (col + t * 128 <= row) | (col + t * 128 >= rows)
                    x = jnp.where(ok, x, NEG)
                parts[t] = x.reshape(block, 128)
        top = jnp.max(functools.reduce(jnp.maximum, parts), axis=1, keepdims=True)
        if not diagonal:
            old = mbuf[s][g, where, :]
            top = jnp.maximum(old, top)
        prob = jnp.concatenate(
            [jnp.exp2((x - top) * factor).astype(BF16) for x in parts], axis=1
        )
        got = jnp.dot(prob, v, preferred_element_type=F32)
        gain, mass = got[:, :width], got[:, width:]
        if not diagonal:
            shrink = jnp.exp2((old - top) * factor)
            gain = acc[s][acc_at].reshape(block, width) * shrink + gain
            mass = lbuf[s][g, where, :] * shrink + mass
        mbuf[s][g, where, :] = jnp.broadcast_to(top, (block, 128))
        lbuf[s][g, where, :] = mass
        acc[s][acc_at] = gain.reshape(block // GROUP, GROUP, width)

    def run(s, at, chunks, diagonal=False, partial=False):
        for g in range(per):
            k = chunks_at(0, s, g, at, chunks)
            v = chunks_at(1, s, g, at, chunks)
            v = jnp.concatenate([v, jnp.ones((chunks * rows, 128), BF16)], axis=1)
            for b in range(m_rows // block):
                one(s, g, b, k, v, at, diagonal, partial)

    def to_lanes(x):
        x = x.reshape(rows, GROUP, 128)[:, :, :rows]
        a = lax.broadcasted_iota(jnp.int32, (rows, GROUP, rows), 0)
        b = lax.broadcasted_iota(jnp.int32, (rows, GROUP, rows), 2)
        return jnp.sum(jnp.where(a == b, x, 0.0), axis=0)

    for load in loads:
        load.wait()
    base = small if begin else 0
    if begin:
        for s in range(here):
            run(s, 0, small, diagonal=True)
    saves = []
    for s, slot in enumerate(slots):
        left = jnp.maximum(seen[s] - base, 0)
        full = left // large
        rest = (left - full * large + small - 1) // small

        def whole(t, _):
            run(s, base + t * large, large)
            return 0

        def part(t, _):
            run(s, base + full * large + t * small, small, partial=True)
            return 0

        lax.fori_loop(0, full, whole, 0)
        lax.fori_loop(0, rest, part, 0)
        if not end:
            continue
        row0 = pl.multiple_of(chunk_of[slot] * rows, rows)
        saves.append(
            pltpu.make_async_copy(acc[s], out_hbm.at[0, pl.ds(row0, rows)], osem.at[s])
        )
        saves[-1].start()
        for g in range(per):
            tops = to_lanes(mbuf[s][g]) * (1.0 / math.sqrt(width))
            sums = to_lanes(lbuf[s][g])
            for d in range(count):

                @pl.when(chunk_of[slot] == d)
                def _():
                    max_ref[g * GROUP : (g + 1) * GROUP, 0, d * rows : (d + 1) * rows] = tops
                    sum_ref[g * GROUP : (g + 1) * GROUP, 0, d * rows : (d + 1) * rows] = sums
    for save in saves:
        save.wait()


def attend(q_list, slots, kv_list, merged, offsets, n, state, end):
    count, here = len(q_list), len(slots)
    per, m_rows, width = q_list[0].shape
    rows = m_rows // GROUP
    total = len(offsets) * count
    loads = len(kv_list) + len(merged)
    begin = state is None
    near, away = pl.BlockSpec(memory_space=pltpu.VMEM), pl.BlockSpec(memory_space=pl.ANY)
    held = [jax.ShapeDtypeStruct((rows, per * GROUP, width), F32)] * here
    held += [jax.ShapeDtypeStruct((per, m_rows, 128), F32)] * (2 * here)
    out_shape, out_specs, aliases = [], [], {}
    if end:
        out_shape += [
            jax.ShapeDtypeStruct((1, count * rows, per * GROUP, width), F32),
            jax.ShapeDtypeStruct((per * GROUP, 1, count * rows), F32),
            jax.ShapeDtypeStruct((per * GROUP, 1, count * rows), F32),
        ]
        out_specs += [away, near, near]
    if not begin:
        aliases = {here + loads + i: len(out_shape) + i for i in range(3 * here)}
    out_shape += held
    out_specs += [near] * len(held)
    outs = pl.pallas_call(
        functools.partial(
            attend_kernel, n, count, slots, len(kv_list), offsets, min(BLOCK, m_rows), begin, end
        ),
        out_shape=out_shape,
        in_specs=[away] * (here + loads) + [near] * (0 if begin else len(held)),
        out_specs=out_specs,
        input_output_aliases=aliases,
        scratch_shapes=[
            pltpu.VMEM((here, per, m_rows, width), BF16),
            pltpu.VMEM((total, 2, per, rows, width), BF16),
            pltpu.SMEM((here, total + 1 + SPAN // rows), jnp.int32),
            pltpu.SemaphoreType.DMA((here,)),
            pltpu.SemaphoreType.DMA((loads,)),
            pltpu.SemaphoreType.DMA((here,)),
        ],
        compiler_params=pltpu.CompilerParams(vmem_limit_bytes=VMEM_LIMIT),
        cost_estimate=pl.CostEstimate(
            flops=COST * len(offsets) * here, bytes_accessed=2**20, transcendentals=0
        ),
    )(*[q_list[s] for s in slots], *kv_list, *merged, *(state or []))
    if end:
        return tuple(outs[:3])
    return [outs[i * here : (i + 1) * here] for i in range(3)]


def join(*states):
    return [x for part in zip(*states) for xs in part for x in xs]


def along(block, axis, target):
    size = lax.axis_size(axis)
    return lax.ppermute(block, axis, [(i, target(i) % size) for i in range(size)])


def climb(block, d, layer):
    n, count = lax.axis_size("ctx"), lax.axis_size("head")
    edges = []
    for p in range(n):
        for h in range(count):
            edges.append((p * count + h, (p + layer) % n * count + (h + d) % count))
    return lax.ppermute(block, ("ctx", "head"), edges)


def local(queries, keys, values):
    n = lax.axis_size("ctx")
    count = lax.axis_size("head")
    me = lax.axis_index("ctx")
    swap = lambda x, d: along(x, "head", lambda i: i + d)

    kv = pack_kv(keys, values, count)
    q = pack_q(queries, count)
    own = [kv[0]] + [swap(kv[d], d) for d in range(1, count)]

    layer = LAYER
    up = jnp.stack([climb(x, d, layer) for d, x in enumerate(kv)])
    q = [q[0]] + [swap(q[d], d) for d in range(1, count)]

    both = lax.optimization_barrier(jnp.stack(own))
    side = along(both, "ctx", lambda i: i + layer // 2)
    far = along(up, "ctx", lambda i: i + layer // 2)
    odd = along(up, "ctx", lambda i: i + layer - 1 if i & 1 else i + 1)
    near = jnp.where(lax.rem(me, 2) == 0, both, up)
    near = along(near, "ctx", lambda i: i ^ 1)
    side_c = along(side, "ctx", lambda i: i ^ 1)

    bit = lambda p, even, other: jnp.where(lax.rem(p, 2) == 0, even, other)
    offsets = [
        lambda p: 0,
        lambda p: layer,
        lambda p: layer + 2,
        lambda p: bit(p, layer + 3, layer + 1),
        lambda p: bit(p, layer + 1, layer + 3),
        lambda p: 2,
        lambda p: bit(p, 3, 1),
        lambda p: bit(p, 1, 3),
    ]
    own_at, up_at, far_at, odd_at, far_c_at, side_at, near_at, side_c_at = offsets
    slots = list(range(count))
    early = [both, up, near], [own_at, up_at, near_at], n
    state = join(attend(q, slots, [], *early, None, False))
    state, far = lax.optimization_barrier((state, far))
    far_c = along(far, "ctx", lambda i: i ^ 1)
    late = [side, side_c, odd, far, far_c], [side_at, side_c_at, odd_at, far_at, far_c_at], n
    return attend(q, slots, [], *late, state, True)


def solution(mesh):
    in_specs = (
        P("ctx", "head", None, None),
        P("ctx", "head", None, None),
        P("ctx", "head", None, None),
    )
    out_specs = (P("ctx", None, "head", None), P("head", "ctx", None), P("head", "ctx", None))
    return jax.shard_map(local, mesh=mesh, in_specs=in_specs, out_specs=out_specs, check_vma=False)
```

time: 46.5 us -> 38.2 us (0.82)
  waiting for transfers between devices: 13.3 us -> 7.01 us
  Pallas kernels: 15.9 us -> 13.3 us
  starting transfers between devices: 14 us -> 14.7 us
    ppermute x13 -> x8, waiting for transfers between devices: 13.3 us -> 5.38 us  [along(): lax.ppermute(block, axis, [(i, target(i) % size) for i in range(size)])]
    pallas_call x3 -> x4, Pallas kernels: 15.9 us -> 13.3 us  [the longest x2 11.2 us: attend(): pl.pallas_call(functools.partial(attend_kernel, n, count, slots, len(kv_l...]
    ppermute x0 -> x2, starting transfers between devices: none -> 2.54 us  [climb(): return lax.ppermute(block, ('ctx', 'head'), edges)]
    ppermute x13 -> x8, starting transfers between devices: 14 us -> 12.2 us  [along(): lax.ppermute(block, axis, [(i, target(i) % size) for i in range(size)])]
    ppermute x0 -> x2, waiting for transfers between devices: none -> 1.63 us  [climb(): return lax.ppermute(block, ('ctx', 'head'), edges)]
    broadcast_in_dim x2 -> x0, other arithmetic: 0.99 us -> none  [local(): jnp.where(core, a, b)[None]]
    another operation x0 -> x1, other arithmetic: none -> 0.93 us  [local(): both = lax.optimization_barrier(jnp.stack(own))]
    unnamed x26 -> x2, local copies, waits for them, and re-layouts: 0.94 us -> 1.22 us
  transfers between devices with their start and end apart: 13 -> 10, of which waited for: 6 -> 4; matrix products, arithmetic and copies ran while one was open for 2% -> 3% of each run, Pallas kernels for 5% -> 10%
where the time goes in v4:
time: 38.2 us; the launch traced here: 38.1 us
  starting transfers between devices  14.7 us (38%)
  Pallas kernels  13.3 us (35%)
  waiting for transfers between devices  7.01 us (18%)
  local copies, waits for them, and re-layouts  1.22 us (3%)
  other arithmetic  0.97 us (3%)
  between operations  0.84 us (2%)
    ppermute x8, starting transfers between devices, along(): lax.ppermute(block, axis, [(i, target(i) % size) for i in range(size)])  12.2 us
    pallas_call x2, Pallas kernels, attend(): pl.pallas_call(functools.partial(attend_kernel, n, count, slots, len(kv_l...  11.2 us
    ppermute x8, waiting for transfers between devices, along(): lax.ppermute(block, axis, [(i, target(i) % size) for i in range(size)])  5.38 us
    ppermute x2, starting transfers between devices, climb(): return lax.ppermute(block, ('ctx', 'head'), edges)  2.54 us
    pallas_call x1, Pallas kernels, pack_kv(): pl.pallas_call(pack_kv_kernel, out_shape=(shape,) * count, in_specs=[pl.B...  1.83 us
    ppermute x2, waiting for transfers between devices, climb(): return lax.ppermute(block, ('ctx', 'head'), edges)  1.63 us
    unnamed x2, local copies, waits for them, and re-layouts  1.22 us
    another operation x1, other arithmetic, local(): both = lax.optimization_barrier(jnp.stack(own))  0.93 us
  transfers between devices with their start and end apart: 10, of which 4 were waited for; matrix products, arithmetic and copies ran while one was open for 3% of the time, Pallas kernels for 10%

profile of v4, /device:TPU:1, one launch (start us, length us, event | category | flops | bytes accessed | tf_op | source)
XLA Modules:
  0.0 38.1 jit_solution(3347529896835515168)
XLA Ops:
  0.6 1.8 %shard_map.59 = (bf16[2,2,128,128]{3,2,1,0:T(8,128)(2,1)}, bf16[2,2,128,128]{3,2,1,0:T(8,128)(2,1)}) custom-call(bf16[1,128,4,128]{3,2,1,0:T(4,128)(2,1)} %k_hbm.1, bf16[1,128,4,128]{3,2,1,0:T(4,128)(2,1)} %v_hbm.1), custom_call_target="tpu_custom_call" | custom-call | tf_op jit(solution)/shard_map/pallas_call | solution.py:58
  2.5 2.1 %collective-permute-start.1 = (bf16[2,2,128,128]{3,2,1,0:T(8,128)(2,1)}, bf16[2,2,128,128]{3,2,1,0:T(8,128)(2,1)S(1)}, u32[]{:S(2)}, u32[]{:S(2)}) collective-permute-start(bf16[2,2,128,128]{3,2,1,0:T(8,128)(2,1)} %get-tuple-element.26), channel_id=1, source_target_pairs={{0,1},{1,0},{2,3},{3,2},{4,5},{5,4},{6,7},{7,6},{8,9},{9,8},{10,11... | collective-permute-start | bytes 393224 | tf_op jit(solution)/shard_map/ppermute | solution.py:306
  4.6 1.3 %collective-permute-start.4 = (bf16[2,2,128,128]{3,2,1,0:T(8,128)(2,1)}, bf16[2,2,128,128]{3,2,1,0:T(8,128)(2,1)S(1)}, u32[]{:S(2)}, u32[]{:S(2)}) collective-permute-start(bf16[2,2,128,128]{3,2,1,0:T(8,128)(2,1)} %get-tuple-element.25), channel_id=1, source_target_pairs={{0,8},{1,9},{2,10},{3,11},{4,12},{5,13},{6,14},{7,15},{8,16},{9,17... | collective-permute-start | bytes 393224 | tf_op jit(solution)/shard_map/ppermute | solution.py:315
  5.9 1.2 %collective-permute-start.5 = (bf16[2,2,128,128]{3,2,1,0:T(8,128)(2,1)}, bf16[2,2,128,128]{3,2,1,0:T(8,128)(2,1)S(1)}, u32[]{:S(2)}, u32[]{:S(2)}) collective-permute-start(bf16[2,2,128,128]{3,2,1,0:T(8,128)(2,1)} %get-tuple-element.26), channel_id=1, source_target_pairs={{0,9},{1,8},{2,11},{3,10},{4,13},{5,12},{6,15},{7,14},{8,17},{9,16... | collective-permute-start | bytes 393224 | tf_op jit(solution)/shard_map/ppermute | solution.py:315
  7.1 0.0 copy-start
  7.1 1.2 %copy-done = bf16[1,128,32,128]{3,2,1,0:T(8,128)(2,1)S(1)} copy-done((bf16[1,128,32,128]{3,2,1,0:T(8,128)(2,1)S(1)}, bf16[1,128,32,128]{3,2,1,0:T(8,128)(2,1)}, u32[]{:S(2)}) %copy-start) | copy-done | bytes 1048600
  8.4 0.3 shard_map.58
  8.7 1.3 %collective-permute-start = (bf16[2,1024,128]{2,1,0:T(8,128)(2,1)S(1)}, bf16[2,1024,128]{2,1,0:T(8,128)(2,1)S(1)}, u32[]{:S(2)}, u32[]{:S(2)}) collective-permute-start(bf16[2,1024,128]{2,1,0:T(8,128)(2,1)S(1)} %get-tuple-element.24), channel_id=1, source_target_pairs={{0,1},{1,0},{2,3},{3,2},{4,5},{5,4},{6,7},{7,6},{8,9},{9,8},{10,11... | collective-permute-start | bytes 1572872 | tf_op jit(solution)/shard_map/ppermute | solution.py:306
  10.0 0.0 collective-permute-done.1
  10.0 0.9 %pad_maximum_fusion.refs_2_ = bf16[2,2,2,128,128]{4,3,2,1,0:T(8,128)(2,1)S(1)} fusion(bf16[1,2,2,128,128]{4,3,2,1,0:T(8,128)(2,1)S(1)} %bitcast.5, bf16[1,2,2,128,128]{4,3,2,1,0:T(8,128)(2,1)} %bitcast.4), kind=kLoop, calls=%fused_computation | loop fusion | flops 131072 | bytes 524288 | tf_op jit(solution)/shard_map/stack | solution.py:332
  10.9 1.3 %collective-permute-start.2 = (bf16[2,2,2,128,128]{4,3,2,1,0:T(8,128)(2,1)S(1)}, bf16[2,2,2,128,128]{4,3,2,1,0:T(8,128)(2,1)S(1)}, u32[]{:S(2)}, u32[]{:S(2)}) collective-permute-start(bf16[2,2,2,128,128]{4,3,2,1,0:T(8,128)(2,1)S(1)} %pad_maximum_fusion.refs_2_), channel_id=1, source_target_pairs={{0,4},{2,6},{4,8},{6,10},{8,12},{10,14},{12,16},{14,18},{16,20},{1... | collective-permute-start | bytes 786440 | tf_op jit(solution)/shard_map/ppermute | solution.py:306
  12.2 0.0 collective-permute-done.4
  12.2 1.6 %collective-permute-done.5 = bf16[2,2,128,128]{3,2,1,0:T(8,128)(2,1)S(1)} collective-permute-done((bf16[2,2,128,128]{3,2,1,0:T(8,128)(2,1)}, bf16[2,2,128,128]{3,2,1,0:T(8,128)(2,1)S(1)}, u32[]{:S(2)}, u32[]{:S(2)}) %collective-permute-start.5) | collective-permute-done | bytes 131104 | tf_op jit(solution)/shard_map/ppermute | solution.py:315
  13.8 1.7 %collective-permute-start.7 = (bf16[2,2,2,128,128]{4,3,2,1,0:T(8,128)(2,1)S(1)}, bf16[2,2,2,128,128]{4,3,2,1,0:T(8,128)(2,1)S(1)}, u32[]{:S(2)}, u32[]{:S(2)}) collective-permute-start(bf16[2,2,2,128,128]{4,3,2,1,0:T(8,128)(2,1)S(1)} %get-tuple-element.43), channel_id=1, source_target_pairs={{0,2},{2,0},{4,6},{6,4},{8,10},{10,8},{12,14},{14,12},{16,18},{18,... | collective-permute-start | bytes 786440 | tf_op jit(solution)/shard_map/ppermute | solution.py:306
  15.5 1.2 %collective-permute-start.8 = (bf16[2,2,2,128,128]{4,3,2,1,0:T(8,128)(2,1)S(1)}, bf16[2,2,2,128,128]{4,3,2,1,0:T(8,128)(2,1)S(1)}, u32[]{:S(2)}, u32[]{:S(2)}) collective-permute-start(bf16[2,2,2,128,128]{4,3,2,1,0:T(8,128)(2,1)S(1)} %get-tuple-element.44.refs_3_), channel_id=1, source_target_pairs={{0,4},{2,6},{4,8},{6,10},{8,12},{10,14},{12,16},{14,18},{16,20},{1... | collective-permute-start | bytes 786440 | tf_op jit(solution)/shard_map/ppermute | solution.py:306
  16.7 0.0 collective-permute-start.6
  16.7 2.9 %collective-permute-done.2.refs_2_ = bf16[2,2,2,128,128]{4,3,2,1,0:T(8,128)(2,1)S(1)} collective-permute-done((bf16[2,2,2,128,128]{4,3,2,1,0:T(8,128)(2,1)S(1)}, bf16[2,2,2,128,128]{4,3,2,1,0:T(8,128)(2,1)S(1)}, u32[]{:S(2)}, u32[]{:S(2)}) %collective-permute-start.2) | collective-permute-done | bytes 262176 | tf_op jit(solution)/shard_map/ppermute | solution.py:306
  19.6 3.7 %collective-permute-start.3 = (bf16[2,2,2,128,128]{4,3,2,1,0:T(8,128)(2,1)S(1)}, bf16[2,2,2,128,128]{4,3,2,1,0:T(8,128)(2,1)S(1)}, u32[]{:S(2)}, u32[]{:S(2)}) collective-permute-start(bf16[2,2,2,128,128]{4,3,2,1,0:T(8,128)(2,1)S(1)} %collective-permute-done.2.refs_2_), channel_id=1, source_target_pairs={{0,2},{2,0},{4,6},{6,4},{8,10},{10,8},{12,14},{14,12},{16,18},{18,... | collective-permute-start | bytes 786440 | tf_op jit(solution)/shard_map/ppermute | solution.py:306
  23.3 0.0 collective-permute-done.7.refs_4_
  23.3 1.3 %collective-permute-done.refs_1_ = bf16[2,1024,128]{2,1,0:T(8,128)(2,1)S(1)} collective-permute-done((bf16[2,1024,128]{2,1,0:T(8,128)(2,1)S(1)}, bf16[2,1024,128]{2,1,0:T(8,128)(2,1)S(1)}, u32[]{:S(2)}, u32[]{:S(2)}) %collective-permute-start) | collective-permute-done | bytes 524320 | tf_op jit(solution)/shard_map/ppermute | solution.py:306
  24.6 3.7 %shard_map.60 = (f32[128,16,128]{2,1,0:T(8,128)S(1)}, f32[128,16,128]{2,1,0:T(8,128)S(1)}, f32[2,1024,128]{2,1,0:T(8,128)S(1)}, f32[2,1024,128]{2,1,0:T(8,128)S(...) custom-call(bf16[2,1024,128]{2,1,0:T(8,128)(2,1)S(1)} %get-tuple-element.23.refs_0_, ...), custom_call_target="tpu_custom_call" | custom-call | flops 6000000000 | bytes 1048576 | tf_op jit(solution)/shard_map/pallas_call | solution.py:274
  28.3 0.0 collective-permute-done.8.refs_5_
  28.3 0.9 %collective-permute-start.9 = (bf16[2,2,2,128,128]{4,3,2,1,0:T(8,128)(2,1)S(1)}, bf16[2,2,2,128,128]{4,3,2,1,0:T(8,128)(2,1)S(1)}, u32[]{:S(2)}, u32[]{:S(2)}) collective-permute-start(bf16[2,2,2,128,128]{4,3,2,1,0:T(8,128)(2,1)S(1)} %collective-permute-done.8.refs_5_), channel_id=1, source_target_pairs={{0,2},{2,0},{4,6},{6,4},{8,10},{10,8},{12,14},{14,12},{16,18},{18,... | collective-permute-start | bytes 786440 | tf_op jit(solution)/shard_map/ppermute | solution.py:306
  29.2 0.0 collective-permute-done.6.refs_4_
  29.2 0.0 collective-permute-done.3.refs_3_
  29.2 1.2 %collective-permute-done.9.refs_6_ = bf16[2,2,2,128,128]{4,3,2,1,0:T(8,128)(2,1)S(1)} collective-permute-done((bf16[2,2,2,128,128]{4,3,2,1,0:T(8,128)(2,1)S(1)}, bf16[2,2,2,128,128]{4,3,2,1,0:T(8,128)(2,1)S(1)}, u32[]{:S(2)}, u32[]{:S(2)}) %collective-permute-start.9) | collective-permute-done | bytes 262176 | tf_op jit(solution)/shard_map/ppermute | solution.py:306
  30.4 7.5 %shard_map.61 = (f32[1,256,16,128]{3,2,1,0:T(8,128)}, f32[16,1,256]{2,1,0:T(1,128)}, f32[16,1,256]{2,1,0:T(1,128)}, f32[128,16,128]{2,1,0:T(8,128)S(1)}, f32[128...) custom-call(bf16[2,1024,128]{2,1,0:T(8,128)(2,1)S(1)} %get-tuple-ele, ...), custom_call_target="tpu_custom_call", output_to_operand_aliasing={{3}: (7, {}), {4}: (8, {}), {5}: (9, {}), {6}: (10, {}), {7... | custom-call | flops 10000000000 | bytes 1048576 | tf_op jit(solution)/shard_map/pallas_call | solution.py:274
  (1 shorter events, 0.0 us)
Async XLA Ops:
  2.5 7.5 %collective-permute-start.1 = (bf16[2,2,128,128]{3,2,1,0:T(8,128)(2,1)}, bf16[2,2,128,128]{3,2,1,0:T(8,128)(2,1)S(1)}, u32[]{:S(2)}, u32[]{:S(2)}) collective-permute-start(bf16[2,2,128,128]{3,2,1,0:T(8,128)(2,1)} %get-tuple-element.26), channel_id=1, source_target_pairs={{0,1},{1,0},{2,3},{3,2},{4,5},{5,4},{6,7},{7,6},{8,9},{9,8},{10,11... | collective-permute-start | bytes 393224 | tf_op jit(solution)/shard_map/ppermute | solution.py:306
  4.6 7.6 %collective-permute-start.4 = (bf16[2,2,128,128]{3,2,1,0:T(8,128)(2,1)}, bf16[2,2,128,128]{3,2,1,0:T(8,128)(2,1)S(1)}, u32[]{:S(2)}, u32[]{:S(2)}) collective-permute-start(bf16[2,2,128,128]{3,2,1,0:T(8,128)(2,1)} %get-tuple-element.25), channel_id=1, source_target_pairs={{0,8},{1,9},{2,10},{3,11},{4,12},{5,13},{6,14},{7,15},{8,16},{9,17... | collective-permute-start | bytes 393224 | tf_op jit(solution)/shard_map/ppermute | solution.py:315
  5.9 7.9 %collective-permute-start.5 = (bf16[2,2,128,128]{3,2,1,0:T(8,128)(2,1)}, bf16[2,2,128,128]{3,2,1,0:T(8,128)(2,1)S(1)}, u32[]{:S(2)}, u32[]{:S(2)}) collective-permute-start(bf16[2,2,128,128]{3,2,1,0:T(8,128)(2,1)} %get-tuple-element.26), channel_id=1, source_target_pairs={{0,9},{1,8},{2,11},{3,10},{4,13},{5,12},{6,15},{7,14},{8,17},{9,16... | collective-permute-start | bytes 393224 | tf_op jit(solution)/shard_map/ppermute | solution.py:315
  7.1 1.2 %copy-start = (bf16[1,128,32,128]{3,2,1,0:T(8,128)(2,1)S(1)}, bf16[1,128,32,128]{3,2,1,0:T(8,128)(2,1)}, u32[]{:S(2)}) copy-start(bf16[1,128,32,128]{3,2,1,0:T(8,128)(2,1)} %q_ref.1) | copy-start | bytes 3145732
  8.7 16.0 %collective-permute-start = (bf16[2,1024,128]{2,1,0:T(8,128)(2,1)S(1)}, bf16[2,1024,128]{2,1,0:T(8,128)(2,1)S(1)}, u32[]{:S(2)}, u32[]{:S(2)}) collective-permute-start(bf16[2,1024,128]{2,1,0:T(8,128)(2,1)S(1)} %get-tuple-element.24), channel_id=1, source_target_pairs={{0,1},{1,0},{2,3},{3,2},{4,5},{5,4},{6,7},{7,6},{8,9},{9,8},{10,11... | collective-permute-start | bytes 1572872 | tf_op jit(solution)/shard_map/ppermute | solution.py:306
  10.9 8.8 %collective-permute-start.2 = (bf16[2,2,2,128,128]{4,3,2,1,0:T(8,128)(2,1)S(1)}, bf16[2,2,2,128,128]{4,3,2,1,0:T(8,128)(2,1)S(1)}, u32[]{:S(2)}, u32[]{:S(2)}) collective-permute-start(bf16[2,2,2,128,128]{4,3,2,1,0:T(8,128)(2,1)S(1)} %pad_maximum_fusion.refs_2_), channel_id=1, source_target_pairs={{0,4},{2,6},{4,8},{6,10},{8,12},{10,14},{12,16},{14,18},{16,20},{1... | collective-permute-start | bytes 786440 | tf_op jit(solution)/shard_map/ppermute | solution.py:306
  13.8 9.5 %collective-permute-start.7 = (bf16[2,2,2,128,128]{4,3,2,1,0:T(8,128)(2,1)S(1)}, bf16[2,2,2,128,128]{4,3,2,1,0:T(8,128)(2,1)S(1)}, u32[]{:S(2)}, u32[]{:S(2)}) collective-permute-start(bf16[2,2,2,128,128]{4,3,2,1,0:T(8,128)(2,1)S(1)} %get-tuple-element.43), channel_id=1, source_target_pairs={{0,2},{2,0},{4,6},{6,4},{8,10},{10,8},{12,14},{14,12},{16,18},{18,... | collective-permute-start | bytes 786440 | tf_op jit(solution)/shard_map/ppermute | solution.py:306
  15.5 12.8 %collective-permute-start.8 = (bf16[2,2,2,128,128]{4,3,2,1,0:T(8,128)(2,1)S(1)}, bf16[2,2,2,128,128]{4,3,2,1,0:T(8,128)(2,1)S(1)}, u32[]{:S(2)}, u32[]{:S(2)}) collective-permute-start(bf16[2,2,2,128,128]{4,3,2,1,0:T(8,128)(2,1)S(1)} %get-tuple-element.44.refs_3_), channel_id=1, source_target_pairs={{0,4},{2,6},{4,8},{6,10},{8,12},{10,14},{12,16},{14,18},{16,20},{1... | collective-permute-start | bytes 786440 | tf_op jit(solution)/shard_map/ppermute | solution.py:306
  16.7 12.5 %collective-permute-start.6 = (bf16[2,2,2,128,128]{4,3,2,1,0:T(8,128)(2,1)S(1)}, bf16[2,2,2,128,128]{4,3,2,1,0:T(8,128)(2,1)S(1)}, u32[]{:S(2)}, u32[]{:S(2)}) collective-permute-start(bf16[2,2,2,128,128]{4,3,2,1,0:T(8,128)(2,1)S(1)} %get-tuple-element.44.refs_3_), channel_id=1, source_target_pairs={{0,2},{2,8},{4,6},{6,12},{8,10},{10,16},{12,14},{14,20},{16,18},{1... | collective-permute-start | bytes 786440 | tf_op jit(solution)/shard_map/ppermute | solution.py:306
  19.6 9.6 %collective-permute-start.3 = (bf16[2,2,2,128,128]{4,3,2,1,0:T(8,128)(2,1)S(1)}, bf16[2,2,2,128,128]{4,3,2,1,0:T(8,128)(2,1)S(1)}, u32[]{:S(2)}, u32[]{:S(2)}) collective-permute-start(bf16[2,2,2,128,128]{4,3,2,1,0:T(8,128)(2,1)S(1)} %collective-permute-done.2.refs_2_), channel_id=1, source_target_pairs={{0,2},{2,0},{4,6},{6,4},{8,10},{10,8},{12,14},{14,12},{16,18},{18,... | collective-permute-start | bytes 786440 | tf_op jit(solution)/shard_map/ppermute | solution.py:306
  28.3 2.1 %collective-permute-start.9 = (bf16[2,2,2,128,128]{4,3,2,1,0:T(8,128)(2,1)S(1)}, bf16[2,2,2,128,128]{4,3,2,1,0:T(8,128)(2,1)S(1)}, u32[]{:S(2)}, u32[]{:S(2)}) collective-permute-start(bf16[2,2,2,128,128]{4,3,2,1,0:T(8,128)(2,1)S(1)} %collective-permute-done.8.refs_5_), channel_id=1, source_target_pairs={{0,2},{2,0},{4,6},{6,4},{8,10},{10,8},{12,14},{14,12},{16,18},{18,... | collective-permute-start | bytes 786440 | tf_op jit(solution)/shard_map/ppermute | solution.py:306

commit v5 on v4

v5 whole, which is shorter than its diff:
```python
import functools
import math

import jax
import jax.numpy as jnp
from jax import lax
from jax.experimental import pallas as pl
from jax.experimental.pallas import tpu as pltpu
from jax.sharding import PartitionSpec as P

QUERY_HEADS = 32
KEY_VALUE_HEADS = 4
WIN = 8
LAYER = 4
GROUP = QUERY_HEADS // KEY_VALUE_HEADS
BF16 = jnp.bfloat16
F32 = jnp.float32
VMEM_LIMIT = 20 * 2**20
NEG = -1e30
SPAN = 256
BLOCK = 128
COST = 10**9
PACK_LIMIT = 56 * 2**20


def slot_of(head, per, count):
    return lax.rem(head // per - lax.axis_index("head") + count, count)


def place(outs, head, per, at, x):
    for d in range(len(outs)):

        @pl.when(slot_of(head, per, len(outs)) == d)
        def _():
            outs[d][at + (head % per,)] = x


def pack_kv_kernel(k_hbm, v_hbm, *refs):
    outs, (flat, wide, sems) = refs[:-3], refs[-3:]
    rows, heads, width = k_hbm.shape[1:]
    loads = [
        pltpu.make_async_copy(ref.at[0], flat.at[i], sems.at[i])
        for i, ref in enumerate((k_hbm, v_hbm))
    ]
    for load in loads:
        load.start()
    for i in range(2):
        loads[i].wait()
        wide.at[i].reshape(rows, 8, width)[:, :heads, :] = flat[i].astype(F32)
        for head in range(heads):
            x = wide[i, pl.ds(head, rows, stride=8), :].astype(BF16)
            place(outs, head, heads // len(outs), (i,), x)


def pack_kv(keys, values, count):
    rows, heads, width = keys.shape[1:]
    shape = jax.ShapeDtypeStruct((2, heads // count, rows, width), BF16)
    return pl.pallas_call(
        pack_kv_kernel,
        out_shape=(shape,) * count,
        in_specs=[pl.BlockSpec(memory_space=pl.ANY)] * 2,
        out_specs=[pl.BlockSpec(memory_space=pltpu.VMEM)] * count,
        scratch_shapes=[
            pltpu.VMEM((2, rows, heads, width), BF16),
            pltpu.VMEM((2, rows * 8, width), F32),
            pltpu.SemaphoreType.DMA((2,)),
        ],
        compiler_params=pltpu.CompilerParams(vmem_limit_bytes=PACK_LIMIT),
    )(keys, values)


def pack_q_kernel(count, q_ref, own, *away):
    rows, heads, width = q_ref.shape[1:]
    per = heads // GROUP // count
    split = len(away) // max(count - 1, 1)
    for head in range(heads // GROUP):
        x = q_ref[0, :, head * GROUP : (head + 1) * GROUP, :].astype(F32)
        x = x.reshape(rows * GROUP, width).astype(BF16)
        part, g = divmod(head % per, per // split) if away else (0, 0)
        for d in range(count):

            @pl.when(slot_of(head, per, count) == d)
            def _():
                if d:
                    away[(d - 1) * split + part][g] = x
                else:
                    own[head % per] = x


def pack_q(queries, count, split):
    rows, heads, width = queries.shape[1:]
    per = heads // GROUP // count
    own = jax.ShapeDtypeStruct((per, rows * GROUP, width), BF16)
    away = jax.ShapeDtypeStruct((per // split, rows * GROUP, width), BF16)
    outs = (own,) + (away,) * (split * (count - 1))
    return pl.pallas_call(
        functools.partial(pack_q_kernel, count),
        out_shape=outs,
        in_specs=[pl.BlockSpec(memory_space=pltpu.VMEM)],
        out_specs=[pl.BlockSpec(memory_space=pltpu.VMEM)] * len(outs),
        compiler_params=pltpu.CompilerParams(vmem_limit_bytes=VMEM_LIMIT),
    )(queries)


def start_of(pair, chunk, n, count, rows, pick):
    half = count * rows // 2
    r = chunk * rows
    return pick(r < half, 2 * pair * half + r, (2 * n - 2 - 2 * pair) * half + r)


def step_range(n, count, rows, offsets, begin, small):
    pick = lambda c, x, y: x if c else y
    found = []
    for p in range(n):
        steps = 0
        for chunk in range(count):
            mine = start_of(p, chunk, n, count, rows, pick)
            seen = sum(
                start_of((p - offset(p)) % n, c, n, count, rows, pick) < mine
                for offset in offsets
                for c in range(count)
            )
            seen = max(seen + 1 - small, 0) if begin else seen
            steps += -(-seen // small)
        found.append(steps)
    return min(found), max(found)


def attend_kernel(n, count, parts, offsets, block, begin, end, *refs):
    total = len(offsets) * count
    if begin:
        q_hbm, refs = refs[:count], refs[count:]
    kv_hbm, refs = refs[: len(offsets)], refs[len(offsets) :]
    held = 4 * len(parts)
    if not begin:
        refs = refs[held:]
    if end:
        out_hbm, max_ref, sum_ref = refs[:3]
        refs = refs[3:]
    states = [refs[i : i + 4] for i in range(0, held, 4)]
    kvbuf, order, qsem, ksem, osem = refs[held:]
    per, m_rows, width = states[0][0].shape[1:]
    rows = m_rows // GROUP
    small = SPAN // rows
    p = lax.axis_index("ctx")
    h = lax.axis_index("head")
    factor = math.log2(math.e) / math.sqrt(width)

    loads = []
    if begin:
        mine = q_hbm[0].at[pl.ds(parts[0] * per, per)]
        for s, ref in enumerate([mine, *q_hbm[1:]]):
            loads.append(pltpu.make_async_copy(ref, states[0][0].at[s], qsem.at[s]))
    for i, ref in enumerate(kv_hbm):
        to = kvbuf.at[pl.ds(i * count, count)]
        ref = ref.at[:, :, pl.ds(parts[0] * per, len(parts) * per)]
        loads.append(pltpu.make_async_copy(ref, to, ksem.at[i]))
    for load in loads:
        load.start()

    chunk_of = [lax.rem(h - d + count, count) for d in range(count)]
    starts = []
    for offset in offsets:
        pair = lax.rem(p - offset(p) + n, n)
        starts += [start_of(pair, chunk, n, count, rows, jnp.where) for chunk in chunk_of]
    seen, ends = [], [jnp.int32(0)]
    base = small if begin else 0
    for s in range(count):
        mine = start_of(p, chunk_of[s], n, count, rows, jnp.where)
        found = jnp.int32(0)
        if begin:
            order[s, 0] = s
            found = jnp.int32(1)
        for c in range(total):
            if not begin or c != s:
                order[s, found] = c
                found = found + (starts[c] < mine).astype(jnp.int32)
        again = order[s, jnp.maximum(found - 1, 0)]
        for t in range(small):
            order[s, found + t] = again
        seen.append(found)
        ends.append(ends[-1] + (jnp.maximum(found - base, 0) + small - 1) // small)

    def chunks_at(kind, s, g, at):
        return [kvbuf[order[s, at + t], kind, g] for t in range(small)]

    def one(part, s, g, b, k, v, left, diagonal):
        qbuf, acc, mbuf, lbuf = states[part]
        where = slice(b * block, (b + 1) * block)
        row = b * (block // GROUP)
        acc_at = s, slice(row, row + block // GROUP), slice(g * GROUP, (g + 1) * GROUP)
        score = lax.dot_general(
            qbuf[s, g, where, :], k, (((1,), (1,)), ((), ())), preferred_element_type=F32
        )
        parts = [score[:, t : t + 128] for t in range(0, small * rows, 128)]
        if diagonal:
            shape = (block // GROUP, GROUP, 128)
            col = lax.broadcasted_iota(jnp.int32, shape, 2)
            row = lax.broadcasted_iota(jnp.int32, shape, 0) + row
            for t, x in enumerate(parts):
                x = x.reshape(shape)
                if t * 128 >= rows and rows % 128 == 0:
                    x = jnp.where(t * 128 < left, x, NEG)
                else:
                    ok = col + t * 128 < left
                    if t * 128 < rows:
                        ok &= (col + t * 128 <= row) | (col + t * 128 >= rows)
                    x = jnp.where(ok, x, NEG)
                parts[t] = x.reshape(block, 128)
        top = jnp.max(functools.reduce(jnp.maximum, parts), axis=1, keepdims=True)
        if not diagonal:
            old = mbuf[s, g, where, :]
            top = jnp.maximum(old, top)
        prob = jnp.concatenate(
            [jnp.exp2((x - top) * factor).astype(BF16) for x in parts], axis=1
        )
        got = jnp.dot(prob, v, preferred_element_type=F32)
        gain, mass = got[:, :width], got[:, width:]
        if not diagonal:
            shrink = jnp.exp2((old - top) * factor)
            gain = acc[acc_at].reshape(block, width) * shrink + gain
            mass = lbuf[s, g, where, :] * shrink + mass
        mbuf[s, g, where, :] = jnp.broadcast_to(top, (block, 128))
        lbuf[s, g, where, :] = mass
        acc[acc_at] = gain.reshape(block // GROUP, GROUP, width)

    def run(s, at, found, diagonal):
        left = (found - at) * rows
        for g in range(len(parts) * per):
            k = jnp.concatenate(chunks_at(0, s, g, at), axis=0)
            v = [jnp.concatenate([x, jnp.ones_like(x)], axis=1) for x in chunks_at(1, s, g, at)]
            if not diagonal:
                v[1:] = [
                    jnp.where(t * rows < left, x, jnp.zeros_like(x))
                    for t, x in enumerate(v[1:], 1)
                ]
            v = jnp.concatenate(v, axis=0)
            for b in range(m_rows // block):
                one(g // per, s, g % per, b, k, v, left, diagonal)

    def step(t):
        s, at, found = jnp.int32(0), base + t * small, seen[0]
        for c in range(1, count):
            after = t >= ends[c]
            s = jnp.where(after, c, s)
            at = jnp.where(after, base + (t - ends[c]) * small, at)
            found = jnp.where(after, seen[c], found)
        run(s, at, found, False)

    def to_lanes(x):
        x = x.reshape(rows, GROUP, 128)[:, :, :rows]
        a = lax.broadcasted_iota(jnp.int32, (rows, GROUP, rows), 0)
        b = lax.broadcasted_iota(jnp.int32, (rows, GROUP, rows), 2)
        return jnp.sum(jnp.where(a == b, x, 0.0), axis=0)

    for load in loads:
        load.wait()
    if begin:
        for s in range(count):
            run(s, 0, seen[s], True)
    least, most = step_range(n, count, rows, offsets, begin, small)
    for t in range(least):
        step(t)
    for t in range(least, most):

        @pl.when(t < ends[-1])
        def _():
            step(t)

    if not end:
        return
    saves = []
    heads = per * GROUP
    for i, part in enumerate(parts):
        for s in range(count):
            row0 = pl.multiple_of(chunk_of[s] * rows, rows)
            to = out_hbm.at[0, pl.ds(row0, rows), pl.ds(part * heads, heads)]
            saves.append(pltpu.make_async_copy(states[i][1].at[s], to, osem.at[i, s]))
            saves[-1].start()
    for i, part in enumerate(parts):
        _, _, mbuf, lbuf = states[i]
        for s in range(count):
            for g in range(per):
                tops = to_lanes(mbuf[s, g]) * (1.0 / math.sqrt(width))
                sums = to_lanes(lbuf[s, g])
                at = slice(part * heads + g * GROUP, part * heads + (g + 1) * GROUP)
                for d in range(count):

                    @pl.when(chunk_of[s] == d)
                    def _():
                        max_ref[at, 0, d * rows : (d + 1) * rows] = tops
                        sum_ref[at, 0, d * rows : (d + 1) * rows] = sums
    for save in saves:
        save.wait()


def attend(q_list, kv_list, offsets, parts, split, n, state, end):
    begin = state is None
    count, all_heads, rows, width = kv_list[0].shape[0], *kv_list[0].shape[2:]
    per = all_heads // split
    m_rows = rows * GROUP
    near, away = pl.BlockSpec(memory_space=pltpu.VMEM), pl.BlockSpec(memory_space=pl.ANY)
    held = [
        jax.ShapeDtypeStruct((count, per, m_rows, width), BF16),
        jax.ShapeDtypeStruct((count, rows, per * GROUP, width), F32),
        jax.ShapeDtypeStruct((count, per, m_rows, 128), F32),
        jax.ShapeDtypeStruct((count, per, m_rows, 128), F32),
    ] * len(parts)
    out_shape, out_specs, aliases = [], [], {}
    if end:
        out_shape += [
            jax.ShapeDtypeStruct((1, count * rows, all_heads * GROUP, width), F32),
            jax.ShapeDtypeStruct((all_heads * GROUP, 1, count * rows), F32),
            jax.ShapeDtypeStruct((all_heads * GROUP, 1, count * rows), F32),
        ]
        out_specs += [away, near, near]
    given = len(q_list) + len(kv_list)
    if not begin:
        aliases = {given + i: len(out_shape) + i for i in range(len(held))}
    out_shape += held
    out_specs += [near] * len(held)
    total = len(offsets) * count
    outs = pl.pallas_call(
        functools.partial(
            attend_kernel, n, count, parts, offsets, min(BLOCK, m_rows), begin, end
        ),
        out_shape=out_shape,
        in_specs=[away] * given + [near] * (0 if begin else len(held)),
        out_specs=out_specs,
        input_output_aliases=aliases,
        scratch_shapes=[
            pltpu.VMEM((total, 2, len(parts) * per, rows, width), BF16),
            pltpu.SMEM((count, total + 1 + SPAN // rows), jnp.int32),
            pltpu.SemaphoreType.DMA((count,)),
            pltpu.SemaphoreType.DMA((len(offsets),)),
            pltpu.SemaphoreType.DMA((len(parts), count)),
        ],
        compiler_params=pltpu.CompilerParams(vmem_limit_bytes=VMEM_LIMIT),
        cost_estimate=pl.CostEstimate(
            flops=COST * len(offsets) * len(parts), bytes_accessed=2**20, transcendentals=0
        ),
    )(*q_list, *kv_list, *(state or []))
    return tuple(outs[:3]) if end else outs


def along(block, axis, target):
    size = lax.axis_size(axis)
    return lax.ppermute(block, axis, [(i, target(i) % size) for i in range(size)])


def climb(block, d, layer):
    n, count = lax.axis_size("ctx"), lax.axis_size("head")
    edges = []
    for p in range(n):
        for h in range(count):
            edges.append((p * count + h, (p + layer) % n * count + (h + d) % count))
    return lax.ppermute(block, ("ctx", "head"), edges)


def local(queries, keys, values):
    n = lax.axis_size("ctx")
    count = lax.axis_size("head")
    me = lax.axis_index("ctx")
    swap = lambda x, d: along(x, "head", lambda i: i + d)

    kv = pack_kv(keys, values, count)
    own = [kv[0]] + [swap(kv[d], d) for d in range(1, count)]

    layer = LAYER
    up = jnp.stack([climb(x, d, layer) for d, x in enumerate(kv)])
    split = 2 if own[0].shape[1] % 2 == 0 else 1
    q_own, *q_away = pack_q(queries, count, split)
    q = [
        [q_own] + [swap(q_away[(d - 1) * split + part], d) for d in range(1, count)]
        for part in range(split)
    ]

    both = lax.optimization_barrier(jnp.stack(own))
    side = along(both, "ctx", lambda i: i + layer // 2)
    far = along(up, "ctx", lambda i: i + layer // 2)
    odd = along(up, "ctx", lambda i: i + layer - 1 if i & 1 else i + 1)
    near = jnp.where(lax.rem(me, 2) == 0, both, up)
    near = along(near, "ctx", lambda i: i ^ 1)
    side_c = along(side, "ctx", lambda i: i ^ 1)

    bit = lambda p, even, other: even + (other - even) * (p & 1)
    offsets = [
        lambda p: 0,
        lambda p: layer,
        lambda p: layer + 2,
        lambda p: bit(p, layer + 3, layer + 1),
        lambda p: bit(p, layer + 1, layer + 3),
        lambda p: 2,
        lambda p: bit(p, 3, 1),
        lambda p: bit(p, 1, 3),
    ]
    own_at, up_at, far_at, odd_at, far_c_at, side_at, near_at, side_c_at = offsets
    first = [both, up, near, side], [own_at, up_at, near_at, side_at]
    state = [x for i in range(split) for x in attend(q[i], *first, [i], split, n, None, False)]
    state, far = lax.optimization_barrier((state, far))
    far_c = along(far, "ctx", lambda i: i ^ 1)
    parts = list(range(split))
    state = attend([], [side_c, odd, far], [side_c_at, odd_at, far_at], parts, split, n, state, False)
    return attend([], [far_c], [far_c_at], parts, split, n, state, True)


def solution(mesh):
    in_specs = (
        P("ctx", "head", None, None),
        P("ctx", "head", None, None),
        P("ctx", "head", None, None),
    )
    out_specs = (P("ctx", None, "head", None), P("head", "ctx", None), P("head", "ctx", None))
    return jax.shard_map(local, mesh=mesh, in_specs=in_specs, out_specs=out_specs, check_vma=False)
```

time: 38.2 us -> 35.2 us (0.921)
  the two profiles are of different devices: /device:TPU:1 before, /device:TPU:2 now
where the time goes in v5:
time: 35.2 us; the launch traced here: 35 us
  Pallas kernels  12.9 us (37%)
  starting transfers between devices  9.69 us (28%)
  waiting for transfers between devices  9.54 us (27%)
  local copies, waits for them, and re-layouts  1.22 us (3%)
  other arithmetic  0.97 us (3%)
  between operations  0.72 us (2%)
    pallas_call x4, Pallas kernels, attend(): pl.pallas_call(functools.partial(attend_kernel, n, count, parts, offsets,...  10.7 us
    ppermute x9, waiting for transfers between devices, along(): lax.ppermute(block, axis, [(i, target(i) % size) for i in range(size)])  8.45 us
    ppermute x9, starting transfers between devices, along(): lax.ppermute(block, axis, [(i, target(i) % size) for i in range(size)])  6.6 us
    ppermute x2, starting transfers between devices, climb(): return lax.ppermute(block, ('ctx', 'head'), edges)  3.1 us
    pallas_call x1, Pallas kernels, pack_kv(): pl.pallas_call(pack_kv_kernel, out_shape=(shape,) * count, in_specs=[pl.B...  1.84 us
    unnamed x2, local copies, waits for them, and re-layouts  1.22 us
    ppermute x2, waiting for transfers between devices, climb(): return lax.ppermute(block, ('ctx', 'head'), edges)  1.1 us
    another operation x1, other arithmetic, local(): both = lax.optimization_barrier(jnp.stack(own))  0.93 us
  transfers between devices with their start and end apart: 11, of which 4 were waited for; matrix products, arithmetic and copies ran while one was open for 3% of the time, Pallas kernels for 23%

profile of v5, /device:TPU:2, one launch (start us, length us, event | category | flops | bytes accessed | tf_op | source)
XLA Modules:
  0.0 35.0 jit_solution(192963939702967519)
XLA Ops:
  0.6 1.8 %shard_map.59 = (bf16[2,2,128,128]{3,2,1,0:T(8,128)(2,1)}, bf16[2,2,128,128]{3,2,1,0:T(8,128)(2,1)}) custom-call(bf16[1,128,4,128]{3,2,1,0:T(4,128)(2,1)} %k_hbm.1, bf16[1,128,4,128]{3,2,1,0:T(4,128)(2,1)} %v_hbm.1), custom_call_target="tpu_custom_call" | custom-call | tf_op jit(solution)/shard_map/pallas_call | solution.py:58
  2.5 1.6 %collective-permute-start.1 = (bf16[2,2,128,128]{3,2,1,0:T(8,128)(2,1)}, bf16[2,2,128,128]{3,2,1,0:T(8,128)(2,1)S(1)}, u32[]{:S(2)}, u32[]{:S(2)}) collective-permute-start(bf16[2,2,128,128]{3,2,1,0:T(8,128)(2,1)} %get-tuple-element.39), channel_id=1, source_target_pairs={{0,1},{1,0},{2,3},{3,2},{4,5},{5,4},{6,7},{7,6},{8,9},{9,8},{10,11... | collective-permute-start | bytes 393224 | tf_op jit(solution)/shard_map/ppermute | solution.py:348
  4.1 1.6 %collective-permute-start.2 = (bf16[2,2,128,128]{3,2,1,0:T(8,128)(2,1)}, bf16[2,2,128,128]{3,2,1,0:T(8,128)(2,1)S(1)}, u32[]{:S(2)}, u32[]{:S(2)}) collective-permute-start(bf16[2,2,128,128]{3,2,1,0:T(8,128)(2,1)} %get-tuple-element.38), channel_id=1, source_target_pairs={{0,8},{1,9},{2,10},{3,11},{4,12},{5,13},{6,14},{7,15},{8,16},{9,17... | collective-permute-start | bytes 393224 | tf_op jit(solution)/shard_map/ppermute | solution.py:357
  5.6 1.5 %collective-permute-start.3 = (bf16[2,2,128,128]{3,2,1,0:T(8,128)(2,1)}, bf16[2,2,128,128]{3,2,1,0:T(8,128)(2,1)S(1)}, u32[]{:S(2)}, u32[]{:S(2)}) collective-permute-start(bf16[2,2,128,128]{3,2,1,0:T(8,128)(2,1)} %get-tuple-element.39), channel_id=1, source_target_pairs={{0,9},{1,8},{2,11},{3,10},{4,13},{5,12},{6,15},{7,14},{8,17},{9,16... | collective-permute-start | bytes 393224 | tf_op jit(solution)/shard_map/ppermute | solution.py:357
  7.2 0.0 copy-start
  7.2 1.2 %copy-done = bf16[1,128,32,128]{3,2,1,0:T(8,128)(2,1)S(1)} copy-done((bf16[1,128,32,128]{3,2,1,0:T(8,128)(2,1)S(1)}, bf16[1,128,32,128]{3,2,1,0:T(8,128)(2,1)}, u32[]{:S(2)}) %copy-start) | copy-done | bytes 1048600
  8.4 0.3 shard_map.58
  8.7 1.6 %collective-permute-start.6 = (bf16[1,1024,128]{2,1,0:T(8,128)(2,1)S(1)}, bf16[1,1024,128]{2,1,0:T(8,128)(2,1)S(1)}, u32[]{:S(2)}, u32[]{:S(2)}) collective-permute-start(bf16[1,1024,128]{2,1,0:T(8,128)(2,1)S(1)} %get-tuple-element.44), channel_id=1, source_target_pairs={{0,1},{1,0},{2,3},{3,2},{4,5},{5,4},{6,7},{7,6},{8,9},{9,8},{10,11... | collective-permute-start | bytes 786440 | tf_op jit(solution)/shard_map/ppermute | solution.py:348
  10.3 0.0 collective-permute-done.1
  10.3 0.9 %pad_maximum_fusion.refs_2_ = bf16[2,2,2,128,128]{4,3,2,1,0:T(8,128)(2,1)S(1)} fusion(bf16[1,2,2,128,128]{4,3,2,1,0:T(8,128)(2,1)S(1)} %bitcast.5, bf16[1,2,2,128,128]{4,3,2,1,0:T(8,128)(2,1)} %bitcast.4), kind=kLoop, calls=%fused_computation | loop fusion | flops 131072 | bytes 524288 | tf_op jit(solution)/shard_map/stack | solution.py:378
  11.2 1.6 %collective-permute-start.5 = (bf16[2,2,2,128,128]{4,3,2,1,0:T(8,128)(2,1)S(1)}, bf16[2,2,2,128,128]{4,3,2,1,0:T(8,128)(2,1)S(1)}, u32[]{:S(2)}, u32[]{:S(2)}) collective-permute-start(bf16[2,2,2,128,128]{4,3,2,1,0:T(8,128)(2,1)S(1)} %pad_maximum_fusion.refs_2_), channel_id=1, source_target_pairs={{0,4},{2,6},{4,8},{6,10},{8,12},{10,14},{12,16},{14,18},{16,20},{1... | collective-permute-start | bytes 786440 | tf_op jit(solution)/shard_map/ppermute | solution.py:348
  12.8 0.0 collective-permute-done.2
  12.8 1.1 %collective-permute-done.3 = bf16[2,2,128,128]{3,2,1,0:T(8,128)(2,1)S(1)} collective-permute-done((bf16[2,2,128,128]{3,2,1,0:T(8,128)(2,1)}, bf16[2,2,128,128]{3,2,1,0:T(8,128)(2,1)S(1)}, u32[]{:S(2)}, u32[]{:S(2)}) %collective-permute-start.3) | collective-permute-done | bytes 131104 | tf_op jit(solution)/shard_map/ppermute | solution.py:357
  13.9 0.1 collective-permute-start.4
  14.0 1.6 %collective-permute-start = (bf16[1,1024,128]{2,1,0:T(8,128)(2,1)S(1)}, bf16[1,1024,128]{2,1,0:T(8,128)(2,1)S(1)}, u32[]{:S(2)}, u32[]{:S(2)}) collective-permute-start(bf16[1,1024,128]{2,1,0:T(8,128)(2,1)S(1)} %get-tuple-element.37), channel_id=1, source_target_pairs={{0,1},{1,0},{2,3},{3,2},{4,5},{5,4},{6,7},{7,6},{8,9},{9,8},{10,11... | collective-permute-start | bytes 786440 | tf_op jit(solution)/shard_map/ppermute | solution.py:348
  15.7 0.0 collective-permute-start.7
  15.7 3.9 %collective-permute-done.6.refs_1_ = bf16[1,1024,128]{2,1,0:T(8,128)(2,1)S(1)} collective-permute-done((bf16[1,1024,128]{2,1,0:T(8,128)(2,1)S(1)}, bf16[1,1024,128]{2,1,0:T(8,128)(2,1)S(1)}, u32[]{:S(2)}, u32[]{:S(2)}) %collective-permute-start.6) | collective-permute-done | bytes 262176 | tf_op jit(solution)/shard_map/ppermute | solution.py:348
  19.6 0.0 collective-permute-start.10
  19.6 0.0 collective-permute-done.5.refs_5_
  19.6 0.0 collective-permute-start.9
  19.6 0.0 collective-permute-done.4.refs_4_
  19.6 2.2 %shard_map.61 = (bf16[2,1,1024,128]{3,2,1,0:T(8,128)(2,1)S(1)}, f32[2,128,8,128]{3,2,1,0:T(8,128)S(1)}, f32[2,1,1024,128]{3,2,1,0:T(8,128)S(1)}, f32[2,1,1024,128]{3,2,1,0:T(8,128)S(1)}) custom-call(bf16[2,1024,128]{2,1,0:T(8,128)(2,1)S(1)} %get-tuple-element.36.refs_0_, bf16[1,1024,128]{2,1,0:T(8,128)(2,1)S(1)} %collective-permute-done.6.refs_1_, ...), custom_call_target="tpu_custom_call" | custom-call | flops 4000000000 | bytes 1048576 | tf_op jit(solution)/shard_map/pallas_call | solution.py:323
  21.8 2.6 %collective-permute-done.refs_1_ = bf16[1,1024,128]{2,1,0:T(8,128)(2,1)S(1)} collective-permute-done((bf16[1,1024,128]{2,1,0:T(8,128)(2,1)S(1)}, bf16[1,1024,128]{2,1,0:T(8,128)(2,1)S(1)}, u32[]{:S(2)}, u32[]{:S(2)}) %collective-permute-start) | collective-permute-done | bytes 262176 | tf_op jit(solution)/shard_map/ppermute | solution.py:348
  24.4 2.2 %shard_map.60 = (bf16[2,1,1024,128]{3,2,1,0:T(8,128)(2,1)S(1)}, f32[2,128,8,128]{3,2,1,0:T(8,128)S(1)}, f32[2,1,1024,128]{3,2,1,0:T(8,128)S(1)}, f32[2,1,1024,128]{3,2,1,0:T(8,128)S(1)}) custom-call(bf16[2,1024,128]{2,1,0:T(8,128)(2,1)S(1)} %get-tuple-element.36.refs_0_, bf16[1,1024,128]{2,1,0:T(8,128)(2,1)S(1)} %collective-permute-done.refs_1_, ...), custom_call_target="tpu_custom_call" | custom-call | flops 4000000000 | bytes 1048576 | tf_op jit(solution)/shard_map/pallas_call | solution.py:323
  26.6 0.0 collective-permute-done.7.refs_2_
  26.6 0.1 collective-permute-start.8
  26.7 2.0 %collective-permute-done.10.refs_1_ = bf16[2,2,2,128,128]{4,3,2,1,0:T(8,128)(2,1)S(1)} collective-permute-done((bf16[2,2,2,128,128]{4,3,2,1,0:T(8,128)(2,1)S(1)}, bf16[2,2,2,128,128]{4,3,2,1,0:T(8,128)(2,1)S(1)}, u32[]{:S(2)}, u32[]{:S(2)}) %collective-permute-start.10) | collective-permute-done | bytes 262176 | tf_op jit(solution)/shard_map/ppermute | solution.py:348
  28.6 0.0 collective-permute-done.9.refs_0_
  28.6 3.4 %shard_map.62 = (bf16[2,1,1024,128]{3,2,1,0:T(8,128)(2,1)S(1)}, f32[2,128,8,128]{3,2,1,0:T(8,128)S(1)}, f32[2,1,1024,128]{3,2,1,0:T(8,128)S(1)}, f32[2,1,1024,12...) custom-call(bf16[2,2,2,128,128]{4,3,2,1,0:T(8,128)(2,1)S(1)} %collec, ...), custom_call_target="tpu_custom_call", output_to_operand_aliasing={{0}: (3, {}), {1}: (4, {}), {2}: (5, {}), {3}: (6, {}), {4}... | custom-call | flops 6000000000 | bytes 1048576 | tf_op jit(solution)/shard_map/pallas_call | solution.py:323
  32.0 0.0 collective-permute-done.8.refs_0_
  32.0 3.0 %shard_map.63 = (f32[1,256,16,128]{3,2,1,0:T(8,128)}, f32[16,1,256]{2,1,0:T(1,128)}, f32[16,1,256]{2,1,0:T(1,128)}, bf16[2,1,1024,128]{3,2,1,0:T(8,128)(2,1)S(1)...) custom-call(bf16[2,2,2,128,128]{4,3,2,1,0:T(8,128)(2,1)S(1)} %collec, ...), custom_call_target="tpu_custom_call", output_to_operand_aliasing={{3}: (1, {}), {4}: (2, {}), {5}: (3, {}), {6}: (4, {}), {7}... | custom-call | flops 2000000000 | bytes 1048576 | tf_op jit(solution)/shard_map/pallas_call | solution.py:323
  (1 shorter events, 0.0 us)
Async XLA Ops:
  2.5 7.8 %collective-permute-start.1 = (bf16[2,2,128,128]{3,2,1,0:T(8,128)(2,1)}, bf16[2,2,128,128]{3,2,1,0:T(8,128)(2,1)S(1)}, u32[]{:S(2)}, u32[]{:S(2)}) collective-permute-start(bf16[2,2,128,128]{3,2,1,0:T(8,128)(2,1)} %get-tuple-element.39), channel_id=1, source_target_pairs={{0,1},{1,0},{2,3},{3,2},{4,5},{5,4},{6,7},{7,6},{8,9},{9,8},{10,11... | collective-permute-start | bytes 393224 | tf_op jit(solution)/shard_map/ppermute | solution.py:348
  4.1 8.7 %collective-permute-start.2 = (bf16[2,2,128,128]{3,2,1,0:T(8,128)(2,1)}, bf16[2,2,128,128]{3,2,1,0:T(8,128)(2,1)S(1)}, u32[]{:S(2)}, u32[]{:S(2)}) collective-permute-start(bf16[2,2,128,128]{3,2,1,0:T(8,128)(2,1)} %get-tuple-element.38), channel_id=1, source_target_pairs={{0,8},{1,9},{2,10},{3,11},{4,12},{5,13},{6,14},{7,15},{8,16},{9,17... | collective-permute-start | bytes 393224 | tf_op jit(solution)/shard_map/ppermute | solution.py:357
  5.6 8.3 %collective-permute-start.3 = (bf16[2,2,128,128]{3,2,1,0:T(8,128)(2,1)}, bf16[2,2,128,128]{3,2,1,0:T(8,128)(2,1)S(1)}, u32[]{:S(2)}, u32[]{:S(2)}) collective-permute-start(bf16[2,2,128,128]{3,2,1,0:T(8,128)(2,1)} %get-tuple-element.39), channel_id=1, source_target_pairs={{0,9},{1,8},{2,11},{3,10},{4,13},{5,12},{6,15},{7,14},{8,17},{9,16... | collective-permute-start | bytes 393224 | tf_op jit(solution)/shard_map/ppermute | solution.py:357
  7.2 1.2 %copy-start = (bf16[1,128,32,128]{3,2,1,0:T(8,128)(2,1)S(1)}, bf16[1,128,32,128]{3,2,1,0:T(8,128)(2,1)}, u32[]{:S(2)}) copy-start(bf16[1,128,32,128]{3,2,1,0:T(8,128)(2,1)} %q_ref.1) | copy-start | bytes 3145732
  8.7 10.9 %collective-permute-start.6 = (bf16[1,1024,128]{2,1,0:T(8,128)(2,1)S(1)}, bf16[1,1024,128]{2,1,0:T(8,128)(2,1)S(1)}, u32[]{:S(2)}, u32[]{:S(2)}) collective-permute-start(bf16[1,1024,128]{2,1,0:T(8,128)(2,1)S(1)} %get-tuple-element.44), channel_id=1, source_target_pairs={{0,1},{1,0},{2,3},{3,2},{4,5},{5,4},{6,7},{7,6},{8,9},{9,8},{10,11... | collective-permute-start | bytes 786440 | tf_op jit(solution)/shard_map/ppermute | solution.py:348
  11.2 8.4 %collective-permute-start.5 = (bf16[2,2,2,128,128]{4,3,2,1,0:T(8,128)(2,1)S(1)}, bf16[2,2,2,128,128]{4,3,2,1,0:T(8,128)(2,1)S(1)}, u32[]{:S(2)}, u32[]{:S(2)}) collective-permute-start(bf16[2,2,2,128,128]{4,3,2,1,0:T(8,128)(2,1)S(1)} %pad_maximum_fusion.refs_2_), channel_id=1, source_target_pairs={{0,4},{2,6},{4,8},{6,10},{8,12},{10,14},{12,16},{14,18},{16,20},{1... | collective-permute-start | bytes 786440 | tf_op jit(solution)/shard_map/ppermute | solution.py:348
  13.9 5.7 %collective-permute-start.4 = (bf16[2,2,2,128,128]{4,3,2,1,0:T(8,128)(2,1)S(1)}, bf16[2,2,2,128,128]{4,3,2,1,0:T(8,128)(2,1)S(1)}, u32[]{:S(2)}, u32[]{:S(2)}) collective-permute-start(bf16[2,2,2,128,128]{4,3,2,1,0:T(8,128)(2,1)S(1)} %get-tuple-element.69), channel_id=1, source_target_pairs={{0,2},{2,0},{4,6},{6,4},{8,10},{10,8},{12,14},{14,12},{16,18},{18,... | collective-permute-start | bytes 786440 | tf_op jit(solution)/shard_map/ppermute | solution.py:348
  14.0 10.4 %collective-permute-start = (bf16[1,1024,128]{2,1,0:T(8,128)(2,1)S(1)}, bf16[1,1024,128]{2,1,0:T(8,128)(2,1)S(1)}, u32[]{:S(2)}, u32[]{:S(2)}) collective-permute-start(bf16[1,1024,128]{2,1,0:T(8,128)(2,1)S(1)} %get-tuple-element.37), channel_id=1, source_target_pairs={{0,1},{1,0},{2,3},{3,2},{4,5},{5,4},{6,7},{7,6},{8,9},{9,8},{10,11... | collective-permute-start | bytes 786440 | tf_op jit(solution)/shard_map/ppermute | solution.py:348
  15.7 10.9 %collective-permute-start.7 = (bf16[2,2,2,128,128]{4,3,2,1,0:T(8,128)(2,1)S(1)}, bf16[2,2,2,128,128]{4,3,2,1,0:T(8,128)(2,1)S(1)}, u32[]{:S(2)}, u32[]{:S(2)}) collective-permute-start(bf16[2,2,2,128,128]{4,3,2,1,0:T(8,128)(2,1)S(1)} %get-tuple-element.70.refs_3_), channel_id=1, source_target_pairs={{0,4},{2,6},{4,8},{6,10},{8,12},{10,14},{12,16},{14,18},{16,20},{1... | collective-permute-start | bytes 786440 | tf_op jit(solution)/shard_map/ppermute | solution.py:348
  19.6 9.0 %collective-permute-start.10 = (bf16[2,2,2,128,128]{4,3,2,1,0:T(8,128)(2,1)S(1)}, bf16[2,2,2,128,128]{4,3,2,1,0:T(8,128)(2,1)S(1)}, u32[]{:S(2)}, u32[]{:S(2)}) collective-permute-start(bf16[2,2,2,128,128]{4,3,2,1,0:T(8,128)(2,1)S(1)} %get-tuple-element.70.refs_3_), channel_id=1, source_target_pairs={{0,2},{2,8},{4,6},{6,12},{8,10},{10,16},{12,14},{14,20},{16,18},{1... | collective-permute-start | bytes 786440 | tf_op jit(solution)/shard_map/ppermute | solution.py:348
  19.6 9.0 %collective-permute-start.9 = (bf16[2,2,2,128,128]{4,3,2,1,0:T(8,128)(2,1)S(1)}, bf16[2,2,2,128,128]{4,3,2,1,0:T(8,128)(2,1)S(1)}, u32[]{:S(2)}, u32[]{:S(2)}) collective-permute-start(bf16[2,2,2,128,128]{4,3,2,1,0:T(8,128)(2,1)S(1)} %collective-permute-done.5.refs_5_), channel_id=1, source_target_pairs={{0,2},{2,0},{4,6},{6,4},{8,10},{10,8},{12,14},{14,12},{16,18},{18,... | collective-permute-start | bytes 786440 | tf_op jit(solution)/shard_map/ppermute | solution.py:348
  26.6 5.4 %collective-permute-start.8 = (bf16[2,2,2,128,128]{4,3,2,1,0:T(8,128)(2,1)S(1)}, bf16[2,2,2,128,128]{4,3,2,1,0:T(8,128)(2,1)S(1)}, u32[]{:S(2)}, u32[]{:S(2)}) collective-permute-start(bf16[2,2,2,128,128]{4,3,2,1,0:T(8,128)(2,1)S(1)} %collective-permute-done.7.refs_2_), channel_id=1, source_target_pairs={{0,2},{2,0},{4,6},{6,4},{8,10},{10,8},{12,14},{14,12},{16,18},{18,... | collective-permute-start | bytes 786440 | tf_op jit(solution)/shard_map/ppermute | solution.py:348

commit v6 on v5

--- a/solution.py
+++ b/solution.py
@@ -135,10 +135,10 @@
     if not begin:
         refs = refs[held:]
     if end:
-        out_hbm, max_ref, sum_ref = refs[:3]
+        out_hbm, max_hbm, sum_hbm = refs[:3]
         refs = refs[3:]
     states = [refs[i : i + 4] for i in range(0, held, 4)]
-    kvbuf, order, qsem, ksem, osem = refs[held:]
+    kvbuf, tops_buf, sums_buf, order, qsem, ksem, osem = refs[held:]
     per, m_rows, width = states[0][0].shape[1:]
     rows = m_rows // GROUP
     small = SPAN // rows
@@ -247,12 +247,6 @@
             found = jnp.where(after, seen[c], found)
         run(s, at, found, False)
 
-    def to_lanes(x):
-        x = x.reshape(rows, GROUP, 128)[:, :, :rows]
-        a = lax.broadcasted_iota(jnp.int32, (rows, GROUP, rows), 0)
-        b = lax.broadcasted_iota(jnp.int32, (rows, GROUP, rows), 2)
-        return jnp.sum(jnp.where(a == b, x, 0.0), axis=0)
-
     for load in loads:
         load.wait()
     if begin:
@@ -271,25 +265,32 @@
         return
     saves = []
     heads = per * GROUP
-    for i, part in enumerate(parts):
-        for s in range(count):
-            row0 = pl.multiple_of(chunk_of[s] * rows, rows)
+    for s in range(count):
+        row0 = pl.multiple_of(chunk_of[s] * rows, rows)
+        for i, part in enumerate(parts):
             to = out_hbm.at[0, pl.ds(row0, rows), pl.ds(part * heads, heads)]
             saves.append(pltpu.make_async_copy(states[i][1].at[s], to, osem.at[i, s]))
             saves[-1].start()
-    for i, part in enumerate(parts):
-        _, _, mbuf, lbuf = states[i]
-        for s in range(count):
-            for g in range(per):
-                tops = to_lanes(mbuf[s, g]) * (1.0 / math.sqrt(width))
-                sums = to_lanes(lbuf[s, g])
-                at = slice(part * heads + g * GROUP, part * heads + (g + 1) * GROUP)
-                for d in range(count):
-
-                    @pl.when(chunk_of[s] == d)
-                    def _():
-                        max_ref[at, 0, d * rows : (d + 1) * rows] = tops
-                        sum_ref[at, 0, d * rows : (d + 1) * rows] = sums
+
+    lane = lax.broadcasted_iota(jnp.int32, (GROUP, 128), 1)
+    for s in range(count):
+        picked = [jnp.zeros((GROUP, 128), F32)] * (2 * len(parts) * per)
+        for r in range(rows):
+            at = slice(r * GROUP, (r + 1) * GROUP)
+            found = [states[i][j][s, g, at, :] for i in range(len(parts)) for g in range(per) for j in (2, 3)]
+            picked = [jnp.where(lane == r, x, old) for x, old in zip(found, picked)]
+        tops = jnp.concatenate(picked[0::2], axis=0)[:, :rows] * (1.0 / math.sqrt(width))
+        sums = jnp.concatenate(picked[1::2], axis=0)[:, :rows]
+        for d in range(count):
+
+            @pl.when(chunk_of[s] == d)
+            def _():
+                tops_buf[:, 0, d * rows : (d + 1) * rows] = tops
+                sums_buf[:, 0, d * rows : (d + 1) * rows] = sums
+    saves.append(pltpu.make_async_copy(tops_buf, max_hbm, qsem.at[0]))
+    saves.append(pltpu.make_async_copy(sums_buf, sum_hbm, ksem.at[0]))
+    for save in saves[-2:]:
+        save.start()
     for save in saves:
         save.wait()
 
@@ -313,7 +314,7 @@
             jax.ShapeDtypeStruct((all_heads * GROUP, 1, count * rows), F32),
             jax.ShapeDtypeStruct((all_heads * GROUP, 1, count * rows), F32),
         ]
-        out_specs += [away, near, near]
+        out_specs += [away] * 3
     given = len(q_list) + len(kv_list)
     if not begin:
         aliases = {given + i: len(out_shape) + i for i in range(len(held))}
@@ -330,6 +331,8 @@
         input_output_aliases=aliases,
         scratch_shapes=[
             pltpu.VMEM((total, 2, len(parts) * per, rows, width), BF16),
+            pltpu.VMEM((all_heads * GROUP, 1, count * rows), F32),
+            pltpu.VMEM((all_heads * GROUP, 1, count * rows), F32),
             pltpu.SMEM((count, total + 1 + SPAN // rows), jnp.int32),
             pltpu.SemaphoreType.DMA((count,)),
             pltpu.SemaphoreType.DMA((len(offsets),)),
@@ -400,8 +403,8 @@
     state, far = lax.optimization_barrier((state, far))
     far_c = along(far, "ctx", lambda i: i ^ 1)
     parts = list(range(split))
-    state = attend([], [side_c, odd, far], [side_c_at, odd_at, far_at], parts, split, n, state, False)
-    return attend([], [far_c], [far_c_at], parts, split, n, state, True)
+    state = attend([], [side_c, far], [side_c_at, far_at], parts, split, n, state, False)
+    return attend([], [odd, far_c], [odd_at, far_c_at], parts, split, n, state, True)
 
 
 def solution(mesh):

time: 35.2 us -> 34 us (0.966)
  the two profiles are of different devices: /device:TPU:2 before, /device:TPU:1 now
where the time goes in v6:
time: 34 us; the launch traced here: 33.9 us
  starting transfers between devices  16.7 us (49%)
  Pallas kernels  11.3 us (33%)
  waiting for transfers between devices  2.92 us (9%)
  local copies, waits for them, and re-layouts  1.22 us (4%)
  other arithmetic  0.97 us (3%)
  between operations  0.7 us (2%)
    ppermute x9, starting transfers between devices, along(): lax.ppermute(block, axis, [(i, target(i) % size) for i in range(size)])  14.2 us
    pallas_call x4, Pallas kernels, attend(): pl.pallas_call(functools.partial(attend_kernel, n, count, parts, offsets,...  9.18 us
    ppermute x2, starting transfers between devices, climb(): return lax.ppermute(block, ('ctx', 'head'), edges)  2.54 us
    pallas_call x1, Pallas kernels, pack_kv(): pl.pallas_call(pack_kv_kernel, out_shape=(shape,) * count, in_specs=[pl.B...  1.84 us
    ppermute x2, waiting for transfers between devices, climb(): return lax.ppermute(block, ('ctx', 'head'), edges)  1.63 us
    ppermute x9, waiting for transfers between devices, along(): lax.ppermute(block, axis, [(i, target(i) % size) for i in range(size)])  1.29 us
    unnamed x2, local copies, waits for them, and re-layouts  1.22 us
    another operation x1, other arithmetic, local(): both = lax.optimization_barrier(jnp.stack(own))  0.93 us
  transfers between devices with their start and end apart: 11, of which 3 were waited for; matrix products, arithmetic and copies ran while one was open for 3% of the time, Pallas kernels for 19%

profile of v6, /device:TPU:1, one launch (start us, length us, event | category | flops | bytes accessed | tf_op | source)
XLA Modules:
  0.0 33.9 jit_solution(1839185486755782729)
XLA Ops:
  0.6 1.8 %shard_map.58 = (bf16[2,2,128,128]{3,2,1,0:T(8,128)(2,1)}, bf16[2,2,128,128]{3,2,1,0:T(8,128)(2,1)}) custom-call(bf16[1,128,4,128]{3,2,1,0:T(4,128)(2,1)} %k_hbm.1, bf16[1,128,4,128]{3,2,1,0:T(4,128)(2,1)} %v_hbm.1), custom_call_target="tpu_custom_call" | custom-call | tf_op jit(solution)/shard_map/pallas_call | solution.py:58
  2.5 2.1 %collective-permute-start.4 = (bf16[2,2,128,128]{3,2,1,0:T(8,128)(2,1)}, bf16[2,2,128,128]{3,2,1,0:T(8,128)(2,1)S(1)}, u32[]{:S(2)}, u32[]{:S(2)}) collective-permute-start(bf16[2,2,128,128]{3,2,1,0:T(8,128)(2,1)} %get-tuple-element.37), channel_id=1, source_target_pairs={{0,1},{1,0},{2,3},{3,2},{4,5},{5,4},{6,7},{7,6},{8,9},{9,8},{10,11... | collective-permute-start | bytes 393224 | tf_op jit(solution)/shard_map/ppermute | solution.py:351
  4.6 1.3 %collective-permute-start = (bf16[2,2,128,128]{3,2,1,0:T(8,128)(2,1)}, bf16[2,2,128,128]{3,2,1,0:T(8,128)(2,1)S(1)}, u32[]{:S(2)}, u32[]{:S(2)}) collective-permute-start(bf16[2,2,128,128]{3,2,1,0:T(8,128)(2,1)} %get-tuple-element.36), channel_id=1, source_target_pairs={{0,8},{1,9},{2,10},{3,11},{4,12},{5,13},{6,14},{7,15},{8,16},{9,17... | collective-permute-start | bytes 393224 | tf_op jit(solution)/shard_map/ppermute | solution.py:360
  5.9 1.2 %collective-permute-start.1 = (bf16[2,2,128,128]{3,2,1,0:T(8,128)(2,1)}, bf16[2,2,128,128]{3,2,1,0:T(8,128)(2,1)S(1)}, u32[]{:S(2)}, u32[]{:S(2)}) collective-permute-start(bf16[2,2,128,128]{3,2,1,0:T(8,128)(2,1)} %get-tuple-element.37), channel_id=1, source_target_pairs={{0,9},{1,8},{2,11},{3,10},{4,13},{5,12},{6,15},{7,14},{8,17},{9,16... | collective-permute-start | bytes 393224 | tf_op jit(solution)/shard_map/ppermute | solution.py:360
  7.1 0.0 copy-start
  7.2 1.2 %copy-done = bf16[1,128,32,128]{3,2,1,0:T(8,128)(2,1)S(1)} copy-done((bf16[1,128,32,128]{3,2,1,0:T(8,128)(2,1)S(1)}, bf16[1,128,32,128]{3,2,1,0:T(8,128)(2,1)}, u32[]{:S(2)}) %copy-start) | copy-done | bytes 1048600
  8.4 0.3 shard_map.59
  8.7 1.3 %collective-permute-start.7 = (bf16[1,1024,128]{2,1,0:T(8,128)(2,1)S(1)}, bf16[1,1024,128]{2,1,0:T(8,128)(2,1)S(1)}, u32[]{:S(2)}, u32[]{:S(2)}) collective-permute-start(bf16[1,1024,128]{2,1,0:T(8,128)(2,1)S(1)} %get-tuple-element.44), channel_id=1, source_target_pairs={{0,1},{1,0},{2,3},{3,2},{4,5},{5,4},{6,7},{7,6},{8,9},{9,8},{10,11... | collective-permute-start | bytes 786440 | tf_op jit(solution)/shard_map/ppermute | solution.py:351
  10.0 0.0 collective-permute-done.4
  10.0 0.9 %pad_maximum_fusion.1.refs_2_ = bf16[2,2,2,128,128]{4,3,2,1,0:T(8,128)(2,1)S(1)} fusion(bf16[1,2,2,128,128]{4,3,2,1,0:T(8,128)(2,1)S(1)} %bitcast.5, bf16[1,2,2,128,128]{4,3,2,1,0:T(8,128)(2,1)} %bitcast.4), kind=kLoop, calls=%fused_computation.1 | loop fusion | flops 131072 | bytes 524288 | tf_op jit(solution)/shard_map/stack | solution.py:381
  10.9 1.3 %collective-permute-start.6 = (bf16[2,2,2,128,128]{4,3,2,1,0:T(8,128)(2,1)S(1)}, bf16[2,2,2,128,128]{4,3,2,1,0:T(8,128)(2,1)S(1)}, u32[]{:S(2)}, u32[]{:S(2)}) collective-permute-start(bf16[2,2,2,128,128]{4,3,2,1,0:T(8,128)(2,1)S(1)} %pad_maximum_fusion.1.refs_2_), channel_id=1, source_target_pairs={{0,4},{2,6},{4,8},{6,10},{8,12},{10,14},{12,16},{14,18},{16,20},{1... | collective-permute-start | bytes 786440 | tf_op jit(solution)/shard_map/ppermute | solution.py:351
  12.2 0.0 collective-permute-done
  12.2 1.6 %collective-permute-done.1 = bf16[2,2,128,128]{3,2,1,0:T(8,128)(2,1)S(1)} collective-permute-done((bf16[2,2,128,128]{3,2,1,0:T(8,128)(2,1)}, bf16[2,2,128,128]{3,2,1,0:T(8,128)(2,1)S(1)}, u32[]{:S(2)}, u32[]{:S(2)}) %collective-permute-start.1) | collective-permute-done | bytes 131104 | tf_op jit(solution)/shard_map/ppermute | solution.py:360
  13.8 1.7 %collective-permute-start.5 = (bf16[2,2,2,128,128]{4,3,2,1,0:T(8,128)(2,1)S(1)}, bf16[2,2,2,128,128]{4,3,2,1,0:T(8,128)(2,1)S(1)}, u32[]{:S(2)}, u32[]{:S(2)}) collective-permute-start(bf16[2,2,2,128,128]{4,3,2,1,0:T(8,128)(2,1)S(1)} %get-tuple-element.69), channel_id=1, source_target_pairs={{0,2},{2,0},{4,6},{6,4},{8,10},{10,8},{12,14},{14,12},{16,18},{18,... | collective-permute-start | bytes 786440 | tf_op jit(solution)/shard_map/ppermute | solution.py:351
  15.6 1.3 %collective-permute-start.3 = (bf16[1,1024,128]{2,1,0:T(8,128)(2,1)S(1)}, bf16[1,1024,128]{2,1,0:T(8,128)(2,1)S(1)}, u32[]{:S(2)}, u32[]{:S(2)}) collective-permute-start(bf16[1,1024,128]{2,1,0:T(8,128)(2,1)S(1)} %get-tuple-element.39), channel_id=1, source_target_pairs={{0,1},{1,0},{2,3},{3,2},{4,5},{5,4},{6,7},{7,6},{8,9},{9,8},{10,11... | collective-permute-start | bytes 786440 | tf_op jit(solution)/shard_map/ppermute | solution.py:351
  16.8 1.2 %collective-permute-start.8 = (bf16[2,2,2,128,128]{4,3,2,1,0:T(8,128)(2,1)S(1)}, bf16[2,2,2,128,128]{4,3,2,1,0:T(8,128)(2,1)S(1)}, u32[]{:S(2)}, u32[]{:S(2)}) collective-permute-start(bf16[2,2,2,128,128]{4,3,2,1,0:T(8,128)(2,1)S(1)} %get-tuple-element.70.refs_3_), channel_id=1, source_target_pairs={{0,4},{2,6},{4,8},{6,10},{8,12},{10,14},{12,16},{14,18},{16,20},{1... | collective-permute-start | bytes 786440 | tf_op jit(solution)/shard_map/ppermute | solution.py:351
  18.0 1.0 %collective-permute-done.7.refs_1_ = bf16[1,1024,128]{2,1,0:T(8,128)(2,1)S(1)} collective-permute-done((bf16[1,1024,128]{2,1,0:T(8,128)(2,1)S(1)}, bf16[1,1024,128]{2,1,0:T(8,128)(2,1)S(1)}, u32[]{:S(2)}, u32[]{:S(2)}) %collective-permute-start.7) | collective-permute-done | bytes 262176 | tf_op jit(solution)/shard_map/ppermute | solution.py:351
  19.0 1.6 %collective-permute-start.2 = (bf16[2,2,2,128,128]{4,3,2,1,0:T(8,128)(2,1)S(1)}, bf16[2,2,2,128,128]{4,3,2,1,0:T(8,128)(2,1)S(1)}, u32[]{:S(2)}, u32[]{:S(2)}) collective-permute-start(bf16[2,2,2,128,128]{4,3,2,1,0:T(8,128)(2,1)S(1)} %get-tuple-element.70.refs_3_), channel_id=1, source_target_pairs={{0,2},{2,8},{4,6},{6,12},{8,10},{10,16},{12,14},{14,20},{16,18},{1... | collective-permute-start | bytes 786440 | tf_op jit(solution)/shard_map/ppermute | solution.py:351
  20.6 0.0 collective-permute-done.6.refs_5_
  20.6 1.8 %collective-permute-start.10 = (bf16[2,2,2,128,128]{4,3,2,1,0:T(8,128)(2,1)S(1)}, bf16[2,2,2,128,128]{4,3,2,1,0:T(8,128)(2,1)S(1)}, u32[]{:S(2)}, u32[]{:S(2)}) collective-permute-start(bf16[2,2,2,128,128]{4,3,2,1,0:T(8,128)(2,1)S(1)} %collective-permute-done.6.refs_5_), channel_id=1, source_target_pairs={{0,2},{2,0},{4,6},{6,4},{8,10},{10,8},{12,14},{14,12},{16,18},{18,... | collective-permute-start | bytes 786440 | tf_op jit(solution)/shard_map/ppermute | solution.py:351
  22.4 0.0 collective-permute-done.5.refs_4_
  22.4 2.2 %shard_map.61 = (bf16[2,1,1024,128]{3,2,1,0:T(8,128)(2,1)S(1)}, f32[2,128,8,128]{3,2,1,0:T(8,128)S(1)}, f32[2,1,1024,128]{3,2,1,0:T(8,128)S(1)}, f32[2,1,1024,128]{3,2,1,0:T(8,128)S(1)}) custom-call(bf16[2,1024,128]{2,1,0:T(8,128)(2,1)S(1)} %get-tuple-element.38.refs_0_, bf16[1,1024,128]{2,1,0:T(8,128)(2,1)S(1)} %collective-permute-done.7.refs_1_, ...), custom_call_target="tpu_custom_call" | custom-call | flops 4000000000 | bytes 1048576 | tf_op jit(solution)/shard_map/pallas_call | solution.py:324
  24.6 0.0 collective-permute-done.3.refs_1_
  24.6 2.2 %shard_map.60 = (bf16[2,1,1024,128]{3,2,1,0:T(8,128)(2,1)S(1)}, f32[2,128,8,128]{3,2,1,0:T(8,128)S(1)}, f32[2,1,1024,128]{3,2,1,0:T(8,128)S(1)}, f32[2,1,1024,128]{3,2,1,0:T(8,128)S(1)}) custom-call(bf16[2,1024,128]{2,1,0:T(8,128)(2,1)S(1)} %get-tuple-element.38.refs_0_, bf16[1,1024,128]{2,1,0:T(8,128)(2,1)S(1)} %collective-permute-done.3.refs_1_, ...), custom_call_target="tpu_custom_call" | custom-call | flops 4000000000 | bytes 1048576 | tf_op jit(solution)/shard_map/pallas_call | solution.py:324
  26.8 0.3 collective-permute-done.8.refs_1_
  27.1 1.9 %collective-permute-start.9 = (bf16[2,2,2,128,128]{4,3,2,1,0:T(8,128)(2,1)S(1)}, bf16[2,2,2,128,128]{4,3,2,1,0:T(8,128)(2,1)S(1)}, u32[]{:S(2)}, u32[]{:S(2)}) collective-permute-start(bf16[2,2,2,128,128]{4,3,2,1,0:T(8,128)(2,1)S(1)} %collective-permute-done.8.refs_1_), channel_id=1, source_target_pairs={{0,2},{2,0},{4,6},{6,4},{8,10},{10,8},{12,14},{14,12},{16,18},{18,... | collective-permute-start | bytes 786440 | tf_op jit(solution)/shard_map/ppermute | solution.py:351
  29.0 0.0 collective-permute-done.10.refs_0_
  29.0 1.7 %shard_map.62 = (bf16[2,1,1024,128]{3,2,1,0:T(8,128)(2,1)S(1)}, f32[2,128,8,128]{3,2,1,0:T(8,128)S(1)}, f32[2,1,1024,128]{3,2,1,0:T(8,128)S(1)}, f32[2,1,1024,12...) custom-call(bf16[2,2,2,128,128]{4,3,2,1,0:T(8,128)(2,1)S(1)} %collec, ...), custom_call_target="tpu_custom_call", output_to_operand_aliasing={{0}: (2, {}), {1}: (3, {}), {2}: (4, {}), {3}: (5, {}), {4}... | custom-call | flops 4000000000 | bytes 1048576 | tf_op jit(solution)/shard_map/pallas_call | solution.py:324
  30.8 0.0 collective-permute-done.2.refs_0_
  30.8 0.0 collective-permute-done.9.refs_1_
  30.8 3.1 %shard_map.63 = (f32[1,256,16,128]{3,2,1,0:T(8,128)}, f32[16,1,256]{2,1,0:T(1,128)}, f32[16,1,256]{2,1,0:T(1,128)}, bf16[2,1,1024,128]{3,2,1,0:T(8,128)(2,1)S(1)...) custom-call(bf16[2,2,2,128,128]{4,3,2,1,0:T(8,128)(2,1)S(1)} %collec, ...), custom_call_target="tpu_custom_call", output_to_operand_aliasing={{3}: (2, {}), {4}: (3, {}), {5}: (4, {}), {6}: (5, {}), {7}... | custom-call | flops 4000000000 | bytes 1048576 | tf_op jit(solution)/shard_map/pallas_call | solution.py:324
  (1 shorter events, 0.0 us)
Async XLA Ops:
  2.5 7.5 %collective-permute-start.4 = (bf16[2,2,128,128]{3,2,1,0:T(8,128)(2,1)}, bf16[2,2,128,128]{3,2,1,0:T(8,128)(2,1)S(1)}, u32[]{:S(2)}, u32[]{:S(2)}) collective-permute-start(bf16[2,2,128,128]{3,2,1,0:T(8,128)(2,1)} %get-tuple-element.37), channel_id=1, source_target_pairs={{0,1},{1,0},{2,3},{3,2},{4,5},{5,4},{6,7},{7,6},{8,9},{9,8},{10,11... | collective-permute-start | bytes 393224 | tf_op jit(solution)/shard_map/ppermute | solution.py:351
  4.6 7.6 %collective-permute-start = (bf16[2,2,128,128]{3,2,1,0:T(8,128)(2,1)}, bf16[2,2,128,128]{3,2,1,0:T(8,128)(2,1)S(1)}, u32[]{:S(2)}, u32[]{:S(2)}) collective-permute-start(bf16[2,2,128,128]{3,2,1,0:T(8,128)(2,1)} %get-tuple-element.36), channel_id=1, source_target_pairs={{0,8},{1,9},{2,10},{3,11},{4,12},{5,13},{6,14},{7,15},{8,16},{9,17... | collective-permute-start | bytes 393224 | tf_op jit(solution)/shard_map/ppermute | solution.py:360
  5.9 7.9 %collective-permute-start.1 = (bf16[2,2,128,128]{3,2,1,0:T(8,128)(2,1)}, bf16[2,2,128,128]{3,2,1,0:T(8,128)(2,1)S(1)}, u32[]{:S(2)}, u32[]{:S(2)}) collective-permute-start(bf16[2,2,128,128]{3,2,1,0:T(8,128)(2,1)} %get-tuple-element.37), channel_id=1, source_target_pairs={{0,9},{1,8},{2,11},{3,10},{4,13},{5,12},{6,15},{7,14},{8,17},{9,16... | collective-permute-start | bytes 393224 | tf_op jit(solution)/shard_map/ppermute | solution.py:360
  7.1 1.2 %copy-start = (bf16[1,128,32,128]{3,2,1,0:T(8,128)(2,1)S(1)}, bf16[1,128,32,128]{3,2,1,0:T(8,128)(2,1)}, u32[]{:S(2)}) copy-start(bf16[1,128,32,128]{3,2,1,0:T(8,128)(2,1)} %q_ref.1) | copy-start | bytes 3145732
  8.7 10.3 %collective-permute-start.7 = (bf16[1,1024,128]{2,1,0:T(8,128)(2,1)S(1)}, bf16[1,1024,128]{2,1,0:T(8,128)(2,1)S(1)}, u32[]{:S(2)}, u32[]{:S(2)}) collective-permute-start(bf16[1,1024,128]{2,1,0:T(8,128)(2,1)S(1)} %get-tuple-element.44), channel_id=1, source_target_pairs={{0,1},{1,0},{2,3},{3,2},{4,5},{5,4},{6,7},{7,6},{8,9},{9,8},{10,11... | collective-permute-start | bytes 786440 | tf_op jit(solution)/shard_map/ppermute | solution.py:351
  10.9 9.7 %collective-permute-start.6 = (bf16[2,2,2,128,128]{4,3,2,1,0:T(8,128)(2,1)S(1)}, bf16[2,2,2,128,128]{4,3,2,1,0:T(8,128)(2,1)S(1)}, u32[]{:S(2)}, u32[]{:S(2)}) collective-permute-start(bf16[2,2,2,128,128]{4,3,2,1,0:T(8,128)(2,1)S(1)} %pad_maximum_fusion.1.refs_2_), channel_id=1, source_target_pairs={{0,4},{2,6},{4,8},{6,10},{8,12},{10,14},{12,16},{14,18},{16,20},{1... | collective-permute-start | bytes 786440 | tf_op jit(solution)/shard_map/ppermute | solution.py:351
  13.8 8.5 %collective-permute-start.5 = (bf16[2,2,2,128,128]{4,3,2,1,0:T(8,128)(2,1)S(1)}, bf16[2,2,2,128,128]{4,3,2,1,0:T(8,128)(2,1)S(1)}, u32[]{:S(2)}, u32[]{:S(2)}) collective-permute-start(bf16[2,2,2,128,128]{4,3,2,1,0:T(8,128)(2,1)S(1)} %get-tuple-element.69), channel_id=1, source_target_pairs={{0,2},{2,0},{4,6},{6,4},{8,10},{10,8},{12,14},{14,12},{16,18},{18,... | collective-permute-start | bytes 786440 | tf_op jit(solution)/shard_map/ppermute | solution.py:351
  15.6 9.1 %collective-permute-start.3 = (bf16[1,1024,128]{2,1,0:T(8,128)(2,1)S(1)}, bf16[1,1024,128]{2,1,0:T(8,128)(2,1)S(1)}, u32[]{:S(2)}, u32[]{:S(2)}) collective-permute-start(bf16[1,1024,128]{2,1,0:T(8,128)(2,1)S(1)} %get-tuple-element.39), channel_id=1, source_target_pairs={{0,1},{1,0},{2,3},{3,2},{4,5},{5,4},{6,7},{7,6},{8,9},{9,8},{10,11... | collective-permute-start | bytes 786440 | tf_op jit(solution)/shard_map/ppermute | solution.py:351
  16.8 10.2 %collective-permute-start.8 = (bf16[2,2,2,128,128]{4,3,2,1,0:T(8,128)(2,1)S(1)}, bf16[2,2,2,128,128]{4,3,2,1,0:T(8,128)(2,1)S(1)}, u32[]{:S(2)}, u32[]{:S(2)}) collective-permute-start(bf16[2,2,2,128,128]{4,3,2,1,0:T(8,128)(2,1)S(1)} %get-tuple-element.70.refs_3_), channel_id=1, source_target_pairs={{0,4},{2,6},{4,8},{6,10},{8,12},{10,14},{12,16},{14,18},{16,20},{1... | collective-permute-start | bytes 786440 | tf_op jit(solution)/shard_map/ppermute | solution.py:351
  19.0 11.8 %collective-permute-start.2 = (bf16[2,2,2,128,128]{4,3,2,1,0:T(8,128)(2,1)S(1)}, bf16[2,2,2,128,128]{4,3,2,1,0:T(8,128)(2,1)S(1)}, u32[]{:S(2)}, u32[]{:S(2)}) collective-permute-start(bf16[2,2,2,128,128]{4,3,2,1,0:T(8,128)(2,1)S(1)} %get-tuple-element.70.refs_3_), channel_id=1, source_target_pairs={{0,2},{2,8},{4,6},{6,12},{8,10},{10,16},{12,14},{14,20},{16,18},{1... | collective-permute-start | bytes 786440 | tf_op jit(solution)/shard_map/ppermute | solution.py:351
  20.6 8.4 %collective-permute-start.10 = (bf16[2,2,2,128,128]{4,3,2,1,0:T(8,128)(2,1)S(1)}, bf16[2,2,2,128,128]{4,3,2,1,0:T(8,128)(2,1)S(1)}, u32[]{:S(2)}, u32[]{:S(2)}) collective-permute-start(bf16[2,2,2,128,128]{4,3,2,1,0:T(8,128)(2,1)S(1)} %collective-permute-done.6.refs_5_), channel_id=1, source_target_pairs={{0,2},{2,0},{4,6},{6,4},{8,10},{10,8},{12,14},{14,12},{16,18},{18,... | collective-permute-start | bytes 786440 | tf_op jit(solution)/shard_map/ppermute | solution.py:351
  27.1 3.7 %collective-permute-start.9 = (bf16[2,2,2,128,128]{4,3,2,1,0:T(8,128)(2,1)S(1)}, bf16[2,2,2,128,128]{4,3,2,1,0:T(8,128)(2,1)S(1)}, u32[]{:S(2)}, u32[]{:S(2)}) collective-permute-start(bf16[2,2,2,128,128]{4,3,2,1,0:T(8,128)(2,1)S(1)} %collective-permute-done.8.refs_1_), channel_id=1, source_target_pairs={{0,2},{2,0},{4,6},{6,4},{8,10},{10,8},{12,14},{14,12},{16,18},{18,... | collective-permute-start | bytes 786440 | tf_op jit(solution)/shard_map/ppermute | solution.py:351

commit v7 on v6

--- a/solution.py
+++ b/solution.py
@@ -138,7 +138,13 @@
         out_hbm, max_hbm, sum_hbm = refs[:3]
         refs = refs[3:]
     states = [refs[i : i + 4] for i in range(0, held, 4)]
-    kvbuf, tops_buf, sums_buf, order, qsem, ksem, osem = refs[held:]
+    if end:
+        kvbuf, tops_buf, sums_buf = kv_hbm[0], *refs[held : held + 2]
+        held += 2
+    else:
+        kvbuf = refs[held]
+        held += 1
+    order, qsem, ksem, osem = refs[held:]
     per, m_rows, width = states[0][0].shape[1:]
     rows = m_rows // GROUP
     small = SPAN // rows
@@ -151,7 +157,7 @@
         mine = q_hbm[0].at[pl.ds(parts[0] * per, per)]
         for s, ref in enumerate([mine, *q_hbm[1:]]):
             loads.append(pltpu.make_async_copy(ref, states[0][0].at[s], qsem.at[s]))
-    for i, ref in enumerate(kv_hbm):
+    for i, ref in enumerate([] if end else kv_hbm):
         to = kvbuf.at[pl.ds(i * count, count)]
         ref = ref.at[:, :, pl.ds(parts[0] * per, len(parts) * per)]
         loads.append(pltpu.make_async_copy(ref, to, ksem.at[i]))
@@ -252,20 +258,27 @@
     if begin:
         for s in range(count):
             run(s, 0, seen[s], True)
-    least, most = step_range(n, count, rows, offsets, begin, small)
-    for t in range(least):
-        step(t)
-    for t in range(least, most):
-
-        @pl.when(t < ends[-1])
-        def _():
+    if not end:
+        least, most = step_range(n, count, rows, offsets, begin, small)
+        for t in range(least):
             step(t)
-
-    if not end:
+        for t in range(least, most):
+
+            @pl.when(t < ends[-1])
+            def _():
+                step(t)
+
         return
+
     saves = []
     heads = per * GROUP
     for s in range(count):
+        for at in range(0, total, small):
+
+            @pl.when(at < seen[s])
+            def _():
+                run(s, at, seen[s], False)
+
         row0 = pl.multiple_of(chunk_of[s] * rows, rows)
         for i, part in enumerate(parts):
             to = out_hbm.at[0, pl.ds(row0, rows), pl.ds(part * heads, heads)]
@@ -326,13 +339,15 @@
             attend_kernel, n, count, parts, offsets, min(BLOCK, m_rows), begin, end
         ),
         out_shape=out_shape,
-        in_specs=[away] * given + [near] * (0 if begin else len(held)),
+        in_specs=[near if end else away] * given + [near] * (0 if begin else len(held)),
         out_specs=out_specs,
         input_output_aliases=aliases,
-        scratch_shapes=[
-            pltpu.VMEM((total, 2, len(parts) * per, rows, width), BF16),
-            pltpu.VMEM((all_heads * GROUP, 1, count * rows), F32),
-            pltpu.VMEM((all_heads * GROUP, 1, count * rows), F32),
+        scratch_shapes=(
+            [pltpu.VMEM((all_heads * GROUP, 1, count * rows), F32)] * 2
+            if end
+            else [pltpu.VMEM((total, 2, len(parts) * per, rows, width), BF16)]
+        )
+        + [
             pltpu.SMEM((count, total + 1 + SPAN // rows), jnp.int32),
             pltpu.SemaphoreType.DMA((count,)),
             pltpu.SemaphoreType.DMA((len(offsets),)),
@@ -398,13 +413,28 @@
         lambda p: bit(p, 1, 3),
     ]
     own_at, up_at, far_at, odd_at, far_c_at, side_at, near_at, side_c_at = offsets
-    first = [both, up, near, side], [own_at, up_at, near_at, side_at]
-    state = [x for i in range(split) for x in attend(q[i], *first, [i], split, n, None, False)]
+    blocks = dict(
+        own=(both, own_at), up=(up, up_at), near=(near, near_at), side=(side, side_at),
+        side_c=(side_c, side_c_at), odd=(odd, odd_at),
+    )
+
+    def take(names):
+        return [blocks[x][0] for x in names], [blocks[x][1] for x in names]
+
+    soon, late = ["own", "up", "near", "side"], ["side_c"]
+    state = []
+    for i in range(split):
+        last = i == split - 1
+        part = attend(q[i], *take(soon + late if last else soon), [i], split, n, None, False)
+        if not last:
+            part = attend([], *take(late), [i], split, n, part, False)
+            part, q[i + 1] = lax.optimization_barrier((part, q[i + 1]))
+        state += part
     state, far = lax.optimization_barrier((state, far))
     far_c = along(far, "ctx", lambda i: i ^ 1)
     parts = list(range(split))
-    state = attend([], [side_c, far], [side_c_at, far_at], parts, split, n, state, False)
-    return attend([], [odd, far_c], [odd_at, far_c_at], parts, split, n, state, True)
+    state = attend([], [odd, far], [odd_at, far_at], parts, split, n, state, False)
+    return attend([], [far_c], [far_c_at], parts, split, n, state, True)
 
 
 def solution(mesh):

time: 34 us -> 33 us (0.971)
  starting transfers between devices: 16.7 us -> 15.8 us
    ppermute x9, starting transfers between devices: 14.2 us -> 13.3 us  [along(): lax.ppermute(block, axis, [(i, target(i) % size) for i in range(size)])]
    pallas_call x4 -> x5, Pallas kernels: 9.18 us -> 9.32 us  [attend(): pl.pallas_call(functools.partial(attend_kernel, n, count, parts, offsets,...]
  transfers between devices with their start and end apart: 11 -> 11, of which waited for: 3 -> 2; matrix products, arithmetic and copies ran while one was open for 3% -> 3% of each run, Pallas kernels for 19% -> 23%
where the time goes in v7:
time: 33 us; the launch traced here: 32.8 us
  starting transfers between devices  15.8 us (48%)
  Pallas kernels  11.4 us (35%)
  waiting for transfers between devices  2.63 us (8%)
  local copies, waits for them, and re-layouts  1.22 us (4%)
  other arithmetic  0.97 us (3%)
  between operations  0.73 us (2%)
    ppermute x9, starting transfers between devices, along(): lax.ppermute(block, axis, [(i, target(i) % size) for i in range(size)])  13.3 us
    pallas_call x5, Pallas kernels, attend(): pl.pallas_call(functools.partial(attend_kernel, n, count, parts, offsets,...  9.32 us
    ppermute x2, starting transfers between devices, climb(): return lax.ppermute(block, ('ctx', 'head'), edges)  2.54 us
    pallas_call x1, Pallas kernels, pack_kv(): pl.pallas_call(pack_kv_kernel, out_shape=(shape,) * count, in_specs=[pl.B...  1.82 us
    ppermute x2, waiting for transfers between devices, climb(): return lax.ppermute(block, ('ctx', 'head'), edges)  1.63 us
    unnamed x2, local copies, waits for them, and re-layouts  1.22 us
    ppermute x9, waiting for transfers between devices, along(): lax.ppermute(block, axis, [(i, target(i) % size) for i in range(size)])  1 us
    another operation x1, other arithmetic, local(): both = lax.optimization_barrier(jnp.stack(own))  0.93 us
  transfers between devices with their start and end apart: 11, of which 2 were waited for; matrix products, arithmetic and copies ran while one was open for 3% of the time, Pallas kernels for 23%

profile of v7, /device:TPU:1, one launch (start us, length us, event | category | flops | bytes accessed | tf_op | source)
XLA Modules:
  0.0 32.8 jit_solution(11131121454556761810)
XLA Ops:
  0.6 1.8 %shard_map.58 = (bf16[2,2,128,128]{3,2,1,0:T(8,128)(2,1)}, bf16[2,2,128,128]{3,2,1,0:T(8,128)(2,1)}) custom-call(bf16[1,128,4,128]{3,2,1,0:T(4,128)(2,1)} %k_hbm.1, bf16[1,128,4,128]{3,2,1,0:T(4,128)(2,1)} %v_hbm.1), custom_call_target="tpu_custom_call" | custom-call | tf_op jit(solution)/shard_map/pallas_call | solution.py:58
  2.5 2.1 %collective-permute-start = (bf16[2,2,128,128]{3,2,1,0:T(8,128)(2,1)}, bf16[2,2,128,128]{3,2,1,0:T(8,128)(2,1)S(1)}, u32[]{:S(2)}, u32[]{:S(2)}) collective-permute-start(bf16[2,2,128,128]{3,2,1,0:T(8,128)(2,1)} %get-tuple-element.47), channel_id=1, source_target_pairs={{0,1},{1,0},{2,3},{3,2},{4,5},{5,4},{6,7},{7,6},{8,9},{9,8},{10,11... | collective-permute-start | bytes 393224 | tf_op jit(solution)/shard_map/ppermute | solution.py:366
  4.6 1.3 %collective-permute-start.4 = (bf16[2,2,128,128]{3,2,1,0:T(8,128)(2,1)}, bf16[2,2,128,128]{3,2,1,0:T(8,128)(2,1)S(1)}, u32[]{:S(2)}, u32[]{:S(2)}) collective-permute-start(bf16[2,2,128,128]{3,2,1,0:T(8,128)(2,1)} %get-tuple-element.46), channel_id=1, source_target_pairs={{0,8},{1,9},{2,10},{3,11},{4,12},{5,13},{6,14},{7,15},{8,16},{9,17... | collective-permute-start | bytes 393224 | tf_op jit(solution)/shard_map/ppermute | solution.py:375
  5.9 1.2 %collective-permute-start.5 = (bf16[2,2,128,128]{3,2,1,0:T(8,128)(2,1)}, bf16[2,2,128,128]{3,2,1,0:T(8,128)(2,1)S(1)}, u32[]{:S(2)}, u32[]{:S(2)}) collective-permute-start(bf16[2,2,128,128]{3,2,1,0:T(8,128)(2,1)} %get-tuple-element.47), channel_id=1, source_target_pairs={{0,9},{1,8},{2,11},{3,10},{4,13},{5,12},{6,15},{7,14},{8,17},{9,16... | collective-permute-start | bytes 393224 | tf_op jit(solution)/shard_map/ppermute | solution.py:375
  7.1 0.0 copy-start
  7.1 1.2 %copy-done = bf16[1,128,32,128]{3,2,1,0:T(8,128)(2,1)S(1)} copy-done((bf16[1,128,32,128]{3,2,1,0:T(8,128)(2,1)S(1)}, bf16[1,128,32,128]{3,2,1,0:T(8,128)(2,1)}, u32[]{:S(2)}) %copy-start) | copy-done | bytes 1048600
  8.4 0.3 shard_map.59
  8.6 1.3 %collective-permute-start.3 = (bf16[1,1024,128]{2,1,0:T(8,128)(2,1)S(1)}, bf16[1,1024,128]{2,1,0:T(8,128)(2,1)S(1)}, u32[]{:S(2)}, u32[]{:S(2)}) collective-permute-start(bf16[1,1024,128]{2,1,0:T(8,128)(2,1)S(1)} %get-tuple-element.49), channel_id=1, source_target_pairs={{0,1},{1,0},{2,3},{3,2},{4,5},{5,4},{6,7},{7,6},{8,9},{9,8},{10,11... | collective-permute-start | bytes 786440 | tf_op jit(solution)/shard_map/ppermute | solution.py:366
  10.0 0.0 collective-permute-done
  10.0 0.9 %pad_maximum_fusion.refs_2_ = bf16[2,2,2,128,128]{4,3,2,1,0:T(8,128)(2,1)S(1)} fusion(bf16[1,2,2,128,128]{4,3,2,1,0:T(8,128)(2,1)S(1)} %bitcast.5, bf16[1,2,2,128,128]{4,3,2,1,0:T(8,128)(2,1)} %bitcast.4), kind=kLoop, calls=%fused_computation | loop fusion | flops 131072 | bytes 524288 | tf_op jit(solution)/shard_map/stack | solution.py:396
  10.9 1.3 %collective-permute-start.1 = (bf16[2,2,2,128,128]{4,3,2,1,0:T(8,128)(2,1)S(1)}, bf16[2,2,2,128,128]{4,3,2,1,0:T(8,128)(2,1)S(1)}, u32[]{:S(2)}, u32[]{:S(2)}) collective-permute-start(bf16[2,2,2,128,128]{4,3,2,1,0:T(8,128)(2,1)S(1)} %pad_maximum_fusion.refs_2_), channel_id=1, source_target_pairs={{0,4},{2,6},{4,8},{6,10},{8,12},{10,14},{12,16},{14,18},{16,20},{1... | collective-permute-start | bytes 786440 | tf_op jit(solution)/shard_map/ppermute | solution.py:366
  12.2 0.0 collective-permute-done.4
  12.2 1.6 %collective-permute-done.5 = bf16[2,2,128,128]{3,2,1,0:T(8,128)(2,1)S(1)} collective-permute-done((bf16[2,2,128,128]{3,2,1,0:T(8,128)(2,1)}, bf16[2,2,128,128]{3,2,1,0:T(8,128)(2,1)S(1)}, u32[]{:S(2)}, u32[]{:S(2)}) %collective-permute-start.5) | collective-permute-done | bytes 131104 | tf_op jit(solution)/shard_map/ppermute | solution.py:375
  13.8 1.7 %collective-permute-start.6 = (bf16[2,2,2,128,128]{4,3,2,1,0:T(8,128)(2,1)S(1)}, bf16[2,2,2,128,128]{4,3,2,1,0:T(8,128)(2,1)S(1)}, u32[]{:S(2)}, u32[]{:S(2)}) collective-permute-start(bf16[2,2,2,128,128]{4,3,2,1,0:T(8,128)(2,1)S(1)} %get-tuple-element.89), channel_id=1, source_target_pairs={{0,2},{2,0},{4,6},{6,4},{8,10},{10,8},{12,14},{14,12},{16,18},{18,... | collective-permute-start | bytes 786440 | tf_op jit(solution)/shard_map/ppermute | solution.py:366
  15.5 1.3 %collective-permute-start.7 = (bf16[1,1024,128]{2,1,0:T(8,128)(2,1)S(1)}, bf16[1,1024,128]{2,1,0:T(8,128)(2,1)S(1)}, u32[]{:S(2)}, u32[]{:S(2)}) collective-permute-start(bf16[1,1024,128]{2,1,0:T(8,128)(2,1)S(1)} %get-tuple-element.58), channel_id=1, source_target_pairs={{0,1},{1,0},{2,3},{3,2},{4,5},{5,4},{6,7},{7,6},{8,9},{9,8},{10,11... | collective-permute-start | bytes 786440 | tf_op jit(solution)/shard_map/ppermute | solution.py:366
  16.8 1.2 %collective-permute-start.8 = (bf16[2,2,2,128,128]{4,3,2,1,0:T(8,128)(2,1)S(1)}, bf16[2,2,2,128,128]{4,3,2,1,0:T(8,128)(2,1)S(1)}, u32[]{:S(2)}, u32[]{:S(2)}) collective-permute-start(bf16[2,2,2,128,128]{4,3,2,1,0:T(8,128)(2,1)S(1)} %get-tuple-element.90.refs_3_), channel_id=1, source_target_pairs={{0,4},{2,6},{4,8},{6,10},{8,12},{10,14},{12,16},{14,18},{16,20},{1... | collective-permute-start | bytes 786440 | tf_op jit(solution)/shard_map/ppermute | solution.py:366
  18.0 1.0 %collective-permute-done.3.refs_1_ = bf16[1,1024,128]{2,1,0:T(8,128)(2,1)S(1)} collective-permute-done((bf16[1,1024,128]{2,1,0:T(8,128)(2,1)S(1)}, bf16[1,1024,128]{2,1,0:T(8,128)(2,1)S(1)}, u32[]{:S(2)}, u32[]{:S(2)}) %collective-permute-start.3) | collective-permute-done | bytes 262176 | tf_op jit(solution)/shard_map/ppermute | solution.py:366
  19.0 1.6 %collective-permute-start.10 = (bf16[2,2,2,128,128]{4,3,2,1,0:T(8,128)(2,1)S(1)}, bf16[2,2,2,128,128]{4,3,2,1,0:T(8,128)(2,1)S(1)}, u32[]{:S(2)}, u32[]{:S(2)}) collective-permute-start(bf16[2,2,2,128,128]{4,3,2,1,0:T(8,128)(2,1)S(1)} %get-tuple-element.90.refs_3_), channel_id=1, source_target_pairs={{0,2},{2,8},{4,6},{6,12},{8,10},{10,16},{12,14},{14,20},{16,18},{1... | collective-permute-start | bytes 786440 | tf_op jit(solution)/shard_map/ppermute | solution.py:366
  20.6 0.0 collective-permute-done.1.refs_5_
  20.6 1.8 %collective-permute-start.2 = (bf16[2,2,2,128,128]{4,3,2,1,0:T(8,128)(2,1)S(1)}, bf16[2,2,2,128,128]{4,3,2,1,0:T(8,128)(2,1)S(1)}, u32[]{:S(2)}, u32[]{:S(2)}) collective-permute-start(bf16[2,2,2,128,128]{4,3,2,1,0:T(8,128)(2,1)S(1)} %collective-permute-done.1.refs_5_), channel_id=1, source_target_pairs={{0,2},{2,0},{4,6},{6,4},{8,10},{10,8},{12,14},{14,12},{16,18},{18,... | collective-permute-start | bytes 786440 | tf_op jit(solution)/shard_map/ppermute | solution.py:366
  22.4 0.0 collective-permute-done.6.refs_4_
  22.4 2.2 %shard_map.60 = (bf16[2,1,1024,128]{3,2,1,0:T(8,128)(2,1)S(1)}, f32[2,128,8,128]{3,2,1,0:T(8,128)S(1)}, f32[2,1,1024,128]{3,2,1,0:T(8,128)S(1)}, f32[2,1,1024,128]{3,2,1,0:T(8,128)S(1)}) custom-call(bf16[2,1024,128]{2,1,0:T(8,128)(2,1)S(1)} %get-tuple-element.63.refs_0_, bf16[1,1024,128]{2,1,0:T(8,128)(2,1)S(1)} %collective-permute-done.3.refs_1_, ...), custom_call_target="tpu_custom_call" | custom-call | flops 4000000000 | bytes 1048576 | tf_op jit(solution)/shard_map/pallas_call | solution.py:337
  24.6 0.0 collective-permute-done.2.refs_0_.refs_6_
  24.6 0.8 %shard_map.61 = (bf16[2,1,1024,128]{3,2,1,0:T(8,128)(2,1)S(1)}, f32[2,128,8,128]{3,2,1,0:T(8,128)S(1)}, f32[2,1,1024,128]{3,2,1,0:T(8,128)S(1)}, f32[2,1,1024,128]{3,2,1,0:T(8,128)S(1)}) custom-call(bf16[2,2,2,128,128]{4,3,2,1,0:T(8,128)(2,1)S(1)} %collective-permute-done.2.refs_0_.refs_6_, ...), custom_call_target="tpu_custom_call", output_to_operand_aliasing={{0}: (1, {}), {1}: (2, {}), {2}: (3, {}), {3}: (4, {})} | custom-call | flops 1000000000 | bytes 1048576 | tf_op jit(solution)/shard_map/pallas_call | solution.py:337
  25.3 0.0 collective-permute-done.7.refs_1_
  25.4 2.6 %shard_map.62 = (bf16[2,1,1024,128]{3,2,1,0:T(8,128)(2,1)S(1)}, f32[2,128,8,128]{3,2,1,0:T(8,128)S(1)}, f32[2,1,1024,128]{3,2,1,0:T(8,128)S(1)}, f32[2,1,1024,128]{3,2,1,0:T(8,128)S(1)}) custom-call(bf16[2,1024,128]{2,1,0:T(8,128)(2,1)S(1)} %get-tuple-element.63.refs_0_, bf16[1,1024,128]{2,1,0:T(8,128)(2,1)S(1)} %collective-permute-done.7.refs_1_, ...), custom_call_target="tpu_custom_call" | custom-call | flops 5000000000 | bytes 1048576 | tf_op jit(solution)/shard_map/pallas_call | solution.py:337
  28.0 0.0 collective-permute-done.8.refs_1_
  28.0 1.0 %collective-permute-start.9 = (bf16[2,2,2,128,128]{4,3,2,1,0:T(8,128)(2,1)S(1)}, bf16[2,2,2,128,128]{4,3,2,1,0:T(8,128)(2,1)S(1)}, u32[]{:S(2)}, u32[]{:S(2)}) collective-permute-start(bf16[2,2,2,128,128]{4,3,2,1,0:T(8,128)(2,1)S(1)} %collective-permute-done.8.refs_1_), channel_id=1, source_target_pairs={{0,2},{2,0},{4,6},{6,4},{8,10},{10,8},{12,14},{14,12},{16,18},{18,... | collective-permute-start | bytes 786440 | tf_op jit(solution)/shard_map/ppermute | solution.py:366
  29.0 0.0 collective-permute-done.10.refs_0_
  29.0 1.7 %shard_map.63 = (bf16[2,1,1024,128]{3,2,1,0:T(8,128)(2,1)S(1)}, f32[2,128,8,128]{3,2,1,0:T(8,128)S(1)}, f32[2,1,1024,128]{3,2,1,0:T(8,128)S(1)}, f32[2,1,1024,12...) custom-call(bf16[2,2,2,128,128]{4,3,2,1,0:T(8,128)(2,1)S(1)} %collec, ...), custom_call_target="tpu_custom_call", output_to_operand_aliasing={{0}: (2, {}), {1}: (3, {}), {2}: (4, {}), {3}: (5, {}), {4}... | custom-call | flops 4000000000 | bytes 1048576 | tf_op jit(solution)/shard_map/pallas_call | solution.py:337
  30.7 0.0 collective-permute-done.9.refs_0_
  30.8 2.0 %shard_map.64 = (f32[1,256,16,128]{3,2,1,0:T(8,128)}, f32[16,1,256]{2,1,0:T(1,128)}, f32[16,1,256]{2,1,0:T(1,128)}, bf16[2,1,1024,128]{3,2,1,0:T(8,128)(2,1)S(1)...) custom-call(bf16[2,2,2,128,128]{4,3,2,1,0:T(8,128)(2,1)S(1)} %collec, ...), custom_call_target="tpu_custom_call", output_to_operand_aliasing={{3}: (1, {}), {4}: (2, {}), {5}: (3, {}), {6}: (4, {}), {7}... | custom-call | flops 2000000000 | bytes 1048576 | tf_op jit(solution)/shard_map/pallas_call | solution.py:337
  (1 shorter events, 0.0 us)
Async XLA Ops:
  2.5 7.5 %collective-permute-start = (bf16[2,2,128,128]{3,2,1,0:T(8,128)(2,1)}, bf16[2,2,128,128]{3,2,1,0:T(8,128)(2,1)S(1)}, u32[]{:S(2)}, u32[]{:S(2)}) collective-permute-start(bf16[2,2,128,128]{3,2,1,0:T(8,128)(2,1)} %get-tuple-element.47), channel_id=1, source_target_pairs={{0,1},{1,0},{2,3},{3,2},{4,5},{5,4},{6,7},{7,6},{8,9},{9,8},{10,11... | collective-permute-start | bytes 393224 | tf_op jit(solution)/shard_map/ppermute | solution.py:366
  4.6 7.6 %collective-permute-start.4 = (bf16[2,2,128,128]{3,2,1,0:T(8,128)(2,1)}, bf16[2,2,128,128]{3,2,1,0:T(8,128)(2,1)S(1)}, u32[]{:S(2)}, u32[]{:S(2)}) collective-permute-start(bf16[2,2,128,128]{3,2,1,0:T(8,128)(2,1)} %get-tuple-element.46), channel_id=1, source_target_pairs={{0,8},{1,9},{2,10},{3,11},{4,12},{5,13},{6,14},{7,15},{8,16},{9,17... | collective-permute-start | bytes 393224 | tf_op jit(solution)/shard_map/ppermute | solution.py:375
  5.9 7.9 %collective-permute-start.5 = (bf16[2,2,128,128]{3,2,1,0:T(8,128)(2,1)}, bf16[2,2,128,128]{3,2,1,0:T(8,128)(2,1)S(1)}, u32[]{:S(2)}, u32[]{:S(2)}) collective-permute-start(bf16[2,2,128,128]{3,2,1,0:T(8,128)(2,1)} %get-tuple-element.47), channel_id=1, source_target_pairs={{0,9},{1,8},{2,11},{3,10},{4,13},{5,12},{6,15},{7,14},{8,17},{9,16... | collective-permute-start | bytes 393224 | tf_op jit(solution)/shard_map/ppermute | solution.py:375
  7.1 1.2 %copy-start = (bf16[1,128,32,128]{3,2,1,0:T(8,128)(2,1)S(1)}, bf16[1,128,32,128]{3,2,1,0:T(8,128)(2,1)}, u32[]{:S(2)}) copy-start(bf16[1,128,32,128]{3,2,1,0:T(8,128)(2,1)} %q_ref.1) | copy-start | bytes 3145732
  8.6 10.3 %collective-permute-start.3 = (bf16[1,1024,128]{2,1,0:T(8,128)(2,1)S(1)}, bf16[1,1024,128]{2,1,0:T(8,128)(2,1)S(1)}, u32[]{:S(2)}, u32[]{:S(2)}) collective-permute-start(bf16[1,1024,128]{2,1,0:T(8,128)(2,1)S(1)} %get-tuple-element.49), channel_id=1, source_target_pairs={{0,1},{1,0},{2,3},{3,2},{4,5},{5,4},{6,7},{7,6},{8,9},{9,8},{10,11... | collective-permute-start | bytes 786440 | tf_op jit(solution)/shard_map/ppermute | solution.py:366
  10.9 9.7 %collective-permute-start.1 = (bf16[2,2,2,128,128]{4,3,2,1,0:T(8,128)(2,1)S(1)}, bf16[2,2,2,128,128]{4,3,2,1,0:T(8,128)(2,1)S(1)}, u32[]{:S(2)}, u32[]{:S(2)}) collective-permute-start(bf16[2,2,2,128,128]{4,3,2,1,0:T(8,128)(2,1)S(1)} %pad_maximum_fusion.refs_2_), channel_id=1, source_target_pairs={{0,4},{2,6},{4,8},{6,10},{8,12},{10,14},{12,16},{14,18},{16,20},{1... | collective-permute-start | bytes 786440 | tf_op jit(solution)/shard_map/ppermute | solution.py:366
  13.8 8.5 %collective-permute-start.6 = (bf16[2,2,2,128,128]{4,3,2,1,0:T(8,128)(2,1)S(1)}, bf16[2,2,2,128,128]{4,3,2,1,0:T(8,128)(2,1)S(1)}, u32[]{:S(2)}, u32[]{:S(2)}) collective-permute-start(bf16[2,2,2,128,128]{4,3,2,1,0:T(8,128)(2,1)S(1)} %get-tuple-element.89), channel_id=1, source_target_pairs={{0,2},{2,0},{4,6},{6,4},{8,10},{10,8},{12,14},{14,12},{16,18},{18,... | collective-permute-start | bytes 786440 | tf_op jit(solution)/shard_map/ppermute | solution.py:366
  15.5 9.8 %collective-permute-start.7 = (bf16[1,1024,128]{2,1,0:T(8,128)(2,1)S(1)}, bf16[1,1024,128]{2,1,0:T(8,128)(2,1)S(1)}, u32[]{:S(2)}, u32[]{:S(2)}) collective-permute-start(bf16[1,1024,128]{2,1,0:T(8,128)(2,1)S(1)} %get-tuple-element.58), channel_id=1, source_target_pairs={{0,1},{1,0},{2,3},{3,2},{4,5},{5,4},{6,7},{7,6},{8,9},{9,8},{10,11... | collective-permute-start | bytes 786440 | tf_op jit(solution)/shard_map/ppermute | solution.py:366
  16.8 11.2 %collective-permute-start.8 = (bf16[2,2,2,128,128]{4,3,2,1,0:T(8,128)(2,1)S(1)}, bf16[2,2,2,128,128]{4,3,2,1,0:T(8,128)(2,1)S(1)}, u32[]{:S(2)}, u32[]{:S(2)}) collective-permute-start(bf16[2,2,2,128,128]{4,3,2,1,0:T(8,128)(2,1)S(1)} %get-tuple-element.90.refs_3_), channel_id=1, source_target_pairs={{0,4},{2,6},{4,8},{6,10},{8,12},{10,14},{12,16},{14,18},{16,20},{1... | collective-permute-start | bytes 786440 | tf_op jit(solution)/shard_map/ppermute | solution.py:366
  19.0 10.0 %collective-permute-start.10 = (bf16[2,2,2,128,128]{4,3,2,1,0:T(8,128)(2,1)S(1)}, bf16[2,2,2,128,128]{4,3,2,1,0:T(8,128)(2,1)S(1)}, u32[]{:S(2)}, u32[]{:S(2)}) collective-permute-start(bf16[2,2,2,128,128]{4,3,2,1,0:T(8,128)(2,1)S(1)} %get-tuple-element.90.refs_3_), channel_id=1, source_target_pairs={{0,2},{2,8},{4,6},{6,12},{8,10},{10,16},{12,14},{14,20},{16,18},{1... | collective-permute-start | bytes 786440 | tf_op jit(solution)/shard_map/ppermute | solution.py:366
  20.6 4.0 %collective-permute-start.2 = (bf16[2,2,2,128,128]{4,3,2,1,0:T(8,128)(2,1)S(1)}, bf16[2,2,2,128,128]{4,3,2,1,0:T(8,128)(2,1)S(1)}, u32[]{:S(2)}, u32[]{:S(2)}) collective-permute-start(bf16[2,2,2,128,128]{4,3,2,1,0:T(8,128)(2,1)S(1)} %collective-permute-done.1.refs_5_), channel_id=1, source_target_pairs={{0,2},{2,0},{4,6},{6,4},{8,10},{10,8},{12,14},{14,12},{16,18},{18,... | collective-permute-start | bytes 786440 | tf_op jit(solution)/shard_map/ppermute | solution.py:366
  28.0 2.8 %collective-permute-start.9 = (bf16[2,2,2,128,128]{4,3,2,1,0:T(8,128)(2,1)S(1)}, bf16[2,2,2,128,128]{4,3,2,1,0:T(8,128)(2,1)S(1)}, u32[]{:S(2)}, u32[]{:S(2)}) collective-permute-start(bf16[2,2,2,128,128]{4,3,2,1,0:T(8,128)(2,1)S(1)} %collective-permute-done.8.refs_1_), channel_id=1, source_target_pairs={{0,2},{2,0},{4,6},{6,4},{8,10},{10,8},{12,14},{14,12},{16,18},{18,... | collective-permute-start | bytes 786440 | tf_op jit(solution)/shard_map/ppermute | solution.py:366

commit v8 on v7

--- a/solution.py
+++ b/solution.py
@@ -20,53 +20,10 @@
 SPAN = 256
 BLOCK = 128
 COST = 10**9
-PACK_LIMIT = 56 * 2**20
 
 
 def slot_of(head, per, count):
     return lax.rem(head // per - lax.axis_index("head") + count, count)
-
-
-def place(outs, head, per, at, x):
-    for d in range(len(outs)):
-
-        @pl.when(slot_of(head, per, len(outs)) == d)
-        def _():
-            outs[d][at + (head % per,)] = x
-
-
-def pack_kv_kernel(k_hbm, v_hbm, *refs):
-    outs, (flat, wide, sems) = refs[:-3], refs[-3:]
-    rows, heads, width = k_hbm.shape[1:]
-    loads = [
-        pltpu.make_async_copy(ref.at[0], flat.at[i], sems.at[i])
-        for i, ref in enumerate((k_hbm, v_hbm))
-    ]
-    for load in loads:
-        load.start()
-    for i in range(2):
-        loads[i].wait()
-        wide.at[i].reshape(rows, 8, width)[:, :heads, :] = flat[i].astype(F32)
-        for head in range(heads):
-            x = wide[i, pl.ds(head, rows, stride=8), :].astype(BF16)
-            place(outs, head, heads // len(outs), (i,), x)
-
-
-def pack_kv(keys, values, count):
-    rows, heads, width = keys.shape[1:]
-    shape = jax.ShapeDtypeStruct((2, heads // count, rows, width), BF16)
-    return pl.pallas_call(
-        pack_kv_kernel,
-        out_shape=(shape,) * count,
-        in_specs=[pl.BlockSpec(memory_space=pl.ANY)] * 2,
-        out_specs=[pl.BlockSpec(memory_space=pltpu.VMEM)] * count,
-        scratch_shapes=[
-            pltpu.VMEM((2, rows, heads, width), BF16),
-            pltpu.VMEM((2, rows * 8, width), F32),
-            pltpu.SemaphoreType.DMA((2,)),
-        ],
-        compiler_params=pltpu.CompilerParams(vmem_limit_bytes=PACK_LIMIT),
-    )(keys, values)
 
 
 def pack_q_kernel(count, q_ref, own, *away):
@@ -381,7 +338,16 @@
     me = lax.axis_index("ctx")
     swap = lambda x, d: along(x, "head", lambda i: i + d)
 
-    kv = pack_kv(keys, values, count)
+    mine = lax.axis_index("head")
+
+    def heads_of(x, d):
+        size = x.shape[2] // count
+        return lax.dynamic_slice_in_dim(x[0], lax.rem(mine + d, count) * size, size, axis=1)
+
+    kv = [
+        jnp.stack([heads_of(keys, d), heads_of(values, d)]).transpose(0, 2, 1, 3)
+        for d in range(count)
+    ]
     own = [kv[0]] + [swap(kv[d], d) for d in range(1, count)]
 
     layer = LAYER

time: 33 us -> 32.5 us (0.985)
  Pallas kernels: 11.4 us -> 9.6 us
  local copies, waits for them, and re-layouts: 1.22 us -> 2.66 us
  other arithmetic: 0.97 us -> 0.08 us
  waiting for transfers between devices: 2.63 us -> 3.48 us
    pallas_call x1 -> x0, Pallas kernels: 1.82 us -> none  [pack_kv(): pl.pallas_call(pack_kv_kernel, out_shape=(shape,) * count, in_specs=[pl.B...]
    dynamic_slice x0 -> x1, local copies, waits for them, and re-layouts: none -> 1.38 us  [heads_of(): lax.dynamic_slice_in_dim(x[0], lax.rem(mine + d, count) * size, size, axi...]
    another operation x1, other arithmetic: 0.93 us -> 0.03 us  [local(): both = lax.optimization_barrier(jnp.stack(own))]
    ppermute x2, waiting for transfers between devices: 1.63 us -> 2.33 us  [climb(): return lax.ppermute(block, ('ctx', 'head'), edges)]
    unnamed x2 -> x5, local copies, waits for them, and re-layouts: 1.22 us -> 1.26 us
  transfers between devices with their start and end apart: 11 -> 11, of which waited for: 2 -> 2; matrix products, arithmetic and copies ran while one was open for 3% -> 0% of each run, Pallas kernels for 23% -> 23%
where the time goes in v8:
time: 32.5 us; the launch traced here: 32.3 us
  starting transfers between devices  15.7 us (48%)
  Pallas kernels  9.6 us (30%)
  waiting for transfers between devices  3.48 us (11%)
  local copies, waits for them, and re-layouts  2.66 us (8%)
  between operations  0.77 us (2%)
    ppermute x9, starting transfers between devices, along(): lax.ppermute(block, axis, [(i, target(i) % size) for i in range(size)])  13.1 us
    pallas_call x5, Pallas kernels, attend(): pl.pallas_call(functools.partial(attend_kernel, n, count, parts, offsets,...  9.32 us
    ppermute x2, starting transfers between devices, climb(): return lax.ppermute(block, ('ctx', 'head'), edges)  2.59 us
    ppermute x2, waiting for transfers between devices, climb(): return lax.ppermute(block, ('ctx', 'head'), edges)  2.33 us
    dynamic_slice x1, local copies, waits for them, and re-layouts, heads_of(): lax.dynamic_slice_in_dim(x[0], lax.rem(mine + d, count) * size, size, axi...  1.38 us
    unnamed x5, local copies, waits for them, and re-layouts  1.26 us
    ppermute x9, waiting for transfers between devices, along(): lax.ppermute(block, axis, [(i, target(i) % size) for i in range(size)])  1.16 us
  transfers between devices with their start and end apart: 11, of which 2 were waited for; matrix products, arithmetic and copies ran while one was open for 0% of the time, Pallas kernels for 23%

profile of v8, /device:TPU:1, one launch (start us, length us, event | category | flops | bytes accessed | tf_op | source)
XLA Modules:
  0.0 32.3 jit_solution(7853770526943935547)
XLA Ops:
  0.6 1.4 %constant_dynamic-slice_fusion.2 = (bf16[1,128,2,128]{3,2,1,0:T(2,128)(2,1)S(1)}, bf16[1,128,2,128]{3,2,1,0:T(2,128)(2,1)S(1)}, bf16[1,128,2,128]{3,2,1,0:T(2,128)(2,1)S(1)}, bf16[1,128,2,128]{3,2,1,0:T(2,128)(2,1)S(1)}) fusion(bf16[1,128,4,128]{3,2,1,0:T(4,128)(2,1)} %param.5, s32[]{:T(128)S(6)} %select_n.16, s32[]{:T(128)S(6)} %select_n.17, ...), kind=kLoop, calls=%fused_computation.8 | loop fusion | bytes 524296 | tf_op jit(solution)/shard_map/dynamic_slice | solution.py:345
  2.1 2.1 %collective-permute-start = (bf16[2,2,128,128]{3,2,1,0:T(8,128)(2,1)S(1)}, bf16[2,2,128,128]{3,2,1,0:T(8,128)(2,1)S(1)}, u32[]{:S(2)}, u32[]{:S(2)}) collective-permute-start(bf16[2,2,128,128]{3,2,1,0:T(8,128)(2,1)S(1)} %maximum_bitcast_fusion), channel_id=1, source_target_pairs={{0,1},{1,0},{2,3},{3,2},{4,5},{5,4},{6,7},{7,6},{8,9},{9,8},{10,11... | collective-permute-start | bytes 393224 | tf_op jit(solution)/shard_map/ppermute | solution.py:323
  4.3 1.3 %collective-permute-start.4 = (bf16[2,2,128,128]{3,2,1,0:T(8,128)(2,1)S(1)}, bf16[2,2,128,128]{3,2,1,0:T(8,128)(2,1)S(1)}, u32[]{:S(2)}, u32[]{:S(2)}) collective-permute-start(bf16[2,2,128,128]{3,2,1,0:T(8,128)(2,1)S(1)} %bitcast.8), channel_id=1, source_target_pairs={{0,8},{1,9},{2,10},{3,11},{4,12},{5,13},{6,14},{7,15},{8,16},{9,17... | collective-permute-start | bytes 393224 | tf_op jit(solution)/shard_map/ppermute | solution.py:332
  5.6 1.2 %collective-permute-start.5 = (bf16[2,2,128,128]{3,2,1,0:T(8,128)(2,1)S(1)}, bf16[2,2,128,128]{3,2,1,0:T(8,128)(2,1)S(1)}, u32[]{:S(2)}, u32[]{:S(2)}) collective-permute-start(bf16[2,2,128,128]{3,2,1,0:T(8,128)(2,1)S(1)} %maximum_bitcast_fusion), channel_id=1, source_target_pairs={{0,9},{1,8},{2,11},{3,10},{4,13},{5,12},{6,15},{7,14},{8,17},{9,16... | collective-permute-start | bytes 393224 | tf_op jit(solution)/shard_map/ppermute | solution.py:332
  6.8 0.0 copy-start
  6.9 1.2 %copy-done = bf16[1,128,32,128]{3,2,1,0:T(8,128)(2,1)S(1)} copy-done((bf16[1,128,32,128]{3,2,1,0:T(8,128)(2,1)S(1)}, bf16[1,128,32,128]{3,2,1,0:T(8,128)(2,1)}, u32[]{:S(2)}) %copy-start) | copy-done | bytes 1048600
  8.1 0.3 shard_map.58
  8.4 1.3 %collective-permute-start.3 = (bf16[1,1024,128]{2,1,0:T(8,128)(2,1)S(1)}, bf16[1,1024,128]{2,1,0:T(8,128)(2,1)S(1)}, u32[]{:S(2)}, u32[]{:S(2)}) collective-permute-start(bf16[1,1024,128]{2,1,0:T(8,128)(2,1)S(1)} %get-tuple-element.45), channel_id=1, source_target_pairs={{0,1},{1,0},{2,3},{3,2},{4,5},{5,4},{6,7},{7,6},{8,9},{9,8},{10,11... | collective-permute-start | bytes 786440 | tf_op jit(solution)/shard_map/ppermute | solution.py:323
  9.7 0.0 collective-permute-done
  9.7 1.3 %collective-permute-start.1 = (bf16[2,2,2,128,128]{4,3,2,1,0:T(8,128)(2,1)S(1)}, bf16[2,2,2,128,128]{4,3,2,1,0:T(8,128)(2,1)S(1)}, u32[]{:S(2)}, u32[]{:S(2)}) collective-permute-start(bf16[2,2,2,128,128]{4,3,2,1,0:T(8,128)(2,1)S(1)} %pad_maximum_fusion.refs_2_), channel_id=1, source_target_pairs={{0,4},{2,6},{4,8},{6,10},{8,12},{10,14},{12,16},{14,18},{16,20},{1... | collective-permute-start | bytes 786440 | tf_op jit(solution)/shard_map/ppermute | solution.py:323
  11.0 0.0 collective-permute-done.4
  11.0 2.3 %collective-permute-done.5 = bf16[2,2,128,128]{3,2,1,0:T(8,128)(2,1)S(1)} collective-permute-done((bf16[2,2,128,128]{3,2,1,0:T(8,128)(2,1)S(1)}, bf16[2,2,128,128]{3,2,1,0:T(8,128)(2,1)S(1)}, u32[]{:S(2)}, u32[]{:S(2)}) %collective-permute-start.5) | collective-permute-done | bytes 131104 | tf_op jit(solution)/shard_map/ppermute | solution.py:332
  13.3 1.7 %collective-permute-start.6 = (bf16[2,2,2,128,128]{4,3,2,1,0:T(8,128)(2,1)S(1)}, bf16[2,2,2,128,128]{4,3,2,1,0:T(8,128)(2,1)S(1)}, u32[]{:S(2)}, u32[]{:S(2)}) collective-permute-start(bf16[2,2,2,128,128]{4,3,2,1,0:T(8,128)(2,1)S(1)} %get-tuple-element.85), channel_id=1, source_target_pairs={{0,2},{2,0},{4,6},{6,4},{8,10},{10,8},{12,14},{14,12},{16,18},{18,... | collective-permute-start | bytes 786440 | tf_op jit(solution)/shard_map/ppermute | solution.py:323
  15.1 1.3 %collective-permute-start.7 = (bf16[1,1024,128]{2,1,0:T(8,128)(2,1)S(1)}, bf16[1,1024,128]{2,1,0:T(8,128)(2,1)S(1)}, u32[]{:S(2)}, u32[]{:S(2)}) collective-permute-start(bf16[1,1024,128]{2,1,0:T(8,128)(2,1)S(1)} %get-tuple-element.54), channel_id=1, source_target_pairs={{0,1},{1,0},{2,3},{3,2},{4,5},{5,4},{6,7},{7,6},{8,9},{9,8},{10,11... | collective-permute-start | bytes 786440 | tf_op jit(solution)/shard_map/ppermute | solution.py:323
  16.3 1.3 %collective-permute-start.8 = (bf16[2,2,2,128,128]{4,3,2,1,0:T(8,128)(2,1)S(1)}, bf16[2,2,2,128,128]{4,3,2,1,0:T(8,128)(2,1)S(1)}, u32[]{:S(2)}, u32[]{:S(2)}) collective-permute-start(bf16[2,2,2,128,128]{4,3,2,1,0:T(8,128)(2,1)S(1)} %get-tuple-element.86.refs_3_), channel_id=1, source_target_pairs={{0,4},{2,6},{4,8},{6,10},{8,12},{10,14},{12,16},{14,18},{16,20},{1... | collective-permute-start | bytes 786440 | tf_op jit(solution)/shard_map/ppermute | solution.py:323
  17.7 1.1 %collective-permute-done.3.refs_1_ = bf16[1,1024,128]{2,1,0:T(8,128)(2,1)S(1)} collective-permute-done((bf16[1,1024,128]{2,1,0:T(8,128)(2,1)S(1)}, bf16[1,1024,128]{2,1,0:T(8,128)(2,1)S(1)}, u32[]{:S(2)}, u32[]{:S(2)}) %collective-permute-start.3) | collective-permute-done | bytes 262176 | tf_op jit(solution)/shard_map/ppermute | solution.py:323
  18.8 1.6 %collective-permute-start.10 = (bf16[2,2,2,128,128]{4,3,2,1,0:T(8,128)(2,1)S(1)}, bf16[2,2,2,128,128]{4,3,2,1,0:T(8,128)(2,1)S(1)}, u32[]{:S(2)}, u32[]{:S(2)}) collective-permute-start(bf16[2,2,2,128,128]{4,3,2,1,0:T(8,128)(2,1)S(1)} %get-tuple-element.86.refs_3_), channel_id=1, source_target_pairs={{0,2},{2,8},{4,6},{6,12},{8,10},{10,16},{12,14},{14,20},{16,18},{1... | collective-permute-start | bytes 786440 | tf_op jit(solution)/shard_map/ppermute | solution.py:323
  20.4 0.0 collective-permute-done.1.refs_5_
  20.4 1.1 %collective-permute-start.2 = (bf16[2,2,2,128,128]{4,3,2,1,0:T(8,128)(2,1)S(1)}, bf16[2,2,2,128,128]{4,3,2,1,0:T(8,128)(2,1)S(1)}, u32[]{:S(2)}, u32[]{:S(2)}) collective-permute-start(bf16[2,2,2,128,128]{4,3,2,1,0:T(8,128)(2,1)S(1)} %collective-permute-done.1.refs_5_), channel_id=1, source_target_pairs={{0,2},{2,0},{4,6},{6,4},{8,10},{10,8},{12,14},{14,12},{16,18},{18,... | collective-permute-start | bytes 786440 | tf_op jit(solution)/shard_map/ppermute | solution.py:323
  21.5 0.0 collective-permute-done.6.refs_4_
  21.5 2.2 %shard_map.59 = (bf16[2,1,1024,128]{3,2,1,0:T(8,128)(2,1)S(1)}, f32[2,128,8,128]{3,2,1,0:T(8,128)S(1)}, f32[2,1,1024,128]{3,2,1,0:T(8,128)S(1)}, f32[2,1,1024,128]{3,2,1,0:T(8,128)S(1)}) custom-call(bf16[2,1024,128]{2,1,0:T(8,128)(2,1)S(1)} %get-tuple-element.59.refs_0_, bf16[1,1024,128]{2,1,0:T(8,128)(2,1)S(1)} %collective-permute-done.3.refs_1_, ...), custom_call_target="tpu_custom_call" | custom-call | flops 4000000000 | bytes 1048576 | tf_op jit(solution)/shard_map/pallas_call | solution.py:294
  23.7 0.0 collective-permute-done.2.refs_0_.refs_6_
  23.7 0.8 %shard_map.60 = (bf16[2,1,1024,128]{3,2,1,0:T(8,128)(2,1)S(1)}, f32[2,128,8,128]{3,2,1,0:T(8,128)S(1)}, f32[2,1,1024,128]{3,2,1,0:T(8,128)S(1)}, f32[2,1,1024,128]{3,2,1,0:T(8,128)S(1)}) custom-call(bf16[2,2,2,128,128]{4,3,2,1,0:T(8,128)(2,1)S(1)} %collective-permute-done.2.refs_0_.refs_6_, ...), custom_call_target="tpu_custom_call", output_to_operand_aliasing={{0}: (1, {}), {1}: (2, {}), {2}: (3, {}), {3}: (4, {})} | custom-call | flops 1000000000 | bytes 1048576 | tf_op jit(solution)/shard_map/pallas_call | solution.py:294
  24.5 0.0 collective-permute-done.7.refs_1_
  24.5 2.6 %shard_map.61 = (bf16[2,1,1024,128]{3,2,1,0:T(8,128)(2,1)S(1)}, f32[2,128,8,128]{3,2,1,0:T(8,128)S(1)}, f32[2,1,1024,128]{3,2,1,0:T(8,128)S(1)}, f32[2,1,1024,128]{3,2,1,0:T(8,128)S(1)}) custom-call(bf16[2,1024,128]{2,1,0:T(8,128)(2,1)S(1)} %get-tuple-element.59.refs_0_, bf16[1,1024,128]{2,1,0:T(8,128)(2,1)S(1)} %collective-permute-done.7.refs_1_, ...), custom_call_target="tpu_custom_call" | custom-call | flops 5000000000 | bytes 1048576 | tf_op jit(solution)/shard_map/pallas_call | solution.py:294
  27.1 0.0 collective-permute-done.8.refs_1_
  27.1 1.4 %collective-permute-start.9 = (bf16[2,2,2,128,128]{4,3,2,1,0:T(8,128)(2,1)S(1)}, bf16[2,2,2,128,128]{4,3,2,1,0:T(8,128)(2,1)S(1)}, u32[]{:S(2)}, u32[]{:S(2)}) collective-permute-start(bf16[2,2,2,128,128]{4,3,2,1,0:T(8,128)(2,1)S(1)} %collective-permute-done.8.refs_1_), channel_id=1, source_target_pairs={{0,2},{2,0},{4,6},{6,4},{8,10},{10,8},{12,14},{14,12},{16,18},{18,... | collective-permute-start | bytes 786440 | tf_op jit(solution)/shard_map/ppermute | solution.py:323
  28.5 0.0 collective-permute-done.10.refs_0_
  28.5 1.7 %shard_map.62 = (bf16[2,1,1024,128]{3,2,1,0:T(8,128)(2,1)S(1)}, f32[2,128,8,128]{3,2,1,0:T(8,128)S(1)}, f32[2,1,1024,128]{3,2,1,0:T(8,128)S(1)}, f32[2,1,1024,12...) custom-call(bf16[2,2,2,128,128]{4,3,2,1,0:T(8,128)(2,1)S(1)} %collec, ...), custom_call_target="tpu_custom_call", output_to_operand_aliasing={{0}: (2, {}), {1}: (3, {}), {2}: (4, {}), {3}: (5, {}), {4}... | custom-call | flops 4000000000 | bytes 1048576 | tf_op jit(solution)/shard_map/pallas_call | solution.py:294
  30.2 0.0 collective-permute-done.9.refs_0_
  30.3 2.0 %shard_map.63 = (f32[1,256,16,128]{3,2,1,0:T(8,128)}, f32[16,1,256]{2,1,0:T(1,128)}, f32[16,1,256]{2,1,0:T(1,128)}, bf16[2,1,1024,128]{3,2,1,0:T(8,128)(2,1)S(1)...) custom-call(bf16[2,2,2,128,128]{4,3,2,1,0:T(8,128)(2,1)S(1)} %collec, ...), custom_call_target="tpu_custom_call", output_to_operand_aliasing={{3}: (1, {}), {4}: (2, {}), {5}: (3, {}), {6}: (4, {}), {7}... | custom-call | flops 2000000000 | bytes 1048576 | tf_op jit(solution)/shard_map/pallas_call | solution.py:294
  (7 shorter events, 0.1 us)
Async XLA Ops:
  2.1 7.6 %collective-permute-start = (bf16[2,2,128,128]{3,2,1,0:T(8,128)(2,1)S(1)}, bf16[2,2,128,128]{3,2,1,0:T(8,128)(2,1)S(1)}, u32[]{:S(2)}, u32[]{:S(2)}) collective-permute-start(bf16[2,2,128,128]{3,2,1,0:T(8,128)(2,1)S(1)} %maximum_bitcast_fusion), channel_id=1, source_target_pairs={{0,1},{1,0},{2,3},{3,2},{4,5},{5,4},{6,7},{7,6},{8,9},{9,8},{10,11... | collective-permute-start | bytes 393224 | tf_op jit(solution)/shard_map/ppermute | solution.py:323
  4.3 6.7 %collective-permute-start.4 = (bf16[2,2,128,128]{3,2,1,0:T(8,128)(2,1)S(1)}, bf16[2,2,128,128]{3,2,1,0:T(8,128)(2,1)S(1)}, u32[]{:S(2)}, u32[]{:S(2)}) collective-permute-start(bf16[2,2,128,128]{3,2,1,0:T(8,128)(2,1)S(1)} %bitcast.8), channel_id=1, source_target_pairs={{0,8},{1,9},{2,10},{3,11},{4,12},{5,13},{6,14},{7,15},{8,16},{9,17... | collective-permute-start | bytes 393224 | tf_op jit(solution)/shard_map/ppermute | solution.py:332
  5.6 7.7 %collective-permute-start.5 = (bf16[2,2,128,128]{3,2,1,0:T(8,128)(2,1)S(1)}, bf16[2,2,128,128]{3,2,1,0:T(8,128)(2,1)S(1)}, u32[]{:S(2)}, u32[]{:S(2)}) collective-permute-start(bf16[2,2,128,128]{3,2,1,0:T(8,128)(2,1)S(1)} %maximum_bitcast_fusion), channel_id=1, source_target_pairs={{0,9},{1,8},{2,11},{3,10},{4,13},{5,12},{6,15},{7,14},{8,17},{9,16... | collective-permute-start | bytes 393224 | tf_op jit(solution)/shard_map/ppermute | solution.py:332
  6.8 1.2 %copy-start = (bf16[1,128,32,128]{3,2,1,0:T(8,128)(2,1)S(1)}, bf16[1,128,32,128]{3,2,1,0:T(8,128)(2,1)}, u32[]{:S(2)}) copy-start(bf16[1,128,32,128]{3,2,1,0:T(8,128)(2,1)} %q_ref.1) | copy-start | bytes 3145732
  8.4 10.4 %collective-permute-start.3 = (bf16[1,1024,128]{2,1,0:T(8,128)(2,1)S(1)}, bf16[1,1024,128]{2,1,0:T(8,128)(2,1)S(1)}, u32[]{:S(2)}, u32[]{:S(2)}) collective-permute-start(bf16[1,1024,128]{2,1,0:T(8,128)(2,1)S(1)} %get-tuple-element.45), channel_id=1, source_target_pairs={{0,1},{1,0},{2,3},{3,2},{4,5},{5,4},{6,7},{7,6},{8,9},{9,8},{10,11... | collective-permute-start | bytes 786440 | tf_op jit(solution)/shard_map/ppermute | solution.py:323
  9.7 10.7 %collective-permute-start.1 = (bf16[2,2,2,128,128]{4,3,2,1,0:T(8,128)(2,1)S(1)}, bf16[2,2,2,128,128]{4,3,2,1,0:T(8,128)(2,1)S(1)}, u32[]{:S(2)}, u32[]{:S(2)}) collective-permute-start(bf16[2,2,2,128,128]{4,3,2,1,0:T(8,128)(2,1)S(1)} %pad_maximum_fusion.refs_2_), channel_id=1, source_target_pairs={{0,4},{2,6},{4,8},{6,10},{8,12},{10,14},{12,16},{14,18},{16,20},{1... | collective-permute-start | bytes 786440 | tf_op jit(solution)/shard_map/ppermute | solution.py:323
  13.3 8.2 %collective-permute-start.6 = (bf16[2,2,2,128,128]{4,3,2,1,0:T(8,128)(2,1)S(1)}, bf16[2,2,2,128,128]{4,3,2,1,0:T(8,128)(2,1)S(1)}, u32[]{:S(2)}, u32[]{:S(2)}) collective-permute-start(bf16[2,2,2,128,128]{4,3,2,1,0:T(8,128)(2,1)S(1)} %get-tuple-element.85), channel_id=1, source_target_pairs={{0,2},{2,0},{4,6},{6,4},{8,10},{10,8},{12,14},{14,12},{16,18},{18,... | collective-permute-start | bytes 786440 | tf_op jit(solution)/shard_map/ppermute | solution.py:323
  15.1 9.4 %collective-permute-start.7 = (bf16[1,1024,128]{2,1,0:T(8,128)(2,1)S(1)}, bf16[1,1024,128]{2,1,0:T(8,128)(2,1)S(1)}, u32[]{:S(2)}, u32[]{:S(2)}) collective-permute-start(bf16[1,1024,128]{2,1,0:T(8,128)(2,1)S(1)} %get-tuple-element.54), channel_id=1, source_target_pairs={{0,1},{1,0},{2,3},{3,2},{4,5},{5,4},{6,7},{7,6},{8,9},{9,8},{10,11... | collective-permute-start | bytes 786440 | tf_op jit(solution)/shard_map/ppermute | solution.py:323
  16.3 10.8 %collective-permute-start.8 = (bf16[2,2,2,128,128]{4,3,2,1,0:T(8,128)(2,1)S(1)}, bf16[2,2,2,128,128]{4,3,2,1,0:T(8,128)(2,1)S(1)}, u32[]{:S(2)}, u32[]{:S(2)}) collective-permute-start(bf16[2,2,2,128,128]{4,3,2,1,0:T(8,128)(2,1)S(1)} %get-tuple-element.86.refs_3_), channel_id=1, source_target_pairs={{0,4},{2,6},{4,8},{6,10},{8,12},{10,14},{12,16},{14,18},{16,20},{1... | collective-permute-start | bytes 786440 | tf_op jit(solution)/shard_map/ppermute | solution.py:323
  18.8 9.7 %collective-permute-start.10 = (bf16[2,2,2,128,128]{4,3,2,1,0:T(8,128)(2,1)S(1)}, bf16[2,2,2,128,128]{4,3,2,1,0:T(8,128)(2,1)S(1)}, u32[]{:S(2)}, u32[]{:S(2)}) collective-permute-start(bf16[2,2,2,128,128]{4,3,2,1,0:T(8,128)(2,1)S(1)} %get-tuple-element.86.refs_3_), channel_id=1, source_target_pairs={{0,2},{2,8},{4,6},{6,12},{8,10},{10,16},{12,14},{14,20},{16,18},{1... | collective-permute-start | bytes 786440 | tf_op jit(solution)/shard_map/ppermute | solution.py:323
  20.4 3.3 %collective-permute-start.2 = (bf16[2,2,2,128,128]{4,3,2,1,0:T(8,128)(2,1)S(1)}, bf16[2,2,2,128,128]{4,3,2,1,0:T(8,128)(2,1)S(1)}, u32[]{:S(2)}, u32[]{:S(2)}) collective-permute-start(bf16[2,2,2,128,128]{4,3,2,1,0:T(8,128)(2,1)S(1)} %collective-permute-done.1.refs_5_), channel_id=1, source_target_pairs={{0,2},{2,0},{4,6},{6,4},{8,10},{10,8},{12,14},{14,12},{16,18},{18,... | collective-permute-start | bytes 786440 | tf_op jit(solution)/shard_map/ppermute | solution.py:323
  27.1 3.2 %collective-permute-start.9 = (bf16[2,2,2,128,128]{4,3,2,1,0:T(8,128)(2,1)S(1)}, bf16[2,2,2,128,128]{4,3,2,1,0:T(8,128)(2,1)S(1)}, u32[]{:S(2)}, u32[]{:S(2)}) collective-permute-start(bf16[2,2,2,128,128]{4,3,2,1,0:T(8,128)(2,1)S(1)} %collective-permute-done.8.refs_1_), channel_id=1, source_target_pairs={{0,2},{2,0},{4,6},{6,4},{8,10},{10,8},{12,14},{14,12},{16,18},{18,... | collective-permute-start | bytes 786440 | tf_op jit(solution)/shard_map/ppermute | solution.py:323

commit v9 on v8

--- a/solution.py
+++ b/solution.py
@@ -18,7 +18,7 @@
 VMEM_LIMIT = 20 * 2**20
 NEG = -1e30
 SPAN = 256
-BLOCK = 128
+BLOCK = 256
 COST = 10**9
 
 
@@ -387,7 +387,7 @@
     def take(names):
         return [blocks[x][0] for x in names], [blocks[x][1] for x in names]
 
-    soon, late = ["own", "up", "near", "side"], ["side_c"]
+    soon, late = ["own", "up", "near"], ["side", "side_c"]
     state = []
     for i in range(split):
         last = i == split - 1

time: 32.5 us -> 32.5 us (level)
  Pallas kernels: 9.6 us -> 10.2 us
  starting transfers between devices: 15.7 us -> 15.1 us
    ppermute x9, starting transfers between devices: 13.1 us -> 12.5 us  [along(): lax.ppermute(block, axis, [(i, target(i) % size) for i in range(size)])]
    pallas_call x5, Pallas kernels: 9.32 us -> 9.91 us  [attend(): pl.pallas_call(functools.partial(attend_kernel, n, count, parts, offsets,...]
  transfers between devices with their start and end apart: 11 -> 11, of which waited for: 2 -> 2; matrix products, arithmetic and copies ran while one was open for 0% -> 0% of each run, Pallas kernels for 23% -> 25%
where the time goes in v9:
time: 32.5 us; the launch traced here: 32.3 us
  starting transfers between devices  15.1 us (46%)
  Pallas kernels  10.2 us (31%)
  waiting for transfers between devices  3.48 us (11%)
  local copies, waits for them, and re-layouts  2.66 us (8%)
  between operations  0.77 us (2%)
    ppermute x9, starting transfers between devices, along(): lax.ppermute(block, axis, [(i, target(i) % size) for i in range(size)])  12.5 us
    pallas_call x5, Pallas kernels, attend(): pl.pallas_call(functools.partial(attend_kernel, n, count, parts, offsets,...  9.91 us
    ppermute x2, starting transfers between devices, climb(): return lax.ppermute(block, ('ctx', 'head'), edges)  2.59 us
    ppermute x2, waiting for transfers between devices, climb(): return lax.ppermute(block, ('ctx', 'head'), edges)  2.33 us
    dynamic_slice x1, local copies, waits for them, and re-layouts, heads_of(): lax.dynamic_slice_in_dim(x[0], lax.rem(mine + d, count) * size, size, axi...  1.38 us
    unnamed x5, local copies, waits for them, and re-layouts  1.26 us
    ppermute x9, waiting for transfers between devices, along(): lax.ppermute(block, axis, [(i, target(i) % size) for i in range(size)])  1.16 us
  transfers between devices with their start and end apart: 11, of which 2 were waited for; matrix products, arithmetic and copies ran while one was open for 0% of the time, Pallas kernels for 25%

profile of v9, /device:TPU:1, one launch (start us, length us, event | category | flops | bytes accessed | tf_op | source)
XLA Modules:
  0.0 32.3 jit_solution(15687528124977205706)
XLA Ops:
  0.6 1.4 %constant_dynamic-slice_fusion.2 = (bf16[1,128,2,128]{3,2,1,0:T(2,128)(2,1)S(1)}, bf16[1,128,2,128]{3,2,1,0:T(2,128)(2,1)S(1)}, bf16[1,128,2,128]{3,2,1,0:T(2,128)(2,1)S(1)}, bf16[1,128,2,128]{3,2,1,0:T(2,128)(2,1)S(1)}) fusion(bf16[1,128,4,128]{3,2,1,0:T(4,128)(2,1)} %param.5, s32[]{:T(128)S(6)} %select_n.16, s32[]{:T(128)S(6)} %select_n.17, ...), kind=kLoop, calls=%fused_computation.8 | loop fusion | bytes 524296 | tf_op jit(solution)/shard_map/dynamic_slice | solution.py:345
  2.1 2.1 %collective-permute-start = (bf16[2,2,128,128]{3,2,1,0:T(8,128)(2,1)S(1)}, bf16[2,2,128,128]{3,2,1,0:T(8,128)(2,1)S(1)}, u32[]{:S(2)}, u32[]{:S(2)}) collective-permute-start(bf16[2,2,128,128]{3,2,1,0:T(8,128)(2,1)S(1)} %maximum_bitcast_fusion), channel_id=1, source_target_pairs={{0,1},{1,0},{2,3},{3,2},{4,5},{5,4},{6,7},{7,6},{8,9},{9,8},{10,11... | collective-permute-start | bytes 393224 | tf_op jit(solution)/shard_map/ppermute | solution.py:323
  4.3 1.3 %collective-permute-start.4 = (bf16[2,2,128,128]{3,2,1,0:T(8,128)(2,1)S(1)}, bf16[2,2,128,128]{3,2,1,0:T(8,128)(2,1)S(1)}, u32[]{:S(2)}, u32[]{:S(2)}) collective-permute-start(bf16[2,2,128,128]{3,2,1,0:T(8,128)(2,1)S(1)} %bitcast.8), channel_id=1, source_target_pairs={{0,8},{1,9},{2,10},{3,11},{4,12},{5,13},{6,14},{7,15},{8,16},{9,17... | collective-permute-start | bytes 393224 | tf_op jit(solution)/shard_map/ppermute | solution.py:332
  5.6 1.2 %collective-permute-start.5 = (bf16[2,2,128,128]{3,2,1,0:T(8,128)(2,1)S(1)}, bf16[2,2,128,128]{3,2,1,0:T(8,128)(2,1)S(1)}, u32[]{:S(2)}, u32[]{:S(2)}) collective-permute-start(bf16[2,2,128,128]{3,2,1,0:T(8,128)(2,1)S(1)} %maximum_bitcast_fusion), channel_id=1, source_target_pairs={{0,9},{1,8},{2,11},{3,10},{4,13},{5,12},{6,15},{7,14},{8,17},{9,16... | collective-permute-start | bytes 393224 | tf_op jit(solution)/shard_map/ppermute | solution.py:332
  6.8 0.0 copy-start
  6.9 1.2 %copy-done = bf16[1,128,32,128]{3,2,1,0:T(8,128)(2,1)S(1)} copy-done((bf16[1,128,32,128]{3,2,1,0:T(8,128)(2,1)S(1)}, bf16[1,128,32,128]{3,2,1,0:T(8,128)(2,1)}, u32[]{:S(2)}) %copy-start) | copy-done | bytes 1048600
  8.1 0.3 shard_map.58
  8.4 1.3 %collective-permute-start.3 = (bf16[1,1024,128]{2,1,0:T(8,128)(2,1)S(1)}, bf16[1,1024,128]{2,1,0:T(8,128)(2,1)S(1)}, u32[]{:S(2)}, u32[]{:S(2)}) collective-permute-start(bf16[1,1024,128]{2,1,0:T(8,128)(2,1)S(1)} %get-tuple-element.45), channel_id=1, source_target_pairs={{0,1},{1,0},{2,3},{3,2},{4,5},{5,4},{6,7},{7,6},{8,9},{9,8},{10,11... | collective-permute-start | bytes 786440 | tf_op jit(solution)/shard_map/ppermute | solution.py:323
  9.7 0.0 collective-permute-done
  9.7 1.3 %collective-permute-start.1 = (bf16[2,2,2,128,128]{4,3,2,1,0:T(8,128)(2,1)S(1)}, bf16[2,2,2,128,128]{4,3,2,1,0:T(8,128)(2,1)S(1)}, u32[]{:S(2)}, u32[]{:S(2)}) collective-permute-start(bf16[2,2,2,128,128]{4,3,2,1,0:T(8,128)(2,1)S(1)} %pad_maximum_fusion.refs_2_), channel_id=1, source_target_pairs={{0,4},{2,6},{4,8},{6,10},{8,12},{10,14},{12,16},{14,18},{16,20},{1... | collective-permute-start | bytes 786440 | tf_op jit(solution)/shard_map/ppermute | solution.py:323
  11.0 0.0 collective-permute-done.4
  11.0 2.3 %collective-permute-done.5 = bf16[2,2,128,128]{3,2,1,0:T(8,128)(2,1)S(1)} collective-permute-done((bf16[2,2,128,128]{3,2,1,0:T(8,128)(2,1)S(1)}, bf16[2,2,128,128]{3,2,1,0:T(8,128)(2,1)S(1)}, u32[]{:S(2)}, u32[]{:S(2)}) %collective-permute-start.5) | collective-permute-done | bytes 131104 | tf_op jit(solution)/shard_map/ppermute | solution.py:332
  13.3 1.7 %collective-permute-start.6 = (bf16[2,2,2,128,128]{4,3,2,1,0:T(8,128)(2,1)S(1)}, bf16[2,2,2,128,128]{4,3,2,1,0:T(8,128)(2,1)S(1)}, u32[]{:S(2)}, u32[]{:S(2)}) collective-permute-start(bf16[2,2,2,128,128]{4,3,2,1,0:T(8,128)(2,1)S(1)} %get-tuple-element.85), channel_id=1, source_target_pairs={{0,2},{2,0},{4,6},{6,4},{8,10},{10,8},{12,14},{14,12},{16,18},{18,... | collective-permute-start | bytes 786440 | tf_op jit(solution)/shard_map/ppermute | solution.py:323
  15.1 1.3 %collective-permute-start.7 = (bf16[1,1024,128]{2,1,0:T(8,128)(2,1)S(1)}, bf16[1,1024,128]{2,1,0:T(8,128)(2,1)S(1)}, u32[]{:S(2)}, u32[]{:S(2)}) collective-permute-start(bf16[1,1024,128]{2,1,0:T(8,128)(2,1)S(1)} %get-tuple-element.54), channel_id=1, source_target_pairs={{0,1},{1,0},{2,3},{3,2},{4,5},{5,4},{6,7},{7,6},{8,9},{9,8},{10,11... | collective-permute-start | bytes 786440 | tf_op jit(solution)/shard_map/ppermute | solution.py:323
  16.3 1.3 %collective-permute-start.8 = (bf16[2,2,2,128,128]{4,3,2,1,0:T(8,128)(2,1)S(1)}, bf16[2,2,2,128,128]{4,3,2,1,0:T(8,128)(2,1)S(1)}, u32[]{:S(2)}, u32[]{:S(2)}) collective-permute-start(bf16[2,2,2,128,128]{4,3,2,1,0:T(8,128)(2,1)S(1)} %get-tuple-element.86.refs_3_), channel_id=1, source_target_pairs={{0,4},{2,6},{4,8},{6,10},{8,12},{10,14},{12,16},{14,18},{16,20},{1... | collective-permute-start | bytes 786440 | tf_op jit(solution)/shard_map/ppermute | solution.py:323
  17.7 1.1 %collective-permute-done.3.refs_1_ = bf16[1,1024,128]{2,1,0:T(8,128)(2,1)S(1)} collective-permute-done((bf16[1,1024,128]{2,1,0:T(8,128)(2,1)S(1)}, bf16[1,1024,128]{2,1,0:T(8,128)(2,1)S(1)}, u32[]{:S(2)}, u32[]{:S(2)}) %collective-permute-start.3) | collective-permute-done | bytes 262176 | tf_op jit(solution)/shard_map/ppermute | solution.py:323
  18.8 1.6 %collective-permute-start.10 = (bf16[2,2,2,128,128]{4,3,2,1,0:T(8,128)(2,1)S(1)}, bf16[2,2,2,128,128]{4,3,2,1,0:T(8,128)(2,1)S(1)}, u32[]{:S(2)}, u32[]{:S(2)}) collective-permute-start(bf16[2,2,2,128,128]{4,3,2,1,0:T(8,128)(2,1)S(1)} %get-tuple-element.86.refs_3_), channel_id=1, source_target_pairs={{0,2},{2,8},{4,6},{6,12},{8,10},{10,16},{12,14},{14,20},{16,18},{1... | collective-permute-start | bytes 786440 | tf_op jit(solution)/shard_map/ppermute | solution.py:323
  20.4 0.0 collective-permute-done.1.refs_0_.refs_5_
  20.4 1.1 %collective-permute-start.2 = (bf16[2,2,2,128,128]{4,3,2,1,0:T(8,128)(2,1)S(1)}, bf16[2,2,2,128,128]{4,3,2,1,0:T(8,128)(2,1)S(1)}, u32[]{:S(2)}, u32[]{:S(2)}) collective-permute-start(bf16[2,2,2,128,128]{4,3,2,1,0:T(8,128)(2,1)S(1)} %collective-permute-done.1.refs_0_.refs_5_), channel_id=1, source_target_pairs={{0,2},{2,0},{4,6},{6,4},{8,10},{10,8},{12,14},{14,12},{16,18},{18,... | collective-permute-start | bytes 786440 | tf_op jit(solution)/shard_map/ppermute | solution.py:323
  21.5 0.0 collective-permute-done.6.refs_4_
  21.5 1.8 %shard_map.59 = (bf16[2,1,1024,128]{3,2,1,0:T(8,128)(2,1)S(1)}, f32[2,128,8,128]{3,2,1,0:T(8,128)S(1)}, f32[2,1,1024,128]{3,2,1,0:T(8,128)S(1)}, f32[2,1,1024,128]{3,2,1,0:T(8,128)S(1)}) custom-call(bf16[2,1024,128]{2,1,0:T(8,128)(2,1)S(1)} %get-tuple-element.59.refs_0_, bf16[1,1024,128]{2,1,0:T(8,128)(2,1)S(1)} %collective-permute-done.3.refs_1_, ...), custom_call_target="tpu_custom_call" | custom-call | flops 3000000000 | bytes 1048576 | tf_op jit(solution)/shard_map/pallas_call | solution.py:294
  23.3 0.0 collective-permute-done.2.refs_1_.refs_6_
  23.3 1.8 %shard_map.60 = (bf16[2,1,1024,128]{3,2,1,0:T(8,128)(2,1)S(1)}, f32[2,128,8,128]{3,2,1,0:T(8,128)S(1)}, f32[2,1,1024,128]{3,2,1,0:T(8,128)S(1)}, f32[2,1,1024,128]{3,2,1,0:T(8,128)S(1)}) custom-call(bf16[2,2,2,128,128]{4,3,2,1,0:T(8,128)(2,1)S(1)} %collective-permute-done.1.refs_0_.refs_5_, ...), custom_call_target="tpu_custom_call", output_to_operand_aliasing={{0}: (2, {}), {1}: (3, {}), {2}: (4, {}), {3}: (5, {})} | custom-call | flops 2000000000 | bytes 1048576 | tf_op jit(solution)/shard_map/pallas_call | solution.py:294
  25.1 0.0 collective-permute-done.7.refs_1_
  25.1 2.6 %shard_map.61 = (bf16[2,1,1024,128]{3,2,1,0:T(8,128)(2,1)S(1)}, f32[2,128,8,128]{3,2,1,0:T(8,128)S(1)}, f32[2,1,1024,128]{3,2,1,0:T(8,128)S(1)}, f32[2,1,1024,128]{3,2,1,0:T(8,128)S(1)}) custom-call(bf16[2,1024,128]{2,1,0:T(8,128)(2,1)S(1)} %get-tuple-element.59.refs_0_, bf16[1,1024,128]{2,1,0:T(8,128)(2,1)S(1)} %collective-permute-done.7.refs_1_, ...), custom_call_target="tpu_custom_call" | custom-call | flops 5000000000 | bytes 1048576 | tf_op jit(solution)/shard_map/pallas_call | solution.py:294
  27.7 0.0 collective-permute-done.8.refs_1_
  27.7 0.8 %collective-permute-start.9 = (bf16[2,2,2,128,128]{4,3,2,1,0:T(8,128)(2,1)S(1)}, bf16[2,2,2,128,128]{4,3,2,1,0:T(8,128)(2,1)S(1)}, u32[]{:S(2)}, u32[]{:S(2)}) collective-permute-start(bf16[2,2,2,128,128]{4,3,2,1,0:T(8,128)(2,1)S(1)} %collective-permute-done.8.refs_1_), channel_id=1, source_target_pairs={{0,2},{2,0},{4,6},{6,4},{8,10},{10,8},{12,14},{14,12},{16,18},{18,... | collective-permute-start | bytes 786440 | tf_op jit(solution)/shard_map/ppermute | solution.py:323
  28.5 0.0 collective-permute-done.10.refs_0_
  28.5 1.7 %shard_map.62 = (bf16[2,1,1024,128]{3,2,1,0:T(8,128)(2,1)S(1)}, f32[2,128,8,128]{3,2,1,0:T(8,128)S(1)}, f32[2,1,1024,128]{3,2,1,0:T(8,128)S(1)}, f32[2,1,1024,12...) custom-call(bf16[2,2,2,128,128]{4,3,2,1,0:T(8,128)(2,1)S(1)} %collec, ...), custom_call_target="tpu_custom_call", output_to_operand_aliasing={{0}: (2, {}), {1}: (3, {}), {2}: (4, {}), {3}: (5, {}), {4}... | custom-call | flops 4000000000 | bytes 1048576 | tf_op jit(solution)/shard_map/pallas_call | solution.py:294
  30.2 0.0 collective-permute-done.9.refs_0_
  30.2 2.0 %shard_map.63 = (f32[1,256,16,128]{3,2,1,0:T(8,128)}, f32[16,1,256]{2,1,0:T(1,128)}, f32[16,1,256]{2,1,0:T(1,128)}, bf16[2,1,1024,128]{3,2,1,0:T(8,128)(2,1)S(1)...) custom-call(bf16[2,2,2,128,128]{4,3,2,1,0:T(8,128)(2,1)S(1)} %collec, ...), custom_call_target="tpu_custom_call", output_to_operand_aliasing={{3}: (1, {}), {4}: (2, {}), {5}: (3, {}), {6}: (4, {}), {7}... | custom-call | flops 2000000000 | bytes 1048576 | tf_op jit(solution)/shard_map/pallas_call | solution.py:294
  (7 shorter events, 0.1 us)
Async XLA Ops:
  2.1 7.6 %collective-permute-start = (bf16[2,2,128,128]{3,2,1,0:T(8,128)(2,1)S(1)}, bf16[2,2,128,128]{3,2,1,0:T(8,128)(2,1)S(1)}, u32[]{:S(2)}, u32[]{:S(2)}) collective-permute-start(bf16[2,2,128,128]{3,2,1,0:T(8,128)(2,1)S(1)} %maximum_bitcast_fusion), channel_id=1, source_target_pairs={{0,1},{1,0},{2,3},{3,2},{4,5},{5,4},{6,7},{7,6},{8,9},{9,8},{10,11... | collective-permute-start | bytes 393224 | tf_op jit(solution)/shard_map/ppermute | solution.py:323
  4.3 6.7 %collective-permute-start.4 = (bf16[2,2,128,128]{3,2,1,0:T(8,128)(2,1)S(1)}, bf16[2,2,128,128]{3,2,1,0:T(8,128)(2,1)S(1)}, u32[]{:S(2)}, u32[]{:S(2)}) collective-permute-start(bf16[2,2,128,128]{3,2,1,0:T(8,128)(2,1)S(1)} %bitcast.8), channel_id=1, source_target_pairs={{0,8},{1,9},{2,10},{3,11},{4,12},{5,13},{6,14},{7,15},{8,16},{9,17... | collective-permute-start | bytes 393224 | tf_op jit(solution)/shard_map/ppermute | solution.py:332
  5.6 7.7 %collective-permute-start.5 = (bf16[2,2,128,128]{3,2,1,0:T(8,128)(2,1)S(1)}, bf16[2,2,128,128]{3,2,1,0:T(8,128)(2,1)S(1)}, u32[]{:S(2)}, u32[]{:S(2)}) collective-permute-start(bf16[2,2,128,128]{3,2,1,0:T(8,128)(2,1)S(1)} %maximum_bitcast_fusion), channel_id=1, source_target_pairs={{0,9},{1,8},{2,11},{3,10},{4,13},{5,12},{6,15},{7,14},{8,17},{9,16... | collective-permute-start | bytes 393224 | tf_op jit(solution)/shard_map/ppermute | solution.py:332
  6.8 1.2 %copy-start = (bf16[1,128,32,128]{3,2,1,0:T(8,128)(2,1)S(1)}, bf16[1,128,32,128]{3,2,1,0:T(8,128)(2,1)}, u32[]{:S(2)}) copy-start(bf16[1,128,32,128]{3,2,1,0:T(8,128)(2,1)} %q_ref.1) | copy-start | bytes 3145732
  8.4 10.4 %collective-permute-start.3 = (bf16[1,1024,128]{2,1,0:T(8,128)(2,1)S(1)}, bf16[1,1024,128]{2,1,0:T(8,128)(2,1)S(1)}, u32[]{:S(2)}, u32[]{:S(2)}) collective-permute-start(bf16[1,1024,128]{2,1,0:T(8,128)(2,1)S(1)} %get-tuple-element.45), channel_id=1, source_target_pairs={{0,1},{1,0},{2,3},{3,2},{4,5},{5,4},{6,7},{7,6},{8,9},{9,8},{10,11... | collective-permute-start | bytes 786440 | tf_op jit(solution)/shard_map/ppermute | solution.py:323
  9.7 10.7 %collective-permute-start.1 = (bf16[2,2,2,128,128]{4,3,2,1,0:T(8,128)(2,1)S(1)}, bf16[2,2,2,128,128]{4,3,2,1,0:T(8,128)(2,1)S(1)}, u32[]{:S(2)}, u32[]{:S(2)}) collective-permute-start(bf16[2,2,2,128,128]{4,3,2,1,0:T(8,128)(2,1)S(1)} %pad_maximum_fusion.refs_2_), channel_id=1, source_target_pairs={{0,4},{2,6},{4,8},{6,10},{8,12},{10,14},{12,16},{14,18},{16,20},{1... | collective-permute-start | bytes 786440 | tf_op jit(solution)/shard_map/ppermute | solution.py:323
  13.3 8.2 %collective-permute-start.6 = (bf16[2,2,2,128,128]{4,3,2,1,0:T(8,128)(2,1)S(1)}, bf16[2,2,2,128,128]{4,3,2,1,0:T(8,128)(2,1)S(1)}, u32[]{:S(2)}, u32[]{:S(2)}) collective-permute-start(bf16[2,2,2,128,128]{4,3,2,1,0:T(8,128)(2,1)S(1)} %get-tuple-element.85), channel_id=1, source_target_pairs={{0,2},{2,0},{4,6},{6,4},{8,10},{10,8},{12,14},{14,12},{16,18},{18,... | collective-permute-start | bytes 786440 | tf_op jit(solution)/shard_map/ppermute | solution.py:323
  15.1 10.0 %collective-permute-start.7 = (bf16[1,1024,128]{2,1,0:T(8,128)(2,1)S(1)}, bf16[1,1024,128]{2,1,0:T(8,128)(2,1)S(1)}, u32[]{:S(2)}, u32[]{:S(2)}) collective-permute-start(bf16[1,1024,128]{2,1,0:T(8,128)(2,1)S(1)} %get-tuple-element.54), channel_id=1, source_target_pairs={{0,1},{1,0},{2,3},{3,2},{4,5},{5,4},{6,7},{7,6},{8,9},{9,8},{10,11... | collective-permute-start | bytes 786440 | tf_op jit(solution)/shard_map/ppermute | solution.py:323
  16.3 11.4 %collective-permute-start.8 = (bf16[2,2,2,128,128]{4,3,2,1,0:T(8,128)(2,1)S(1)}, bf16[2,2,2,128,128]{4,3,2,1,0:T(8,128)(2,1)S(1)}, u32[]{:S(2)}, u32[]{:S(2)}) collective-permute-start(bf16[2,2,2,128,128]{4,3,2,1,0:T(8,128)(2,1)S(1)} %get-tuple-element.86.refs_3_), channel_id=1, source_target_pairs={{0,4},{2,6},{4,8},{6,10},{8,12},{10,14},{12,16},{14,18},{16,20},{1... | collective-permute-start | bytes 786440 | tf_op jit(solution)/shard_map/ppermute | solution.py:323
  18.8 9.7 %collective-permute-start.10 = (bf16[2,2,2,128,128]{4,3,2,1,0:T(8,128)(2,1)S(1)}, bf16[2,2,2,128,128]{4,3,2,1,0:T(8,128)(2,1)S(1)}, u32[]{:S(2)}, u32[]{:S(2)}) collective-permute-start(bf16[2,2,2,128,128]{4,3,2,1,0:T(8,128)(2,1)S(1)} %get-tuple-element.86.refs_3_), channel_id=1, source_target_pairs={{0,2},{2,8},{4,6},{6,12},{8,10},{10,16},{12,14},{14,20},{16,18},{1... | collective-permute-start | bytes 786440 | tf_op jit(solution)/shard_map/ppermute | solution.py:323
  20.4 2.9 %collective-permute-start.2 = (bf16[2,2,2,128,128]{4,3,2,1,0:T(8,128)(2,1)S(1)}, bf16[2,2,2,128,128]{4,3,2,1,0:T(8,128)(2,1)S(1)}, u32[]{:S(2)}, u32[]{:S(2)}) collective-permute-start(bf16[2,2,2,128,128]{4,3,2,1,0:T(8,128)(2,1)S(1)} %collective-permute-done.1.refs_0_.refs_5_), channel_id=1, source_target_pairs={{0,2},{2,0},{4,6},{6,4},{8,10},{10,8},{12,14},{14,12},{16,18},{18,... | collective-permute-start | bytes 786440 | tf_op jit(solution)/shard_map/ppermute | solution.py:323
  27.7 2.5 %collective-permute-start.9 = (bf16[2,2,2,128,128]{4,3,2,1,0:T(8,128)(2,1)S(1)}, bf16[2,2,2,128,128]{4,3,2,1,0:T(8,128)(2,1)S(1)}, u32[]{:S(2)}, u32[]{:S(2)}) collective-permute-start(bf16[2,2,2,128,128]{4,3,2,1,0:T(8,128)(2,1)S(1)} %collective-permute-done.8.refs_1_), channel_id=1, source_target_pairs={{0,2},{2,0},{4,6},{6,4},{8,10},{10,8},{12,14},{14,12},{16,18},{18,... | collective-permute-start | bytes 786440 | tf_op jit(solution)/shard_map/ppermute | solution.py:323
